TPU v7x, 32 devices: a whole 2x2x4 slice. The times are simulated.
32 devices in a mesh: dp: 8 (over z, y), shard: 4 (over x, core).
Axes of the slice: x: 2, y: 2, z: 4, core: 2. Of those that a mesh axis runs over, the one named last changes fastest.
Arguments:
- tokens: bfloat16 [4096, 1024], P(('dp', 'shard')), may hold values from -6 to 6
- out_grad: bfloat16 [4096, 1024], P(('dp', 'shard')), may hold values from -6 to 6
- dest: int32 [8, 4, 128], P(None, 'shard'), may hold values from 0 to 1023, as said below
- lengths: int32 [8, 4], P('dp'), may hold values from 1 to 384, 512 in all within a row
- classes: int32 [8, 4], P('dp'), may hold values from 0 to 999
- class_table: bfloat16 [1000, 1024], P(None, 'shard'), may hold values from -6 to 6
- w_ada: bfloat16 [2, 1024, 6144], P(None, 'shard', 'dp'), may hold values from -0.1875 to 0.1875
- w_qkv: bfloat16 [2, 1024, 3, 1024], P(None, 'dp', None, 'shard'), may hold values from -0.1875 to 0.1875
- head_scale: float32 [2, 16], P(None, 'shard'), may hold values from 2.1 to 3.2
- w_proj: bfloat16 [2, 1024, 1024], P(None, 'shard', 'dp'), may hold values from -0.5 to 0.5
- w_fc1: bfloat16 [2, 1024, 4096], P(None, 'dp', 'shard'), may hold values from -0.1875 to 0.1875
- w_fc2: bfloat16 [2, 4096, 1024], P(None, 'shard', 'dp'), may hold values from -0.09375 to 0.09375
Outputs:
- mixed: bfloat16 [4096, 1024], P(('dp', 'shard'))
- tokens_grad: bfloat16 [4096, 1024], P(('dp', 'shard'))
- class_table_grad: float32 [1000, 1024], P(None, 'shard')
- w_ada_grad: float32 [2, 1024, 6144], P(None, 'shard', 'dp')
- w_qkv_grad: float32 [2, 1024, 3, 1024], P(None, 'dp', None, 'shard')
- head_scale_grad: float32 [2, 16], P(None, 'shard')
- w_proj_grad: float32 [2, 1024, 1024], P(None, 'shard', 'dp')
- w_fc1_grad: float32 [2, 1024, 4096], P(None, 'dp', 'shard')
- w_fc2_grad: float32 [2, 4096, 1024], P(None, 'shard', 'dp')
Inputs may be any that keep to these rules, and one draw needn't show every extreme that they name: dest is a one-to-one map of all loader rows of shard index s onto the rows of shard index s of all packs; the loader rows of one dp index and one shard index send exactly 16 rows to each pack. The 4 lengths of a pack sum to 512; each pack has one item of exactly 384 tokens.
All inputs are finite; a program needn't handle non-finite values.
Results may differ from a plain program's by a relative error of at most 0.025.
Values may be sent and summed in bfloat16 or wider, within the bound.
No kernel may reach another device: no remote copies, remote signals or barrier semaphores. Data moves between devices by JAX's collectives and lax.ppermute only.
A program may use at most 192 MiB of HBM per device.

v0:
```python
import jax
import jax.numpy as jnp
from jax import lax
from jax.sharding import PartitionSpec as P

highest = lax.Precision.HIGHEST
epsilon = 1e-06
masked_score = -1e30
query_block = 512
level_ends = (1, 5, 14, 30, 55, 91, 155, 255, 424, 680)


def layer_norm(value):
    centered = value - jnp.mean(value, axis=-1, keepdims=True)
    return centered * lax.rsqrt(jnp.mean(centered * centered, axis=-1, keepdims=True) + epsilon)


def modulate(value, scale, shift):
    return layer_norm(value) * (1.0 + scale) + shift


def unit_rows(value):
    return value * lax.rsqrt(jnp.sum(value * value, axis=-1, keepdims=True) + epsilon)


def query_norm(value, log_scale):
    return unit_rows(value) * jnp.exp(log_scale)[None, :, None]


def gelu_tanh(value):
    return jax.nn.gelu(value, approximate=True)


def pack_layout(lengths, rows):
    ends = jnp.cumsum(lengths)
    starts = ends - lengths
    place = jnp.arange(rows, dtype=jnp.int32)
    member = jnp.sum((place[:, None] >= ends[None, :]).astype(jnp.int32), axis=1)
    onehot = member[:, None] == jnp.arange(lengths.shape[0], dtype=jnp.int32)[None, :]
    start = jnp.sum(jnp.where(onehot, starts[None, :], jnp.int32(0)), axis=1)
    bounds = jnp.array(level_ends, dtype=jnp.int32)
    level = jnp.sum(((place - start)[:, None] >= bounds[None, :]).astype(jnp.int32), axis=1)
    allowed = (member[:, None] == member[None, :]) & (level[None, :] <= level[:, None])
    return (onehot, allowed)


def contract_rows(left, right):
    return lax.dot_general(
        left, right, (((0,), (0,)), ((), ())), preferred_element_type=jnp.float32
    )


def contract_last(left, right):
    return lax.dot_general(
        left, right, (((1,), (1,)), ((), ())), preferred_element_type=jnp.float32
    )


def split_six(per_token, width):
    return tuple((per_token[:, part * width : (part + 1) * width] for part in range(6)))


def widen(value):
    return lax.all_gather(value, "shard", axis=0, tiled=True)


def narrow(value):
    return lax.psum_scatter(value, "shard", scatter_dimension=0, tiled=True)


def item_total(value):
    return lax.psum(value, "shard")


def route_maps(dest):
    table = dest[:, 0, :]
    groups, rows = table.shape
    capacity = rows // groups
    here_index = lax.axis_index("dp")
    own_row = lax.dynamic_index_in_dim(table, here_index, 0, keepdims=False)
    target_pack = own_row // rows
    peers = jnp.arange(groups, dtype=jnp.int32)
    hits = (target_pack[:, None] == peers[None, :]).astype(jnp.int32)
    rank = jnp.sum((jnp.cumsum(hits, axis=0) - 1) * hits, axis=1)
    send_slot = target_pack * capacity + rank
    mine = table // rows == here_index
    rank_in = jnp.cumsum(mine.astype(jnp.int32), axis=1) - 1
    slot_in = jnp.where(mine, peers[:, None] * capacity + rank_in, rows)
    row_of_slot = (
        jnp.zeros(rows + 1, jnp.int32)
        .at[slot_in.reshape(-1)]
        .set((table % rows).reshape(-1))[:rows]
    )
    return (send_slot, row_of_slot)


def attend(queries, keys, values, allowed):
    scores = jnp.einsum("thd,shd->hts", queries, keys, preferred_element_type=jnp.float32)
    scores = jnp.where(allowed[None], scores, masked_score)
    top = jnp.max(scores, axis=-1, keepdims=True)
    raised = jnp.exp(scores - top)
    total = jnp.sum(raised, axis=-1, keepdims=True)
    probs = (raised / total).astype(jnp.bfloat16)
    outputs = jnp.einsum("hts,shd->thd", probs, values, preferred_element_type=jnp.float32)
    totals = (top + jnp.log(total))[:, :, 0]
    return (outputs, totals)


def attend_back(queries, keys, values, allowed, log_total, grad_heads):
    rows = queries.shape[0]
    pieces = max(1, rows // query_block)
    span = rows // pieces
    scores = jnp.einsum("thd,shd->hts", queries, keys, preferred_element_type=jnp.float32)
    probs = jnp.where(allowed[None], jnp.exp(scores - log_total[:, 0:span, None]), 0.0)
    grad_probs = jnp.einsum("thd,shd->hts", grad_heads, values, preferred_element_type=jnp.float32)
    inner = jnp.sum(probs * grad_probs, axis=-1, keepdims=True)
    grad_scores = (probs * (grad_probs - inner)).astype(jnp.bfloat16)
    grad_queries = jnp.einsum("hts,shd->thd", grad_scores, keys, preferred_element_type=jnp.float32)
    grad_keys = jnp.einsum("hts,thd->shd", grad_scores, queries, preferred_element_type=jnp.float32)
    grad_values = jnp.einsum(
        "hts,thd->shd", probs.astype(jnp.bfloat16), grad_heads, preferred_element_type=jnp.float32
    )
    return (grad_queries, grad_keys, grad_values)


def on_device(
    tokens,
    out_grad,
    dest,
    lengths,
    classes,
    class_table,
    w_ada,
    w_qkv,
    head_scale,
    w_proj,
    w_fc1,
    w_fc2,
):
    rows, width = tokens.shape
    layers = w_ada.shape[0]
    pack = rows * lax.axis_size("shard")
    heads_here = head_scale.shape[1]
    send_slot, row_of_slot = route_maps(dest)
    outgoing_tokens = jnp.zeros_like(tokens).at[send_slot].set(tokens)
    outgoing_grads = jnp.zeros_like(out_grad).at[send_slot].set(out_grad)
    arrived_tokens, arrived_grads = (
        lax.all_to_all(outgoing_tokens, "dp", split_axis=0, concat_axis=0, tiled=True),
        lax.all_to_all(outgoing_grads, "dp", split_axis=0, concat_axis=0, tiled=True),
    )
    carried = jnp.zeros_like(tokens).at[row_of_slot].set(arrived_tokens).astype(jnp.float32)
    grad_carried = jnp.zeros_like(out_grad).at[row_of_slot].set(arrived_grads).astype(jnp.float32)
    onehot, allowed = pack_layout(lengths[0], pack)
    members = lax.dynamic_slice_in_dim(
        onehot.astype(jnp.float32), lax.axis_index("shard") * rows, rows, 0
    )
    class_hits = (
        classes[0][:, None] == jnp.arange(class_table.shape[0], dtype=jnp.int32)[None, :]
    ).astype(jnp.float32)
    cond = jnp.dot(class_hits, class_table.astype(jnp.float32), precision=highest)
    cond_low = jax.nn.silu(cond).astype(jnp.bfloat16)
    saved = []
    for layer in range(layers):
        qkv_full, proj_full, fc1_full, fc2_full, ada_full = (
            lax.all_gather(w_qkv[layer], "dp", axis=0, tiled=True),
            lax.all_gather(w_proj[layer], "dp", axis=1, tiled=True),
            lax.all_gather(w_fc1[layer], "dp", axis=0, tiled=True),
            lax.all_gather(w_fc2[layer], "dp", axis=1, tiled=True),
            lax.all_gather(w_ada[layer], "dp", axis=1, tiled=True),
        )
        modulation = item_total(jnp.dot(cond_low, ada_full, preferred_element_type=jnp.float32))
        per_token = jnp.dot(members, modulation, precision=highest)
        gain_one, gain_two, scale_one, scale_two, shift_one, shift_two = split_six(per_token, width)
        first_input = modulate(carried, scale_one, shift_one).astype(jnp.bfloat16)
        first_all = widen(first_input)
        projected = jnp.einsum(
            "td,dcf->tcf", first_all, qkv_full, preferred_element_type=jnp.float32
        )
        query = projected[:, 0].reshape(pack, heads_here, -1)
        key_part = projected[:, 1].reshape(pack, heads_here, -1)
        values = projected[:, 2].reshape(pack, heads_here, -1).astype(jnp.bfloat16)
        queries = query_norm(query, head_scale[layer]).astype(jnp.bfloat16)
        keys = unit_rows(key_part).astype(jnp.bfloat16)
        heads_out, log_total = attend(queries, keys, values, allowed)
        heads_low = heads_out.reshape(pack, -1).astype(jnp.bfloat16)
        attended = narrow(jnp.dot(heads_low, proj_full, preferred_element_type=jnp.float32))
        middle = carried + gain_one * attended
        second_input = modulate(middle, scale_two, shift_two).astype(jnp.bfloat16)
        second_all = widen(second_input)
        hidden = jnp.dot(second_all, fc1_full, preferred_element_type=jnp.float32)
        activated = gelu_tanh(hidden).astype(jnp.bfloat16)
        branch = narrow(jnp.dot(activated, fc2_full, preferred_element_type=jnp.float32))
        kept_weights = None
        saved.append(
            (
                carried,
                middle,
                per_token,
                first_all,
                query,
                key_part,
                queries,
                keys,
                values,
                log_total,
                heads_low,
                attended,
                second_all,
                hidden,
                branch,
                kept_weights,
            )
        )
        carried = middle + gain_two * branch
    grad_silu = jnp.zeros(cond.shape, jnp.float32)
    layer_grads = [None] * layers
    scale_grads = [None] * layers
    for layer in range(layers - 1, -1, -1):
        (
            carried_in,
            middle,
            per_token,
            first_all,
            query,
            key_part,
            queries,
            keys,
            values,
            log_total,
            heads_low,
            attended,
            second_all,
            hidden,
            branch,
            kept_weights,
        ) = saved[layer]
        qkv_full, proj_full, fc1_full, fc2_full, ada_full = (
            lax.all_gather(w_qkv[layer], "dp", axis=0, tiled=True),
            lax.all_gather(w_proj[layer], "dp", axis=1, tiled=True),
            lax.all_gather(w_fc1[layer], "dp", axis=0, tiled=True),
            lax.all_gather(w_fc2[layer], "dp", axis=1, tiled=True),
            lax.all_gather(w_ada[layer], "dp", axis=1, tiled=True),
        )
        gain_one, gain_two, scale_one, scale_two, shift_one, shift_two = split_six(per_token, width)
        grad_gain_two = grad_carried * branch
        grad_branch = widen((grad_carried * gain_two).astype(jnp.bfloat16))
        grad_activated = contract_last(grad_branch, fc2_full)
        activated = gelu_tanh(hidden).astype(jnp.bfloat16)
        grad_fc2 = contract_rows(activated, grad_branch)
        _, gelu_pull = jax.vjp(gelu_tanh, hidden)
        grad_hidden = gelu_pull(grad_activated)[0].astype(jnp.bfloat16)
        grad_fc1 = contract_rows(second_all, grad_hidden)
        grad_second = narrow(contract_last(grad_hidden, fc1_full))
        _, second_pull = jax.vjp(modulate, middle, scale_two, shift_two)
        grad_middle_part, grad_scale_two, grad_shift_two = second_pull(grad_second)
        grad_middle = grad_carried + grad_middle_part
        grad_gain_one = grad_middle * attended
        grad_attended = widen((grad_middle * gain_one).astype(jnp.bfloat16))
        grad_proj = contract_rows(heads_low, grad_attended)
        grad_heads = (
            contract_last(grad_attended, proj_full)
            .astype(jnp.bfloat16)
            .reshape(pack, heads_here, -1)
        )
        grad_queries, grad_keys, grad_values = attend_back(
            queries, keys, values, allowed, log_total, grad_heads
        )
        _, query_pull = jax.vjp(query_norm, query, head_scale[layer])
        grad_query, grad_log = query_pull(grad_queries)
        _, key_pull = jax.vjp(unit_rows, key_part)
        (grad_key,) = key_pull(grad_keys)
        grad_projected = jnp.stack(
            [
                grad_query.reshape(pack, -1),
                grad_key.reshape(pack, -1),
                grad_values.reshape(pack, -1),
            ],
            axis=1,
        ).astype(jnp.bfloat16)
        grad_qkv = jnp.einsum(
            "td,tcf->dcf", first_all, grad_projected, preferred_element_type=jnp.float32
        )
        grad_first = narrow(
            jnp.einsum("tcf,dcf->td", grad_projected, qkv_full, preferred_element_type=jnp.float32)
        )
        _, first_pull = jax.vjp(modulate, carried_in, scale_one, shift_one)
        grad_carried_part, grad_scale_one, grad_shift_one = first_pull(grad_first)
        grad_carried = grad_middle + grad_carried_part
        grad_per_token = jnp.concatenate(
            [
                grad_gain_one,
                grad_gain_two,
                grad_scale_one,
                grad_scale_two,
                grad_shift_one,
                grad_shift_two,
            ],
            axis=1,
        )
        grad_modulation = item_total(jnp.dot(members.T, grad_per_token, precision=highest)).astype(
            jnp.bfloat16
        )
        grad_ada = contract_rows(cond_low, grad_modulation)
        grad_silu = grad_silu + contract_last(grad_modulation, ada_full)
        scale_grads[layer] = grad_log
        layer_grads[layer] = (
            lax.psum_scatter(grad_qkv, "dp", scatter_dimension=0, tiled=True),
            lax.psum_scatter(grad_proj, "dp", scatter_dimension=1, tiled=True),
            lax.psum_scatter(grad_fc1, "dp", scatter_dimension=0, tiled=True),
            lax.psum_scatter(grad_fc2, "dp", scatter_dimension=1, tiled=True),
            lax.psum_scatter(grad_ada, "dp", scatter_dimension=1, tiled=True),
        )
    stacked_qkv = jnp.stack([layer_grads[layer][0] for layer in range(layers)])
    stacked_proj = jnp.stack([layer_grads[layer][1] for layer in range(layers)])
    stacked_fc1 = jnp.stack([layer_grads[layer][2] for layer in range(layers)])
    stacked_fc2 = jnp.stack([layer_grads[layer][3] for layer in range(layers)])
    stacked_ada = jnp.stack([layer_grads[layer][4] for layer in range(layers)])
    qkv_grad, proj_grad, fc1_grad, fc2_grad, ada_grad = (
        stacked_qkv,
        stacked_proj,
        stacked_fc1,
        stacked_fc2,
        stacked_ada,
    )
    _, silu_pull = jax.vjp(jax.nn.silu, cond)
    (grad_cond,) = silu_pull(grad_silu)
    table_part = jnp.dot(class_hits.T, grad_cond, precision=highest)
    table_grad, scale_grad = lax.psum((table_part, jnp.stack(scale_grads)), "dp")
    leaving_tokens = carried.astype(jnp.bfloat16)[row_of_slot]
    leaving_grads = grad_carried.astype(jnp.bfloat16)[row_of_slot]
    back_tokens, back_grads = (
        lax.all_to_all(leaving_tokens, "dp", split_axis=0, concat_axis=0, tiled=True),
        lax.all_to_all(leaving_grads, "dp", split_axis=0, concat_axis=0, tiled=True),
    )
    mixed = back_tokens[send_slot]
    tokens_grad = back_grads[send_slot]
    return (
        mixed,
        tokens_grad,
        table_grad,
        ada_grad,
        qkv_grad,
        scale_grad,
        proj_grad,
        fc1_grad,
        fc2_grad,
    )


def solution(mesh):
    placed = (
        P(("dp", "shard"), None),
        P(("dp", "shard"), None),
        P(None, "shard", None),
        P("dp", None),
        P("dp", None),
        P(None, "shard"),
        P(None, "shard", "dp"),
        P(None, "dp", None, "shard"),
        P(None, "shard"),
        P(None, "shard", "dp"),
        P(None, "dp", "shard"),
        P(None, "shard", "dp"),
    )
    return jax.shard_map(
        on_device,
        mesh=mesh,
        in_specs=placed,
        out_specs=(
            P(("dp", "shard"), None),
            P(("dp", "shard"), None),
            P(None, "shard"),
            P(None, "shard", "dp"),
            P(None, "dp", None, "shard"),
            P(None, "shard"),
            P(None, "shard", "dp"),
            P(None, "dp", "shard"),
            P(None, "shard", "dp"),
        ),
        check_vma=False,
    )
```

profile of v0, /device:TPU:0, one launch (start us, length us, event | category | flops | bytes accessed | tf_op | source)
XLA Modules:
  0.0 1968.9 jit_solution(813149957439661510)
XLA Ops:
  12.9 7.3 all-to-all-start
  20.4 57.1 %all-gather.43.cloned.1.call-done = bf16[1,256,6144]{2,1,0:T(8,128)(2,1)} async-done(((bf16[1,256,768]{2,1,0:T(8,128)(2,1)}), bf16[1,256,6144]{2,1,0:T(8,128)(2,1)}) %all-gather.43.cloned.1.call-update) | async-done | bytes 3145744 | tf_op jit(solution)/shard_map/all_gather | solution.py:169
  80.6 58.7 %all-gather.51.cloned.1.call-done = bf16[1,256,6144]{2,1,0:T(8,128)(2,1)} async-done(((bf16[1,256,768]{2,1,0:T(8,128)(2,1)}), bf16[1,256,6144]{2,1,0:T(8,128)(2,1)}) %all-gather.51.cloned.1.call-update) | async-done | bytes 3145744 | tf_op jit(solution)/shard_map/all_gather | solution.py:169
  150.0 22.9 %all-reduce.8.cloned.1.call-done = (f32[4,6144]{1,0:T(4,128)}, f32[4,6144]{1,0:T(4,128)}) async-done(((f32[4,6144]{1,0:T(4,128)}, f32[4,6144]{1,0:T(4,128)}), (f32[4,6144]{1,0:T(4,128)}, f32[4,6144]{1,0:T(4,128)})) %all-reduce.8.cloned.1.call-update) | async-done | bytes 196624 | tf_op jit(solution)/shard_map/psum | solution.py:72
  178.3 29.2 %all-gather.2 = bf16[1,256,1024]{2,1,0:T(8,128)(2,1)S(1)} all-gather(bf16[1,256,128]{2,1,0:T(8,128)(2,1)S(1)} %get-tuple-element.55), channel_id=4, replica_groups=mesh['dp'=8,'shard'=4] {'dp'}, dimensions={2}, use_global_device_ids=true | all-gather | bytes 589824 | tf_op jit(solution)/shard_map/all_gather | solution.py:166
  207.7 16.3 all-gather.45.cloned.1.call-done
  224.0 17.0 all-gather.27.cloned.1.call-done
  251.2 30.4 %reduce-scatter.19.cloned.1.call-done = f32[128,1024]{1,0:T(8,128)} async-done(((f32[512,1024]{1,0:T(8,128)}), f32[128,1024]{1,0:T(8,128)}) %reduce-scatter.19.cloned.1.call-update) | async-done | bytes 524304 | tf_op jit(solution)/shard_map/reduce_scatter | solution.py:68
  286.3 47.4 %all-gather.47.cloned.1.call-done = bf16[1,1024,1024]{2,1,0:T(8,128)(2,1)} async-done(((bf16[1,128,1024]{2,1,0:T(8,128)(2,1)}), bf16[1,1024,1024]{2,1,0:T(8,128)(2,1)}) %all-gather.47.cloned.1.call-update) | async-done | bytes 2097168 | tf_op jit(solution)/shard_map/all_gather | solution.py:167
  333.7 17.4 all-gather.29.cloned.1.call-done
  351.0 4.5 fusion.44
  355.6 49.2 %all-gather.49.cloned.1.call-done = bf16[1,1024,1024]{2,1,0:T(8,128)(2,1)} async-done(((bf16[1,1024,128]{2,1,0:T(8,128)(2,1)}), bf16[1,1024,1024]{2,1,0:T(8,128)(2,1)}) %all-gather.49.cloned.1.call-update) | async-done | bytes 2097168 | tf_op jit(solution)/shard_map/all_gather | solution.py:168
  404.8 5.0 fusion.40
  413.9 25.6 %reduce-scatter.21.cloned.1.call-done = f32[128,1024]{1,0:T(8,128)} async-done(((f32[512,1024]{1,0:T(8,128)}), f32[128,1024]{1,0:T(8,128)}) %reduce-scatter.21.cloned.1.call-update) | async-done | bytes 524304 | tf_op jit(solution)/shard_map/reduce_scatter | solution.py:68
  443.4 29.7 %all-gather.7 = bf16[1,256,1024]{2,1,0:T(8,128)(2,1)} all-gather(bf16[1,256,128]{2,1,0:T(8,128)(2,1)S(1)} %get-tuple-element.54), channel_id=9, replica_groups=mesh['dp'=8,'shard'=4] {'dp'}, dimensions={2}, use_global_device_ids=true | all-gather | bytes 589824 | tf_op jit(solution)/shard_map/all_gather | solution.py:166
  473.1 17.8 all-gather.53.cloned.1.call-done
  490.8 17.0 all-gather.31.cloned.1.call-done
  519.8 14.6 all_to_all.48
  535.7 13.5 reduce-scatter.23.cloned.1.call-done
  554.8 46.3 %all-gather.55.cloned.1.call-done = bf16[1,1024,1024]{2,1,0:T(8,128)(2,1)} async-done(((bf16[1,128,1024]{2,1,0:T(8,128)(2,1)}), bf16[1,1024,1024]{2,1,0:T(8,128)(2,1)}) %all-gather.55.cloned.1.call-update) | async-done | bytes 2097168 | tf_op jit(solution)/shard_map/all_gather | solution.py:167
  601.1 17.2 all-gather.33.cloned.1.call-done
  622.8 49.1 %all-gather.57.cloned.1.call-done = bf16[1,1024,1024]{2,1,0:T(8,128)(2,1)} async-done(((bf16[1,1024,128]{2,1,0:T(8,128)(2,1)}), bf16[1,1024,1024]{2,1,0:T(8,128)(2,1)}) %all-gather.57.cloned.1.call-update) | async-done | bytes 2097168 | tf_op jit(solution)/shard_map/all_gather | solution.py:168
  671.9 16.9 all-gather.35.cloned.1.call-done
  688.8 5.0 fusion.29
  697.5 5.0 fusion.32
  702.5 26.4 %reduce-scatter.27.cloned.1.call-done = f32[128,1024]{1,0:T(8,128)} async-done(((f32[512,1024]{1,0:T(8,128)}), f32[128,1024]{1,0:T(8,128)}) %reduce-scatter.27.cloned.1.call-update) | async-done | bytes 524304 | tf_op jit(solution)/shard_map/reduce_scatter | solution.py:68
  730.4 32.7 %reduce-scatter.25.cloned.1.call-done = f32[128,1024]{1,0:T(8,128)} async-done(((f32[512,1024]{1,0:T(8,128)}), f32[128,1024]{1,0:T(8,128)}) %reduce-scatter.25.cloned.1.call-update) | async-done | bytes 524304 | tf_op jit(solution)/shard_map/reduce_scatter | solution.py:68
  768.2 16.8 all-gather.37.cloned.1.call-done
  810.9 28.7 %reduce-scatter.29.cloned.1.call-done = f32[128,1024]{1,0:T(8,128)} async-done(((f32[512,1024]{1,0:T(8,128)}), f32[128,1024]{1,0:T(8,128)}) %reduce-scatter.29.cloned.1.call-update) | async-done | bytes 524304 | tf_op jit(solution)/shard_map/reduce_scatter | solution.py:68
  845.5 16.8 all-gather.39.cloned.1.call-done
  862.3 5.0 fusion.22
  871.1 31.5 %reduce-scatter.31.cloned.1.call-done = f32[128,1024]{1,0:T(8,128)} async-done(((f32[512,1024]{1,0:T(8,128)}), f32[128,1024]{1,0:T(8,128)}) %reduce-scatter.31.cloned.1.call-update) | async-done | bytes 524304 | tf_op jit(solution)/shard_map/reduce_scatter | solution.py:68
  909.5 16.8 all-gather.41.cloned.1.call-done
  952.5 5.3 fusion.163
  959.1 5.0 fusion.162
  1003.1 13.3 all-reduce.9
  1025.7 5.4 all-to-all-start.1
  1048.3 22.4 %psum.47 = f32[2,4]{1,0:T(2,128)} all-reduce(f32[2,4]{1,0:T(2,128)S(1)} %pad_maximum_fusion.11), channel_id=1, replica_groups=mesh['dp'=8,'shard'=4] {'dp'}, use_global_device_ids=true, to_apply=%region_61.62 | all-reduce | flops 8 | bytes 64 | tf_op jit(solution)/shard_map/psum | solution.py:328
  1070.8 42.3 %reduce-scatter.43.cloned.1.call-done = f32[256,128]{1,0:T(8,128)} async-done(((f32[256,1024]{1,0:T(8,128)}), f32[256,128]{1,0:T(8,128)}) %reduce-scatter.43.cloned.1.call-update) | async-done | bytes 131088 | tf_op jit(solution)/shard_map/reduce_scatter | solution.py:308
  1114.8 89.9 %reduce-scatter.53.cloned.1.call-done = f32[1024,128]{1,0:T(8,128)} async-done(((f32[1024,1024]{1,0:T(8,128)}), f32[1024,128]{1,0:T(8,128)}) %reduce-scatter.53.cloned.1.call-update) | async-done | bytes 524304 | tf_op jit(solution)/shard_map/reduce_scatter | solution.py:310
  1204.7 91.7 %reduce-scatter.51.cloned.1.call-done = f32[1024,128]{1,0:T(8,128)} async-done(((f32[1024,1024]{1,0:T(8,128)}), f32[1024,128]{1,0:T(8,128)}) %reduce-scatter.51.cloned.1.call-update) | async-done | bytes 524304 | tf_op jit(solution)/shard_map/reduce_scatter | solution.py:310
  1298.7 89.5 %reduce-scatter.49.cloned.1.call-done = f32[128,1024]{1,0:T(8,128)} async-done(((f32[1024,1024]{1,0:T(8,128)}), f32[128,1024]{1,0:T(8,128)}) %reduce-scatter.49.cloned.1.call-update) | async-done | bytes 524304 | tf_op jit(solution)/shard_map/reduce_scatter | solution.py:309
  1388.2 91.3 %reduce-scatter.47.cloned.1.call-done = f32[128,1024]{1,0:T(8,128)} async-done(((f32[1024,1024]{1,0:T(8,128)}), f32[128,1024]{1,0:T(8,128)}) %reduce-scatter.47.cloned.1.call-update) | async-done | bytes 524304 | tf_op jit(solution)/shard_map/reduce_scatter | solution.py:309
  1483.4 74.8 %reduce-scatter.41.cloned.1.call-done = f32[128,3,256]{2,0,1:T(8,128)} async-done(((f32[1024,3,256]{2,0,1:T(8,128)}), f32[128,3,256]{2,0,1:T(8,128)}) %reduce-scatter.41.cloned.1.call-update) | async-done | bytes 393232 | tf_op jit(solution)/shard_map/reduce_scatter | solution.py:307
  1558.2 77.9 %reduce-scatter.39.cloned.1.call-done = f32[128,3,256]{2,0,1:T(8,128)} async-done(((f32[1024,3,256]{2,0,1:T(8,128)}), f32[128,3,256]{2,0,1:T(8,128)}) %reduce-scatter.39.cloned.1.call-update) | async-done | bytes 393232 | tf_op jit(solution)/shard_map/reduce_scatter | solution.py:307
  1638.2 119.1 %reduce-scatter.35.cloned.1.call-done = f32[256,768]{1,0:T(8,128)} async-done(((f32[256,6144]{1,0:T(8,128)}), f32[256,768]{1,0:T(8,128)}) %reduce-scatter.35.cloned.1.call-update) | async-done | bytes 786448 | tf_op jit(solution)/shard_map/reduce_scatter | solution.py:311
  1757.3 121.2 %reduce-scatter.37.cloned.1.call-done = f32[256,768]{1,0:T(8,128)} async-done(((f32[256,6144]{1,0:T(8,128)}), f32[256,768]{1,0:T(8,128)}) %reduce-scatter.37.cloned.1.call-update) | async-done | bytes 786448 | tf_op jit(solution)/shard_map/reduce_scatter | solution.py:311
  1881.1 78.6 %all-reduce.6.cloned.1.call-done = f32[1000,256]{1,0:T(8,128)} async-done(((f32[1000,256]{1,0:T(8,128)}), f32[1000,256]{1,0:T(8,128)}) %all-reduce.6.cloned.1.call-update) | async-done | bytes 1024016 | tf_op jit(solution)/shard_map/psum | solution.py:328
  (372 shorter events, 230.4 us)
Async XLA Ops:
  7.2 13.0 copy-start
  7.2 70.3 %all-gather.43.cloned.1.call-start = ((), (), s32[]{:S(2)}) async-start(), calls=%async_computation.49 | async-start | bytes 3538944 | tf_op jit(solution)/shard_map/all_gather | solution.py:169
  9.4 129.9 %all-gather.51.cloned.1.call-start = ((), (), s32[]{:S(2)}) async-start(), calls=%async_computation.53 | async-start | bytes 3538944 | tf_op jit(solution)/shard_map/all_gather | solution.py:169
  12.9 135.5 %all-to-all-start = ((bf16[8,16,1024]{2,1,0:T(8,128)(2,1)}), bf16[8,16,1024]{2,1,0:T(8,128)(2,1)S(1)}, u32[]{:S(2)}, u32[]{:S(2)}) async-start(bf16[8,16,1024]{2,1,0:T(8,128)(2,1)} %bitcast.9), calls=%async_computation | async-start | bytes 524288 | tf_op jit(solution)/shard_map/all_to_all | solution.py:148
  20.1 152.7 %all-reduce.8.cloned.1.call-start = ((), (), s32[]{:S(2)}) async-start(), calls=%async_computation.57 | async-start | bytes 393216 | tf_op jit(solution)/shard_map/psum | solution.py:72
  80.6 61.9 %copy-start.40 = (bf16[2,128,3,256]{3,1,2,0:T(8,128)(2,1)S(1)}, bf16[2,128,3,256]{3,1,2,0:T(8,128)(2,1)}, u32[]{:S(2)}) copy-start(bf16[2,128,3,256]{3,1,2,0:T(8,128)(2,1)} %param.20) | copy-start | bytes 1179652
  80.6 62.8 %copy-start.62 = (s32[1,4]{1,0:T(1,128)S(1)}, s32[1,4]{1,0:T(1,128)}, u32[]{:S(2)}) copy-start(s32[1,4]{1,0:T(1,128)} %param.16) | copy-start | bytes 52
  142.4 81.6 %all-gather.45.cloned.1.call-start = ((), (), s32[]{:S(2)}) async-start(), calls=%async_computation.50 | async-start | bytes 1769472 | tf_op jit(solution)/shard_map/all_gather | solution.py:165
  143.3 97.7 %all-gather.27.cloned.1.call-start = ((), (), s32[]{:S(2)}) async-start(), calls=%async_computation.22 | async-start | bytes 1310720 | tf_op jit(solution)/shard_map/all_gather | solution.py:64
  149.6 132.0 %copy-start.11 = (bf16[128,1024]{1,0:T(8,128)(2,1)}, bf16[128,1024]{1,0:T(8,128)(2,1)S(1)}, u32[]{:S(2)}) copy-start(bf16[128,1024]{1,0:T(8,128)(2,1)S(1)} %scatter_custom_fusion.2) | copy-start | bytes 786436
  178.0 103.7 %reduce-scatter.19.cloned.1.call-start = ((), (), s32[]{:S(2)}) async-start(), calls=%async_computation.23 | async-start | bytes 2621440 | tf_op jit(solution)/shard_map/reduce_scatter | solution.py:68
  207.4 40.8 %copy-start.24 = (bf16[1,256,1024]{2,1,0:T(8,128)(2,1)}, bf16[1,256,1024]{2,1,0:T(8,128)(2,1)S(1)}, u32[]{:S(2)}) copy-start(bf16[1,256,1024]{2,1,0:T(8,128)(2,1)S(1)} %all-gather.2) | copy-start | bytes 1572868
  250.0 83.6 %all-gather.47.cloned.1.call-start = ((), (), s32[]{:S(2)}) async-start(), calls=%async_computation.51 | async-start | bytes 2359296 | tf_op jit(solution)/shard_map/all_gather | solution.py:167
  251.0 34.4 %copy-start.39 = (bf16[2,1024,128]{2,1,0:T(8,128)(2,1)S(1)}, bf16[2,1024,128]{2,1,0:T(8,128)(2,1)}, u32[]{:S(2)}) copy-start(bf16[2,1024,128]{2,1,0:T(8,128)(2,1)} %param.24) | copy-start | bytes 1572868
  251.0 100.1 %all-gather.29.cloned.1.call-start = ((), (), s32[]{:S(2)}) async-start(), calls=%async_computation.24 | async-start | bytes 1310720 | tf_op jit(solution)/shard_map/all_gather | solution.py:64
  285.3 119.5 %all-gather.49.cloned.1.call-start = ((), (), s32[]{:S(2)}) async-start(), calls=%async_computation.52 | async-start | bytes 2359296 | tf_op jit(solution)/shard_map/all_gather | solution.py:168
  286.2 153.3 %reduce-scatter.21.cloned.1.call-start = ((), (), s32[]{:S(2)}) async-start(), calls=%async_computation.25 | async-start | bytes 2621440 | tf_op jit(solution)/shard_map/reduce_scatter | solution.py:68
  409.8 81.0 %all-gather.53.cloned.1.call-start = ((), (), s32[]{:S(2)}) async-start(), calls=%async_computation.54 | async-start | bytes 1769472 | tf_op jit(solution)/shard_map/all_gather | solution.py:165
  410.7 97.2 %all-gather.31.cloned.1.call-start = ((), (), s32[]{:S(2)}) async-start(), calls=%async_computation.26 | async-start | bytes 1310720 | tf_op jit(solution)/shard_map/all_gather | solution.py:64
  443.3 105.9 %reduce-scatter.23.cloned.1.call-start = ((), (), s32[]{:S(2)}) async-start(), calls=%async_computation.27 | async-start | bytes 2621440 | tf_op jit(solution)/shard_map/reduce_scatter | solution.py:68
  517.6 83.5 %all-gather.55.cloned.1.call-start = ((), (), s32[]{:S(2)}) async-start(), calls=%async_computation.55 | async-start | bytes 2359296 | tf_op jit(solution)/shard_map/all_gather | solution.py:167
  518.2 100.1 %all-gather.33.cloned.1.call-start = ((), (), s32[]{:S(2)}) async-start(), calls=%async_computation.28 | async-start | bytes 1310720 | tf_op jit(solution)/shard_map/all_gather | solution.py:64
  535.7 17.5 copy-start.15
  553.2 118.7 %all-gather.57.cloned.1.call-start = ((), (), s32[]{:S(2)}) async-start(), calls=%async_computation.56 | async-start | bytes 2359296 | tf_op jit(solution)/shard_map/all_gather | solution.py:168
  553.8 135.0 %all-gather.35.cloned.1.call-start = ((), (), s32[]{:S(2)}) async-start(), calls=%async_computation.30 | async-start | bytes 1310720 | tf_op jit(solution)/shard_map/all_gather | solution.py:64
  554.3 174.6 %reduce-scatter.27.cloned.1.call-start = ((), (), s32[]{:S(2)}) async-start(), calls=%async_computation.31 | async-start | bytes 2621440 | tf_op jit(solution)/shard_map/reduce_scatter | solution.py:68
  697.4 65.7 %reduce-scatter.25.cloned.1.call-start = ((), (), s32[]{:S(2)}) async-start(), calls=%async_computation.29 | async-start | bytes 2621440 | tf_op jit(solution)/shard_map/reduce_scatter | solution.py:68
  702.5 82.5 %all-gather.37.cloned.1.call-start = ((), (), s32[]{:S(2)}) async-start(), calls=%async_computation.32 | async-start | bytes 1310720 | tf_op jit(solution)/shard_map/all_gather | solution.py:64
  768.1 71.5 %reduce-scatter.29.cloned.1.call-start = ((), (), s32[]{:S(2)}) async-start(), calls=%async_computation.33 | async-start | bytes 2621440 | tf_op jit(solution)/shard_map/reduce_scatter | solution.py:68
  808.1 54.2 %all-gather.39.cloned.1.call-start = ((), (), s32[]{:S(2)}) async-start(), calls=%async_computation.34 | async-start | bytes 1310720 | tf_op jit(solution)/shard_map/all_gather | solution.py:64
  845.4 60.1 %copy-start.17 = (f32[128,1024]{1,0:T(8,128)}, f32[128,1024]{1,0:T(8,128)S(1)}, u32[]{:S(2)}) copy-start(f32[128,1024]{1,0:T(8,128)S(1)} %get-tuple-element.24) | copy-start | bytes 1572868
  845.4 57.2 %reduce-scatter.31.cloned.1.call-start = ((), (), s32[]{:S(2)}) async-start(), calls=%async_computation.35 | async-start | bytes 2621440 | tf_op jit(solution)/shard_map/reduce_scatter | solution.py:68
  871.0 55.3 %all-gather.41.cloned.1.call-start = ((), (), s32[]{:S(2)}) async-start(), calls=%async_computation.36 | async-start | bytes 1310720 | tf_op jit(solution)/shard_map/all_gather | solution.py:64
  909.4 84.1 %reduce-scatter.33.cloned.1.call-start = ((), (), s32[]{:S(2)}) async-start(), calls=%async_computation.37 | async-start | bytes 2621440 | tf_op jit(solution)/shard_map/reduce_scatter | solution.py:68
  945.8 125.0 %reduce-scatter.45.cloned.1.call-start = ((), (), s32[]{:S(2)}) async-start(), calls=%async_computation.44 | async-start | bytes 1179648 | tf_op jit(solution)/shard_map/reduce_scatter | solution.py:308
  949.4 163.7 %reduce-scatter.43.cloned.1.call-start = ((), (), s32[]{:S(2)}) async-start(), calls=%async_computation.43 | async-start | bytes 1179648 | tf_op jit(solution)/shard_map/reduce_scatter | solution.py:308
  952.2 252.5 %reduce-scatter.53.cloned.1.call-start = ((), (), s32[]{:S(2)}) async-start(), calls=%async_computation.48 | async-start | bytes 4718592 | tf_op jit(solution)/shard_map/reduce_scatter | solution.py:310
  957.9 338.6 %reduce-scatter.51.cloned.1.call-start = ((), (), s32[]{:S(2)}) async-start(), calls=%async_computation.47 | async-start | bytes 4718592 | tf_op jit(solution)/shard_map/reduce_scatter | solution.py:310
  964.1 424.1 %reduce-scatter.49.cloned.1.call-start = ((), (), s32[]{:S(2)}) async-start(), calls=%async_computation.46 | async-start | bytes 4718592 | tf_op jit(solution)/shard_map/reduce_scatter | solution.py:309
  969.9 509.6 %reduce-scatter.47.cloned.1.call-start = ((), (), s32[]{:S(2)}) async-start(), calls=%async_computation.45 | async-start | bytes 4718592 | tf_op jit(solution)/shard_map/reduce_scatter | solution.py:309
  975.6 582.5 %reduce-scatter.41.cloned.1.call-start = ((), (), s32[]{:S(2)}) async-start(), calls=%async_computation.42 | async-start | bytes 3538944 | tf_op jit(solution)/shard_map/reduce_scatter | solution.py:307
  980.7 655.4 %reduce-scatter.39.cloned.1.call-start = ((), (), s32[]{:S(2)}) async-start(), calls=%async_computation.41 | async-start | bytes 3538944 | tf_op jit(solution)/shard_map/reduce_scatter | solution.py:307
  985.8 771.5 %reduce-scatter.35.cloned.1.call-start = ((), (), s32[]{:S(2)}) async-start(), calls=%async_computation.39 | async-start | bytes 7077888 | tf_op jit(solution)/shard_map/reduce_scatter | solution.py:311
  1020.1 858.3 %reduce-scatter.37.cloned.1.call-start = ((), (), s32[]{:S(2)}) async-start(), calls=%async_computation.40 | async-start | bytes 7077888 | tf_op jit(solution)/shard_map/reduce_scatter | solution.py:311
  1025.7 17.6 all-to-all-start.1
  1031.2 928.5 %all-reduce.6.cloned.1.call-start = ((), (), s32[]{:S(2)}) async-start(), calls=%async_computation.38 | async-start | bytes 2048000 | tf_op jit(solution)/shard_map/psum | solution.py:328
  1043.3 438.5 %all-to-all-start.3 = ((bf16[8,16,1024]{2,1,0:T(8,128)(2,1)}), bf16[8,16,1024]{2,1,0:T(8,128)(2,1)S(1)}, u32[]{:S(2)}, u32[]{:S(2)}) async-start(bf16[8,16,1024]{2,1,0:T(8,128)(2,1)} %bitcast.60), calls=%async_computation.11 | async-start | bytes 524288 | tf_op jit(solution)/shard_map/all_to_all | solution.py:333
  1878.4 83.5 %copy-start.1 = (bf16[1000,256]{1,0:T(8,128)(2,1)S(1)}, bf16[1000,256]{1,0:T(8,128)(2,1)}, u32[]{:S(2)}) copy-start(bf16[1000,256]{1,0:T(8,128)(2,1)} %param.18) | copy-start | bytes 1536004
  (54 other events, 143.1 us)
Sparse Core Ops, SparseCore 0:
  10.8 66.6 all-gather.42
  80.3 58.9 all-gather.50
  142.5 30.2 all-reduce.7
  175.5 48.3 all-gather.44
  226.0 14.9 all-gather.26
  250.2 31.4 reduce-scatter.18
  284.3 49.2 all-gather.46
  335.8 15.1 all-gather.28
  353.7 51.0 all-gather.48
  409.9 29.5 reduce-scatter.20
  442.4 48.4 all-gather.52
  492.9 14.8 all-gather.30
  517.7 31.4 reduce-scatter.22
  551.7 49.2 all-gather.54
  603.0 15.1 all-gather.32
  620.7 51.0 all-gather.56
  673.8 14.8 all-gather.34
  697.5 31.4 reduce-scatter.26
  731.7 31.4 reduce-scatter.24
  768.2 16.7 all-gather.36
  808.2 31.4 reduce-scatter.28
  845.5 16.7 all-gather.38
  871.1 31.4 reduce-scatter.30
  909.5 16.7 all-gather.40
  946.0 31.4 reduce-scatter.32
  981.7 64.7 reduce-scatter.44
  1050.3 62.7 reduce-scatter.42
  1117.2 87.5 reduce-scatter.52
  1208.4 88.0 reduce-scatter.50
  1300.4 87.8 reduce-scatter.48
  1391.8 87.6 reduce-scatter.46
  1483.6 74.5 reduce-scatter.40
  1562.1 73.9 reduce-scatter.38
  1640.1 117.1 reduce-scatter.34
  1761.3 117.1 reduce-scatter.36
  1882.8 76.8 all-reduce.5
where the time goes:
time: 1980 us; the launch traced here: 1970 us
  waiting for transfers between devices  1570 us (79%)
  matrix products  141 us (7%)
  blocking collectives  109 us (6%)
  other arithmetic  62.2 us (3%)
  local copies, waits for them, and re-layouts  50.5 us (3%)
    reduce_scatter x2, waiting for transfers between devices, on_device(): lax.psum_scatter(grad_ada, 'dp', scatter_dimension=1, tiled=True)  240 us
    reduce_scatter x8, waiting for transfers between devices, narrow(): return lax.psum_scatter(value, 'shard', scatter_dimension=0, tiled=True)  189 us
    reduce_scatter x2, waiting for transfers between devices, on_device(): lax.psum_scatter(grad_fc2, 'dp', scatter_dimension=1, tiled=True)  182 us
    reduce_scatter x2, waiting for transfers between devices, on_device(): lax.psum_scatter(grad_fc1, 'dp', scatter_dimension=0, tiled=True)  181 us
    reduce_scatter x2, waiting for transfers between devices, on_device(): lax.psum_scatter(grad_qkv, 'dp', scatter_dimension=0, tiled=True)  153 us
    all_gather x8, waiting for transfers between devices, widen(): return lax.all_gather(value, 'shard', axis=0, tiled=True)  136 us
    all_gather x2, waiting for transfers between devices, on_device(): lax.all_gather(w_ada[layer], 'dp', axis=1, tiled=True)  116 us
    all_gather x2, waiting for transfers between devices, on_device(): lax.all_gather(w_fc2[layer], 'dp', axis=1, tiled=True)  98.3 us
  transfers between devices with their start and end apart: 39, of which 35 were waited for; matrix products, arithmetic and copies ran while one was open for 7% of the time, Pallas kernels for 0%

commit v1 on v0

v1 whole, which is shorter than its diff:
```python
import jax
import jax.numpy as jnp
from jax import lax
from jax.sharding import PartitionSpec as P

epsilon = 1e-06
masked_score = -1e30
level_ends = (1, 5, 14, 30, 55, 91, 155, 255, 424, 680)
wide = jnp.float32
low = jnp.bfloat16


def matmul(left, right):
    return jnp.dot(left, right, preferred_element_type=wide)


def contract_rows(left, right):
    return lax.dot_general(left, right, (((0,), (0,)), ((), ())), preferred_element_type=wide)


def contract_last(left, right):
    return lax.dot_general(left, right, (((1,), (1,)), ((), ())), preferred_element_type=wide)


def layer_norm(value):
    centered = value - jnp.mean(value, axis=-1, keepdims=True)
    return centered * lax.rsqrt(jnp.mean(centered * centered, axis=-1, keepdims=True) + epsilon)


def modulate(value, scale, shift):
    return layer_norm(value) * (1.0 + scale) + shift


def unit_rows(value):
    return value * lax.rsqrt(jnp.sum(value * value, axis=-1, keepdims=True) + epsilon)


def query_norm(value, log_scale):
    return unit_rows(value) * jnp.exp(log_scale)[None, :, None]


def gelu_tanh(value):
    return jax.nn.gelu(value, approximate=True)


def swap(value, axis, offset):
    size = lax.axis_size(axis)
    return lax.ppermute(value, axis, [(i, i ^ offset) for i in range(size)])


def after(value, marker):
    return lax.optimization_barrier((value, marker))[0]


def paired(groups):
    return groups == 8


def block_order(groups):
    half = [offset for offset in range(groups) if offset % 2 == 0]
    return half + [offset + 1 for offset in half]


def to_own_order(value, axis, groups):
    if not paired(groups):
        return value
    here = lax.axis_index("dp")
    width = value.shape[axis]
    lead, tail = value.shape[:axis], value.shape[axis + 1 :]
    split = value.reshape(lead + (2, 2, 2, width // 8) + tail)
    return split, here


def into_order(value, groups):
    if not paired(groups):
        return value
    here = lax.axis_index("dp")
    shape = value.shape
    width = shape[-1] // groups
    blocks = value.reshape(shape[:-1] + (groups, width))
    ordered = [
        lax.dynamic_index_in_dim(blocks, here ^ offset, blocks.ndim - 2, keepdims=False)
        for offset in block_order(groups)
    ]
    return jnp.concatenate(ordered, axis=-1)


def from_order(value, groups):
    if not paired(groups):
        return value
    here = lax.axis_index("dp")
    shape = value.shape
    width = shape[-1] // groups
    blocks = value.reshape(shape[:-1] + (groups, width))
    order = block_order(groups)
    place = jnp.array([order.index(offset) for offset in range(groups)], jnp.int32)
    ordered = [
        lax.dynamic_index_in_dim(blocks, place[here ^ index], blocks.ndim - 2, keepdims=False)
        for index in range(groups)
    ]
    return jnp.concatenate(ordered, axis=-1)


def gather_blocks(block, axis):
    groups = lax.axis_size("dp")
    if not paired(groups):
        return lax.all_gather(block, "dp", axis=axis, tiled=True)
    held = [block] + [swap(block, "dp", offset) for offset in (2, 4, 6)]
    held = held + [swap(part, "dp", 1) for part in held]
    return jnp.concatenate(held, axis=axis)


def scatter_sum(kept, sent, axis):
    groups = lax.axis_size("dp")
    if not paired(groups):
        whole = jnp.concatenate([kept.astype(low), sent.astype(low)], axis=axis)
        return lax.psum_scatter(whole, "dp", scatter_dimension=axis, tiled=True).astype(wide)
    total = kept + swap(sent.astype(low), "dp", 1).astype(wide)
    span = total.shape[axis] // 4
    parts = [lax.slice_in_dim(total, i * span, (i + 1) * span, axis=axis) for i in range(4)]
    arrived = [swap(parts[i].astype(low), "dp", 2 * i).astype(wide) for i in (1, 2, 3)]
    return parts[0] + arrived[0] + arrived[1] + arrived[2]


def widen(value):
    return jnp.concatenate([value, swap(value, "shard", 1)], axis=0)


def narrow(value):
    half = value.shape[0] // 2
    here = (value[:half] + swap(value[half:].astype(low), "shard", 1).astype(wide)).astype(low)
    there = swap(here, "shard", 2)
    quarter = half // 2
    there = jnp.concatenate([there[quarter:], there[:quarter]], axis=0)
    return here.astype(wide) + there.astype(wide)


def route(dest, rows):
    table = dest[:, 0, :]
    groups = table.shape[0]
    capacity = rows // groups
    here = lax.axis_index("dp")
    own = lax.dynamic_index_in_dim(table, here, 0, keepdims=False)
    pack = own // rows
    index = jnp.arange(rows, dtype=jnp.int32)
    earlier = index[None, :] < index[:, None]
    rank = jnp.sum((earlier & (pack[None, :] == pack[:, None])).astype(jnp.int32), axis=1)
    slot = pack * capacity + rank
    to_slots = (slot[None, :] == index[:, None]).astype(low)
    mine = table // rows == here
    rank_in = jnp.sum((earlier[None] & mine[:, None, :]).astype(jnp.int32), axis=2)
    slot_in = jnp.arange(groups, dtype=jnp.int32)[:, None] * capacity + rank_in
    slot_in = jnp.where(mine, slot_in, rows).reshape(-1)
    row_in = (table % rows).reshape(-1)
    by_row = (row_in[None, :] == index[:, None]).astype(low)
    by_slot = (slot_in[None, :] == index[:, None]).astype(low)
    to_rows = contract_last(by_row, by_slot).astype(low)
    return to_slots, to_rows


def exchange(value, groups):
    return lax.all_to_all(value, "dp", split_axis=0, concat_axis=0, tiled=True)


def pack_layout(lengths, place):
    ends = jnp.cumsum(lengths)
    starts = ends - lengths
    member = jnp.sum((place[:, None] >= ends[None, :]).astype(jnp.int32), axis=1)
    onehot = member[:, None] == jnp.arange(lengths.shape[0], dtype=jnp.int32)[None, :]
    start = jnp.sum(jnp.where(onehot, starts[None, :], jnp.int32(0)), axis=1)
    bounds = jnp.array(level_ends, dtype=jnp.int32)
    level = jnp.sum(((place - start)[:, None] >= bounds[None, :]).astype(jnp.int32), axis=1)
    allowed = (member[:, None] == member[None, :]) & (level[None, :] <= level[:, None])
    return member, allowed


def attend(queries, keys, values, allowed):
    scores = jnp.einsum("thd,shd->hts", queries, keys, preferred_element_type=wide)
    scores = jnp.where(allowed[None], scores, masked_score)
    top = jnp.max(scores, axis=-1, keepdims=True)
    raised = jnp.exp(scores - top)
    total = jnp.sum(raised, axis=-1, keepdims=True)
    probs = (raised / total).astype(low)
    outputs = jnp.einsum("hts,shd->thd", probs, values, preferred_element_type=wide)
    return outputs, top + jnp.log(total)


def attend_back(queries, keys, values, allowed, log_total, grad_heads):
    scores = jnp.einsum("thd,shd->hts", queries, keys, preferred_element_type=wide)
    probs = jnp.where(allowed[None], jnp.exp(scores - log_total), 0.0)
    grad_probs = jnp.einsum("thd,shd->hts", grad_heads, values, preferred_element_type=wide)
    inner = jnp.sum(probs * grad_probs, axis=-1, keepdims=True)
    grad_scores = (probs * (grad_probs - inner)).astype(low)
    grad_queries = jnp.einsum("hts,shd->thd", grad_scores, keys, preferred_element_type=wide)
    grad_keys = jnp.einsum("hts,thd->shd", grad_scores, queries, preferred_element_type=wide)
    grad_values = jnp.einsum("hts,thd->shd", probs.astype(low), grad_heads, preferred_element_type=wide)
    return grad_queries, grad_keys, grad_values


def on_device(
    tokens,
    out_grad,
    dest,
    lengths,
    classes,
    class_table,
    w_ada,
    w_qkv,
    head_scale,
    w_proj,
    w_fc1,
    w_fc2,
):
    rows, width = tokens.shape
    groups, shards = lax.axis_size("dp"), lax.axis_size("shard")
    layers = w_ada.shape[0]
    pack = rows * shards
    heads_here = head_scale.shape[1]
    items = lengths.shape[1]
    slots = rows // groups
    columns = w_ada.shape[2]
    me = lax.axis_index("shard")

    to_slots, to_rows = route(dest, rows)
    coded = jnp.concatenate([classes[0] // 32, classes[0] % 32]).astype(low)
    coded = jnp.pad(coded, (0, width - 2 * items))
    leaving = jnp.concatenate(
        [
            matmul(to_slots, tokens).astype(low).reshape(groups, slots, width),
            jnp.broadcast_to(coded[None, None], (groups, 1, width)),
        ],
        axis=1,
    )
    arrived = exchange(leaving, groups)
    packed = matmul(to_rows, arrived[:, :slots].reshape(rows, width)).astype(low)
    packed = into_order(packed, groups)
    carried = jnp.concatenate([packed, swap(packed, "shard", 2)], axis=0).astype(wide)
    codes = arrived[:, slots, : 2 * items].astype(jnp.int32)
    all_classes = (codes[:, :items] * 32 + codes[:, items:]).reshape(-1)

    hits = (all_classes[:, None] == jnp.arange(class_table.shape[0], dtype=jnp.int32)[None, :]).astype(low)
    cond = matmul(hits, class_table)
    cond_low = jax.nn.silu(cond).astype(low)
    part = jnp.stack([matmul(cond_low, w_ada[layer]) for layer in range(layers)])
    part = part + swap(part, "shard", 1)
    part = part + swap(part, "shard", 2)
    part = jnp.swapaxes(part.reshape(layers, groups, items, columns), 0, 1)
    upper = lax.reduce_precision(part, 8, 7)
    both = jnp.stack([upper.astype(low), (part - upper).astype(low)], axis=1)
    both = both.reshape(groups, -1, width if (2 * layers * items * columns) % width == 0 else columns)
    grads_out = matmul(to_slots, out_grad).astype(low).reshape(groups, slots, width)
    if both.shape[2] == width:
        lines = both.shape[1]
        mixed_in = exchange(jnp.concatenate([both, grads_out], axis=1), groups)
        both, grads_out = mixed_in[:, :lines], mixed_in[:, lines:]
    else:
        both, grads_out = exchange(both, groups), exchange(grads_out, groups)
    both = both.reshape(groups, 2, layers, items, columns).astype(wide)
    modulation = jnp.transpose(both[:, 0] + both[:, 1], (1, 2, 0, 3)).reshape(layers, items, 6, width)
    modulation = into_order(modulation, groups)
    grad_packed = matmul(to_rows, grads_out.reshape(rows, width)).astype(low)
    grad_packed = into_order(grad_packed, groups)
    grad_carried = jnp.concatenate([grad_packed, swap(grad_packed, "shard", 2)], axis=0).astype(wide)

    place = jnp.concatenate(
        [(me ^ offset) * rows + jnp.arange(rows, dtype=jnp.int32) for offset in (0, 2, 1, 3)]
    )
    member, allowed = pack_layout(lengths[0], place)
    member_here = member[: 2 * rows, None]

    def spread(layer, part):
        choice = modulation[layer, :, part]
        result = choice[items - 1][None]
        for item in range(items - 2, -1, -1):
            result = jnp.where(member_here == item, choice[item][None], result)
        return result

    gains = [(spread(l, 0), spread(l, 1)) for l in range(layers)]
    scales = [(spread(l, 2), spread(l, 3)) for l in range(layers)]
    shifts = [(spread(l, 4), spread(l, 5)) for l in range(layers)]

    weights = []
    for layer in range(layers):
        qkv = w_qkv[layer].reshape(w_qkv.shape[1], -1)
        weights.append(
            (
                gather_blocks(qkv, 0),
                gather_blocks(w_proj[layer], 1),
                gather_blocks(w_fc1[layer], 0),
                gather_blocks(w_fc2[layer], 1),
            )
        )

    saved = []
    for layer in range(layers):
        qkv_full, proj_full, fc1_full, fc2_full = weights[layer]
        gain_one, gain_two = gains[layer]
        scale_one, scale_two = scales[layer]
        shift_one, shift_two = shifts[layer]
        first_all = widen(modulate(carried, scale_one, shift_one).astype(low))
        projected = matmul(first_all, qkv_full)
        span = projected.shape[1] // 3
        query = projected[:, :span].reshape(pack, heads_here, -1)
        key_part = projected[:, span : 2 * span].reshape(pack, heads_here, -1)
        values = projected[:, 2 * span :].reshape(pack, heads_here, -1).astype(low)
        queries = query_norm(query, head_scale[layer]).astype(low)
        keys = unit_rows(key_part).astype(low)
        heads_out, log_total = attend(queries, keys, values, allowed)
        heads_low = heads_out.reshape(pack, -1).astype(low)
        attended = narrow(matmul(heads_low, proj_full))
        middle = carried + gain_one * attended
        second_all = widen(modulate(middle, scale_two, shift_two).astype(low))
        hidden = matmul(second_all, fc1_full)
        activated = gelu_tanh(hidden).astype(low)
        branch = narrow(matmul(activated, fc2_full))
        saved.append(
            (carried, middle, first_all, query, key_part, queries, keys, values, log_total)
            + (heads_low, attended, second_all, hidden, activated, branch)
        )
        carried = middle + gain_two * branch

    choose = (member_here == jnp.arange(items, dtype=jnp.int32)[None, :]).astype(wide)

    def item_sums(value):
        return lax.dot_general(
            choose, value, (((0,), (0,)), ((), ())), precision=lax.Precision.HIGHEST
        )

    mixed_out = matmul(to_rows.T, from_order(carried[:rows].astype(low), groups)).astype(low)
    mixed_out = mixed_out.reshape(groups, slots, width)

    layer_grads = [None] * layers
    scale_grads = [None] * layers
    mod_grads = [None] * layers
    for layer in range(layers - 1, -1, -1):
        qkv_full, proj_full, fc1_full, fc2_full = weights[layer]
        gain_one, gain_two = gains[layer]
        scale_one, scale_two = scales[layer]
        shift_one, shift_two = shifts[layer]
        (
            carried_in,
            middle,
            first_all,
            query,
            key_part,
            queries,
            keys,
            values,
            log_total,
            heads_low,
            attended,
            second_all,
            hidden,
            activated,
            branch,
        ) = saved[layer]
        half = width // 2
        grad_gain_two = grad_carried * branch
        grad_branch = widen((grad_carried * gain_two).astype(low))
        grad_activated = contract_last(grad_branch, fc2_full)
        _, gelu_pull = jax.vjp(gelu_tanh, hidden)
        grad_hidden = gelu_pull(grad_activated)[0].astype(low)
        grad_second = narrow(contract_last(grad_hidden, fc1_full))
        grad_fc2 = scatter_sum(
            contract_rows(activated, grad_branch[:, :half]), contract_rows(activated, grad_branch[:, half:]), 1
        )
        grad_fc1 = scatter_sum(
            contract_rows(second_all[:, :half], grad_hidden), contract_rows(second_all[:, half:], grad_hidden), 0
        )
        _, second_pull = jax.vjp(modulate, middle, scale_two, shift_two)
        grad_middle_part, grad_scale_two, grad_shift_two = second_pull(grad_second)
        grad_middle = grad_carried + grad_middle_part
        grad_gain_one = grad_middle * attended
        grad_attended = widen((grad_middle * gain_one).astype(low))
        grad_heads = contract_last(grad_attended, proj_full).astype(low).reshape(pack, heads_here, -1)
        grad_queries, grad_keys, grad_values = attend_back(
            queries, keys, values, allowed, log_total, grad_heads
        )
        _, query_pull = jax.vjp(query_norm, query, head_scale[layer])
        grad_query, grad_log = query_pull(grad_queries)
        _, key_pull = jax.vjp(unit_rows, key_part)
        (grad_key,) = key_pull(grad_keys)
        grad_projected = jnp.concatenate(
            [grad_query.reshape(pack, -1), grad_key.reshape(pack, -1), grad_values.reshape(pack, -1)], axis=1
        ).astype(low)
        grad_first = narrow(contract_last(grad_projected, qkv_full))
        grad_proj = scatter_sum(
            contract_rows(heads_low, grad_attended[:, :half]), contract_rows(heads_low, grad_attended[:, half:]), 1
        )
        grad_qkv = scatter_sum(
            contract_rows(first_all[:, :half], grad_projected), contract_rows(first_all[:, half:], grad_projected), 0
        )
        _, first_pull = jax.vjp(modulate, carried_in, scale_one, shift_one)
        grad_carried_part, grad_scale_one, grad_shift_one = first_pull(grad_first)
        grad_carried = grad_middle + grad_carried_part
        sums = jnp.stack(
            [
                item_sums(term)
                for term in (
                    grad_gain_one,
                    grad_gain_two,
                    grad_scale_one,
                    grad_scale_two,
                    grad_shift_one,
                    grad_shift_two,
                )
            ],
            axis=1,
        )
        sums = (sums + swap(sums, "shard", 1)).astype(low)
        mod_grads[layer] = from_order(sums, groups).reshape(items, groups, columns)
        scale_grads[layer] = grad_log
        layer_grads[layer] = (grad_qkv.reshape(w_qkv.shape[1:]), grad_proj, grad_fc1, grad_fc2)

    grads_back = matmul(to_rows.T, from_order(grad_carried[:rows].astype(low), groups)).astype(low)
    grads_back = grads_back.reshape(groups, slots, width)
    sent = jnp.swapaxes(jnp.stack(mod_grads), 0, 2).reshape(groups, items * layers * columns)
    if sent.shape[1] % width:
        mods_back = exchange(sent, groups)
        rows_back = exchange(jnp.concatenate([mixed_out, grads_back], axis=1), groups)
    else:
        sent = sent.reshape(groups, -1, width)
        back = exchange(jnp.concatenate([mixed_out, grads_back, sent], axis=1), groups)
        rows_back, mods_back = back[:, : 2 * slots], back[:, 2 * slots :]
    mixed = matmul(to_slots.T, rows_back[:, :slots].reshape(rows, width)).astype(low)
    tokens_grad = matmul(to_slots.T, rows_back[:, slots:].reshape(rows, width)).astype(low)
    mods_back = mods_back.reshape(groups, items, layers, columns)
    mods_back = jnp.swapaxes(mods_back, 1, 2)
    grad_silu = jnp.zeros(cond.shape, wide)
    ada_grads = []
    for layer in range(layers):
        grad_modulation = mods_back[:, layer].reshape(groups * items, columns)
        ada_grads.append(contract_rows(cond_low, grad_modulation))
        grad_silu = grad_silu + contract_last(grad_modulation, w_ada[layer])
    logs = jnp.pad(jnp.stack(scale_grads).reshape(1, -1), ((0, 7), (0, cond.shape[1] - layers * heads_here)))
    summed = jnp.concatenate([grad_silu, logs], axis=0)
    if paired(groups):
        for offset in (1, 2, 4):
            summed = summed + swap(summed, "dp", offset)
    else:
        summed = lax.psum(summed, "dp")
    grad_silu = summed[: cond.shape[0]]
    scale_grad = summed[cond.shape[0], : layers * heads_here].reshape(layers, heads_here)
    _, silu_pull = jax.vjp(jax.nn.silu, cond)
    (grad_cond,) = silu_pull(grad_silu)
    table_grad = lax.dot_general(
        hits.astype(wide), grad_cond, (((0,), (0,)), ((), ())), precision=lax.Precision.HIGHEST
    )
    qkv_grad, proj_grad, fc1_grad, fc2_grad = (
        jnp.stack([layer_grads[layer][i] for layer in range(layers)]) for i in range(4)
    )
    return (
        mixed,
        tokens_grad,
        table_grad,
        jnp.stack(ada_grads),
        qkv_grad,
        scale_grad,
        proj_grad,
        fc1_grad,
        fc2_grad,
    )


def solution(mesh):
    placed = (
        P(("dp", "shard"), None),
        P(("dp", "shard"), None),
        P(None, "shard", None),
        P("dp", None),
        P("dp", None),
        P(None, "shard"),
        P(None, "shard", "dp"),
        P(None, "dp", None, "shard"),
        P(None, "shard"),
        P(None, "shard", "dp"),
        P(None, "dp", "shard"),
        P(None, "shard", "dp"),
    )
    return jax.shard_map(
        on_device,
        mesh=mesh,
        in_specs=placed,
        out_specs=(
            P(("dp", "shard"), None),
            P(("dp", "shard"), None),
            P(None, "shard"),
            P(None, "shard", "dp"),
            P(None, "dp", None, "shard"),
            P(None, "shard"),
            P(None, "shard", "dp"),
            P(None, "dp", "shard"),
            P(None, "shard", "dp"),
        ),
        check_vma=False,
    )
```

time: 1980 us -> 659 us (0.33)
  waiting for transfers between devices: 1570 us -> 279 us
  starting transfers between devices: 18.9 us -> 144 us
  blocking collectives: 109 us -> 0 us
  matrix products: 141 us -> 79.2 us
  local copies, waits for them, and re-layouts: 50.5 us -> 81.7 us
    reduce_scatter x18 -> x0, waiting for transfers between devices: 987 us -> none  [the longest x2 240 us: on_device(): lax.psum_scatter(grad_ada, 'dp', scatter_dimension=1, tiled=True)]
    all_gather x16 -> x0, waiting for transfers between devices: 478 us -> none  [the longest x8 136 us: widen(): return lax.all_gather(value, 'shard', axis=0, tiled=True)]
    ppermute x0 -> x121, waiting for transfers between devices: none -> 279 us  [swap(): return lax.ppermute(value, axis, [(i, i ^ offset) for i in range(size)])]
    ppermute x0 -> x121, starting transfers between devices: none -> 129 us  [swap(): return lax.ppermute(value, axis, [(i, i ^ offset) for i in range(size)])]
    psum x2 -> x0, waiting for transfers between devices: 101 us -> none  [the longest x1 78.6 us: on_device(): lax.psum((table_part, jnp.stack(scale_grads)), 'dp')]
    all_gather x2 -> x0, blocking collectives: 58.9 us -> none  [on_device(): lax.all_gather(w_proj[layer], 'dp', axis=1, tiled=True)]
    dot_general x32 -> x44, matrix products: 84.1 us -> 42.7 us  [the longest x19 16.1 us: matmul(): return jnp.dot(left, right, preferred_element_type=wide)]
    psum x2 -> x0, blocking collectives: 35.7 us -> none  [the longest x1 22.4 us: on_device(): lax.psum((table_part, jnp.stack(scale_grads)), 'dp')]
  transfers between devices with their start and end apart: 39 -> 124, of which waited for: 35 -> 52; matrix products, arithmetic and copies ran while one was open for 7% -> 26% of each run, Pallas kernels for 0% -> 0%
where the time goes in v1:
time: 659 us; the launch traced here: 653 us
  waiting for transfers between devices  279 us (42%)
  starting transfers between devices  144 us (22%)
  local copies, waits for them, and re-layouts  81.7 us (12%)
  matrix products  79.2 us (12%)
  other arithmetic  47.7 us (7%)
  between operations  21 us (3%)
    ppermute x121, waiting for transfers between devices, swap(): return lax.ppermute(value, axis, [(i, i ^ offset) for i in range(size)])  279 us
    ppermute x121, starting transfers between devices, swap(): return lax.ppermute(value, axis, [(i, i ^ offset) for i in range(size)])  129 us
    unnamed x602, local copies, waits for them, and re-layouts  52.4 us
    dot_general x18, matrix products, contract_rows(): lax.dot_general(left, right, (((0,), (0,)), ((), ())), preferred_element_...  22.3 us
    dot_general x19, matrix products, matmul(): return jnp.dot(left, right, preferred_element_type=wide)  16.1 us
    all_to_all x3, starting transfers between devices, exchange(): return lax.all_to_all(value, 'dp', split_axis=0, concat_axis=0, tiled=True)  14.6 us
    dot_general x11, matrix products, contract_last(): lax.dot_general(left, right, (((1,), (1,)), ((), ())), preferred_element_...  14.2 us
  transfers between devices with their start and end apart: 124, of which 52 were waited for; matrix products, arithmetic and copies ran while one was open for 26% of the time, Pallas kernels for 0%

profile of v1, /device:TPU:0, one launch (start us, length us, event | category | flops | bytes accessed | tf_op | source)
XLA Modules:
  0.0 652.5 jit_solution(16550827540752350880)
XLA Ops:
  2.3 3.0 collective-permute-start.48
  5.3 3.6 collective-permute-start.47
  14.3 6.1 all-to-all-start
  44.8 3.8 collective-permute-start.13
  55.9 2.8 collective-permute-start.40
  73.1 2.8 collective-permute-done.51
  102.9 6.3 collective-permute-done.4
  112.4 4.6 all-to-all-start.1
  128.2 8.5 %collective-permute-done.21 = bf16[128,1024]{1,0:T(8,128)(2,1)S(1)} collective-permute-done((bf16[128,1024]{1,0:T(8,128)(2,1)}, bf16[128,1024]{1,0:T(8,128)(2,1)S(1)}, u32[]{:S(2)}, u32[]{:S(2)}) %collective-permute-start.21) | collective-permute-done | bytes 262176 | tf_op jit(solution)/shard_map/ppermute | solution.py:48
  138.3 10.6 %collective-permute-done.22 = bf16[128,1024]{1,0:T(8,128)(2,1)S(1)} collective-permute-done((bf16[128,1024]{1,0:T(8,128)(2,1)}, bf16[128,1024]{1,0:T(8,128)(2,1)S(1)}, u32[]{:S(2)}, u32[]{:S(2)}) %collective-permute-start.22) | collective-permute-done | bytes 262176 | tf_op jit(solution)/shard_map/ppermute | solution.py:48
  156.1 3.4 collective-permute-done
  167.8 4.9 collective-permute-done.9
  185.6 4.5 collective-permute-done.28
  191.1 3.9 collective-permute-done.29
  201.1 3.1 collective-permute-done.25
  206.5 8.9 %collective-permute-done.26 = bf16[128,1024]{1,0:T(8,128)(2,1)S(1)} collective-permute-done((bf16[128,1024]{1,0:T(8,128)(2,1)S(1)}, bf16[128,1024]{1,0:T(8,128)(2,1)S(1)}, u32[]{:S(2)}, u32[]{:S(2)}) %collective-permute-start.26) | collective-permute-done | bytes 262176 | tf_op jit(solution)/shard_map/ppermute | solution.py:48
  217.9 8.8 %collective-permute-done.32 = bf16[1024,128]{1,0:T(8,128)(2,1)S(1)} collective-permute-done((bf16[1024,128]{1,0:T(8,128)(2,1)}, bf16[1024,128]{1,0:T(8,128)(2,1)S(1)}, u32[]{:S(2)}, u32[]{:S(2)}) %collective-permute-start.32) | collective-permute-done | bytes 262176 | tf_op jit(solution)/shard_map/ppermute | solution.py:48
  226.7 2.7 collective-permute-start.57
  244.0 10.8 %collective-permute-done.36 = bf16[256,1024]{1,0:T(8,128)(2,1)S(1)} collective-permute-done((bf16[256,1024]{1,0:T(8,128)(2,1)S(1)}, bf16[256,1024]{1,0:T(8,128)(2,1)S(1)}, u32[]{:S(2)}, u32[]{:S(2)}) %collective-permute-start.36) | collective-permute-done | bytes 524320 | tf_op jit(solution)/shard_map/ppermute | solution.py:48
  255.6 3.9 collective-permute-done.71
  268.8 4.5 collective-permute-done.43
  277.0 2.7 collective-permute-start.63
  280.4 2.6 fusion.64
  306.4 8.1 %collective-permute-done.59 = bf16[128,1024]{1,0:T(8,128)(2,1)S(1)} collective-permute-done((bf16[128,1024]{1,0:T(8,128)(2,1)S(1)}, bf16[128,1024]{1,0:T(8,128)(2,1)S(1)}, u32[]{:S(2)}, u32[]{:S(2)}) %collective-permute-start.59) | collective-permute-done | bytes 262176 | tf_op jit(solution)/shard_map/ppermute | solution.py:48
  317.3 8.4 %collective-permute-done.66 = bf16[1024,128]{1,0:T(8,128)(2,1)S(1)} collective-permute-done((bf16[1024,128]{1,0:T(8,128)(2,1)}, bf16[1024,128]{1,0:T(8,128)(2,1)S(1)}, u32[]{:S(2)}, u32[]{:S(2)}) %collective-permute-start.66) | collective-permute-done | bytes 262176 | tf_op jit(solution)/shard_map/ppermute | solution.py:48
  325.8 4.9 collective-permute-done.67
  349.2 16.4 %collective-permute-done.117 = bf16[1024,512]{1,0:T(8,128)(2,1)S(1)} collective-permute-done((bf16[1024,512]{1,0:T(8,128)(2,1)S(1)}, bf16[1024,512]{1,0:T(8,128)(2,1)S(1)}, u32[]{:S(2)}, u32[]{:S(2)}) %collective-permute-start.117) | collective-permute-done | bytes 1048608 | tf_op jit(solution)/shard_map/ppermute | solution.py:48
  370.1 17.4 %collective-permute-done.109 = bf16[512,1024]{1,0:T(8,128)(2,1)S(1)} collective-permute-done((bf16[512,1024]{1,0:T(8,128)(2,1)S(1)}, bf16[512,1024]{1,0:T(8,128)(2,1)S(1)}, u32[]{:S(2)}, u32[]{:S(2)}) %collective-permute-start.109) | collective-permute-done | bytes 1048608 | tf_op jit(solution)/shard_map/ppermute | solution.py:48
  415.7 8.9 %collective-permute-done.111 = bf16[128,1024]{1,0:T(8,128)(2,1)S(1)} collective-permute-done((bf16[128,1024]{1,0:T(8,128)(2,1)S(1)}, bf16[128,1024]{1,0:T(8,128)(2,1)S(1)}, u32[]{:S(2)}, u32[]{:S(2)}) %collective-permute-start.111) | collective-permute-done | bytes 262176 | tf_op jit(solution)/shard_map/ppermute | solution.py:48
  426.0 2.6 collective-permute-start.104
  431.9 2.9 collective-permute-done.93
  439.8 3.4 collective-permute-done.94
  443.2 5.6 collective-permute-done.96
  448.8 7.2 %collective-permute-done.95 = bf16[128,768]{1,0:T(8,128)(2,1)S(1)} collective-permute-done((bf16[128,768]{1,0:T(8,128)(2,1)S(1)}, bf16[128,768]{1,0:T(8,128)(2,1)S(1)}, u32[]{:S(2)}, u32[]{:S(2)}) %collective-permute-start.95) | collective-permute-done | bytes 196640 | tf_op jit(solution)/shard_map/ppermute | solution.py:48
  472.6 3.7 convolution_convert_fusion.1
  477.0 3.6 fusion.14
  490.6 12.0 %collective-permute-done.113 = bf16[1024,512]{1,0:T(8,128)(2,1)} collective-permute-done((bf16[1024,512]{1,0:T(8,128)(2,1)}, bf16[1024,512]{1,0:T(8,128)(2,1)}, u32[]{:S(2)}, u32[]{:S(2)}) %collective-permute-start.113) | collective-permute-done | bytes 1048608 | tf_op jit(solution)/shard_map/ppermute | solution.py:48
  502.6 3.0 fusion.303
  509.3 15.2 %collective-permute-done.105 = bf16[512,1024]{1,0:T(8,128)(2,1)} collective-permute-done((bf16[512,1024]{1,0:T(8,128)(2,1)}, bf16[512,1024]{1,0:T(8,128)(2,1)}, u32[]{:S(2)}, u32[]{:S(2)}) %collective-permute-start.105) | collective-permute-done | bytes 1048608 | tf_op jit(solution)/shard_map/ppermute | solution.py:48
  535.5 6.9 %collective-permute-done.106 = bf16[128,1024]{1,0:T(8,128)(2,1)S(1)} collective-permute-done((bf16[128,1024]{1,0:T(8,128)(2,1)S(1)}, bf16[128,1024]{1,0:T(8,128)(2,1)S(1)}, u32[]{:S(2)}, u32[]{:S(2)}) %collective-permute-start.106) | collective-permute-done | bytes 262176 | tf_op jit(solution)/shard_map/ppermute | solution.py:48
  542.4 11.2 %collective-permute-done.107 = bf16[128,1024]{1,0:T(8,128)(2,1)S(1)} collective-permute-done((bf16[128,1024]{1,0:T(8,128)(2,1)S(1)}, bf16[128,1024]{1,0:T(8,128)(2,1)S(1)}, u32[]{:S(2)}, u32[]{:S(2)}) %collective-permute-start.107) | collective-permute-done | bytes 262176 | tf_op jit(solution)/shard_map/ppermute | solution.py:48
  571.8 4.0 collective-permute-done.97
  593.7 3.9 all-to-all-start.2
  605.8 8.0 %collective-permute-done.90 = bf16[128,768]{1,0:T(8,128)(2,1)S(1)} collective-permute-done((bf16[128,768]{1,0:T(8,128)(2,1)S(1)}, bf16[128,768]{1,0:T(8,128)(2,1)S(1)}, u32[]{:S(2)}, u32[]{:S(2)}) %collective-permute-start.90) | collective-permute-done | bytes 196640 | tf_op jit(solution)/shard_map/ppermute | solution.py:48
  613.8 8.4 %collective-permute-done.92 = bf16[128,768]{1,0:T(8,128)(2,1)S(1)} collective-permute-done((bf16[128,768]{1,0:T(8,128)(2,1)S(1)}, bf16[128,768]{1,0:T(8,128)(2,1)S(1)}, u32[]{:S(2)}, u32[]{:S(2)}) %collective-permute-start.92) | collective-permute-done | bytes 196640 | tf_op jit(solution)/shard_map/ppermute | solution.py:48
  622.2 10.0 %collective-permute-done.91 = bf16[128,768]{1,0:T(8,128)(2,1)S(1)} collective-permute-done((bf16[128,768]{1,0:T(8,128)(2,1)S(1)}, bf16[128,768]{1,0:T(8,128)(2,1)S(1)}, u32[]{:S(2)}, u32[]{:S(2)}) %collective-permute-start.91) | collective-permute-done | bytes 196640 | tf_op jit(solution)/shard_map/ppermute | solution.py:48
  641.3 3.7 collective-permute-done.87
  646.3 3.6 collective-permute-done.88
  (1098 shorter events, 331.7 us)
Async XLA Ops:
  2.3 49.6 %collective-permute-start.48 = (bf16[256,128]{1,0:T(8,128)(2,1)}, bf16[256,128]{1,0:T(8,128)(2,1)}, u32[]{:S(2)}, u32[]{:S(2)}) collective-permute-start(bf16[256,128]{1,0:T(8,128)(2,1)} %get-tuple-element.197), channel_id=1, source_target_pairs={{0,4},{4,0},{8,12},{12,8},{16,20},{20,16},{24,28},{28,24},{1,5},{5... | collective-permute-start | bytes 196616 | tf_op jit(solution)/shard_map/ppermute | solution.py:48
  5.3 45.4 %collective-permute-start.47 = (bf16[256,128]{1,0:T(8,128)(2,1)}, bf16[256,128]{1,0:T(8,128)(2,1)S(1)}, u32[]{:S(2)}, u32[]{:S(2)}) collective-permute-start(bf16[256,128]{1,0:T(8,128)(2,1)} %get-tuple-element.197), channel_id=1, source_target_pairs={{0,24},{4,28},{8,16},{12,20},{16,8},{20,12},{24,0},{28,4},{1,25},{... | collective-permute-start | bytes 196616 | tf_op jit(solution)/shard_map/ppermute | solution.py:48
  8.9 41.2 %collective-permute-start.46 = (bf16[256,128]{1,0:T(8,128)(2,1)}, bf16[256,128]{1,0:T(8,128)(2,1)S(1)}, u32[]{:S(2)}, u32[]{:S(2)}) collective-permute-start(bf16[256,128]{1,0:T(8,128)(2,1)} %get-tuple-element.197), channel_id=1, source_target_pairs={{0,16},{4,20},{8,24},{12,28},{16,0},{20,4},{24,8},{28,12},{1,17},{... | collective-permute-start | bytes 196616 | tf_op jit(solution)/shard_map/ppermute | solution.py:48
  8.9 35.9 %collective-permute-start.45 = (bf16[256,128]{1,0:T(8,128)(2,1)}, bf16[256,128]{1,0:T(8,128)(2,1)}, u32[]{:S(2)}, u32[]{:S(2)}) collective-permute-start(bf16[256,128]{1,0:T(8,128)(2,1)} %get-tuple-element.197), channel_id=1, source_target_pairs={{0,8},{4,12},{8,0},{12,4},{16,24},{20,28},{24,16},{28,20},{1,9},{5... | collective-permute-start | bytes 196616 | tf_op jit(solution)/shard_map/ppermute | solution.py:48
  9.7 52.5 %collective-permute-start.14 = (bf16[256,128]{1,0:T(8,128)(2,1)}, bf16[256,128]{1,0:T(8,128)(2,1)}, u32[]{:S(2)}, u32[]{:S(2)}) collective-permute-start(bf16[256,128]{1,0:T(8,128)(2,1)} %get-tuple-element.198), channel_id=1, source_target_pairs={{0,4},{4,0},{8,12},{12,8},{16,20},{20,16},{24,28},{28,24},{1,5},{5... | collective-permute-start | bytes 196616 | tf_op jit(solution)/shard_map/ppermute | solution.py:48
  14.3 79.1 %all-to-all-start = ((bf16[8,17,1024]{2,1,0:T(8,128)(2,1)}), bf16[8,17,1024]{2,1,0:T(8,128)(2,1)S(1)}, u32[]{:S(2)}, u32[]{:S(2)}) async-start(bf16[8,17,1024]{2,1,0:T(8,128)(2,1)} %pad_maximum_fusion.37), calls=%async_computation | async-start | bytes 786432 | tf_op jit(solution)/shard_map/all_to_all | solution.py:162
  52.0 47.8 %collective-permute-start.41 = (bf16[128,768]{0,1:T(8,128)(2,1)S(1)}, bf16[128,768]{0,1:T(8,128)(2,1)}, u32[]{:S(2)}, u32[]{:S(2)}) collective-permute-start(bf16[128,768]{0,1:T(8,128)(2,1)S(1)} %bitcast.618), channel_id=1, source_target_pairs={{0,4},{4,0},{8,12},{12,8},{16,20},{20,16},{24,28},{28,24},{1,5},{5... | collective-permute-start | bytes 589832 | tf_op jit(solution)/shard_map/ppermute | solution.py:48
  55.9 40.6 %collective-permute-start.40 = (bf16[128,768]{0,1:T(8,128)(2,1)S(1)}, bf16[128,768]{0,1:T(8,128)(2,1)S(1)}, u32[]{:S(2)}, u32[]{:S(2)}) collective-permute-start(bf16[128,768]{0,1:T(8,128)(2,1)S(1)} %bitcast.619), channel_id=1, source_target_pairs={{0,24},{4,28},{8,16},{12,20},{16,8},{20,12},{24,0},{28,4},{1,25},{... | collective-permute-start | bytes 589832 | tf_op jit(solution)/shard_map/ppermute | solution.py:48
  59.3 35.5 %collective-permute-start.39 = (bf16[128,768]{0,1:T(8,128)(2,1)S(1)}, bf16[128,768]{0,1:T(8,128)(2,1)}, u32[]{:S(2)}, u32[]{:S(2)}) collective-permute-start(bf16[128,768]{0,1:T(8,128)(2,1)S(1)} %bitcast.620), channel_id=1, source_target_pairs={{0,16},{4,20},{8,24},{12,28},{16,0},{20,4},{24,8},{28,12},{1,17},{... | collective-permute-start | bytes 589832 | tf_op jit(solution)/shard_map/ppermute | solution.py:48
  60.1 30.7 %collective-permute-start.38 = (bf16[128,768]{0,1:T(8,128)(2,1)S(1)}, bf16[128,768]{0,1:T(8,128)(2,1)S(1)}, u32[]{:S(2)}, u32[]{:S(2)}) collective-permute-start(bf16[128,768]{0,1:T(8,128)(2,1)S(1)} %bitcast.621), channel_id=1, source_target_pairs={{0,8},{4,12},{8,0},{12,4},{16,24},{20,28},{24,16},{28,20},{1,9},{5... | collective-permute-start | bytes 589832 | tf_op jit(solution)/shard_map/ppermute | solution.py:48
  88.7 34.2 %collective-permute-start.7 = (bf16[128,768]{0,1:T(8,128)(2,1)S(1)}, bf16[128,768]{0,1:T(8,128)(2,1)}, u32[]{:S(2)}, u32[]{:S(2)}) collective-permute-start(bf16[128,768]{0,1:T(8,128)(2,1)S(1)} %bitcast.613), channel_id=1, source_target_pairs={{0,4},{4,0},{8,12},{12,8},{16,20},{20,16},{24,28},{28,24},{1,5},{5... | collective-permute-start | bytes 589832 | tf_op jit(solution)/shard_map/ppermute | solution.py:48
  90.8 29.0 %collective-permute-start.6 = (bf16[128,768]{0,1:T(8,128)(2,1)S(1)}, bf16[128,768]{0,1:T(8,128)(2,1)}, u32[]{:S(2)}, u32[]{:S(2)}) collective-permute-start(bf16[128,768]{0,1:T(8,128)(2,1)S(1)} %bitcast.614), channel_id=1, source_target_pairs={{0,24},{4,28},{8,16},{12,20},{16,8},{20,12},{24,0},{28,4},{1,25},{... | collective-permute-start | bytes 589832 | tf_op jit(solution)/shard_map/ppermute | solution.py:48
  109.2 183.6 %collective-permute-start.58 = (bf16[128,1024]{1,0:T(8,128)(2,1)}, bf16[128,1024]{1,0:T(8,128)(2,1)}, u32[]{:S(2)}, u32[]{:S(2)}) collective-permute-start(bf16[128,1024]{1,0:T(8,128)(2,1)} %get-tuple-element.89), channel_id=1, source_target_pairs={{0,4},{4,0},{8,12},{12,8},{16,20},{20,16},{24,28},{28,24},{1,5},{5... | collective-permute-start | bytes 786440 | tf_op jit(solution)/shard_map/ppermute | solution.py:48
  112.4 37.5 %all-to-all-start.1 = ((bf16[8,28,1024]{2,1,0:T(8,128)(2,1)}), bf16[8,28,1024]{2,1,0:T(8,128)(2,1)S(1)}, u32[]{:S(2)}, u32[]{:S(2)}) async-start(bf16[8,28,1024]{2,1,0:T(8,128)(2,1)} %pad_maximum_fusion.28), calls=%async_computation.1 | async-start | bytes 1048576 | tf_op jit(solution)/shard_map/all_to_all | solution.py:162
  117.1 47.9 %collective-permute-start.24 = (bf16[128,1024]{1,0:T(8,128)(2,1)}, bf16[128,1024]{1,0:T(8,128)(2,1)S(1)}, u32[]{:S(2)}, u32[]{:S(2)}) collective-permute-start(bf16[128,1024]{1,0:T(8,128)(2,1)} %get-tuple-element.90), channel_id=1, source_target_pairs={{0,4},{4,0},{8,12},{12,8},{16,20},{20,16},{24,28},{28,24},{1,5},{5... | collective-permute-start | bytes 786440 | tf_op jit(solution)/shard_map/ppermute | solution.py:48
  122.9 26.0 %collective-permute-start.22 = (bf16[128,1024]{1,0:T(8,128)(2,1)}, bf16[128,1024]{1,0:T(8,128)(2,1)S(1)}, u32[]{:S(2)}, u32[]{:S(2)}) collective-permute-start(bf16[128,1024]{1,0:T(8,128)(2,1)} %get-tuple-element.90), channel_id=1, source_target_pairs={{0,16},{4,20},{8,24},{12,28},{16,0},{20,4},{24,8},{28,12},{1,17},{... | collective-permute-start | bytes 786440 | tf_op jit(solution)/shard_map/ppermute | solution.py:48
  126.9 36.1 %collective-permute-start.23 = (bf16[128,1024]{1,0:T(8,128)(2,1)}, bf16[128,1024]{1,0:T(8,128)(2,1)}, u32[]{:S(2)}, u32[]{:S(2)}) collective-permute-start(bf16[128,1024]{1,0:T(8,128)(2,1)} %get-tuple-element.90), channel_id=1, source_target_pairs={{0,24},{4,28},{8,16},{12,20},{16,8},{20,12},{24,0},{28,4},{1,25},{... | collective-permute-start | bytes 786440 | tf_op jit(solution)/shard_map/ppermute | solution.py:48
  136.7 62.4 %collective-permute-start.31 = (bf16[1024,128]{1,0:T(8,128)(2,1)}, bf16[1024,128]{1,0:T(8,128)(2,1)}, u32[]{:S(2)}, u32[]{:S(2)}) collective-permute-start(bf16[1024,128]{1,0:T(8,128)(2,1)} %get-tuple-element.86), channel_id=1, source_target_pairs={{0,4},{4,0},{8,12},{12,8},{16,20},{20,16},{24,28},{28,24},{1,5},{5... | collective-permute-start | bytes 786440 | tf_op jit(solution)/shard_map/ppermute | solution.py:48
  172.7 24.2 %collective-permute-start.30 = (bf16[1024,128]{1,0:T(8,128)(2,1)}, bf16[1024,128]{1,0:T(8,128)(2,1)}, u32[]{:S(2)}, u32[]{:S(2)}) collective-permute-start(bf16[1024,128]{1,0:T(8,128)(2,1)} %get-tuple-element.86), channel_id=1, source_target_pairs={{0,24},{4,28},{8,16},{12,20},{16,8},{20,12},{24,0},{28,4},{1,25},{... | collective-permute-start | bytes 786440 | tf_op jit(solution)/shard_map/ppermute | solution.py:48
  204.2 25.2 %collective-permute-start.33 = (bf16[1024,128]{1,0:T(8,128)(2,1)}, bf16[1024,128]{1,0:T(8,128)(2,1)S(1)}, u32[]{:S(2)}, u32[]{:S(2)}) collective-permute-start(bf16[1024,128]{1,0:T(8,128)(2,1)} %collective-permute-done.29), channel_id=1, source_target_pairs={{0,4},{4,0},{8,12},{12,8},{16,20},{20,16},{24,28},{28,24},{1,5},{5... | collective-permute-start | bytes 786440 | tf_op jit(solution)/shard_map/ppermute | solution.py:48
  226.7 38.7 %collective-permute-start.57 = (bf16[128,1024]{1,0:T(8,128)(2,1)S(1)}, bf16[128,1024]{1,0:T(8,128)(2,1)S(1)}, u32[]{:S(2)}, u32[]{:S(2)}) collective-permute-start(bf16[128,1024]{1,0:T(8,128)(2,1)S(1)} %copy-done.107), channel_id=1, source_target_pairs={{0,24},{4,28},{8,16},{12,20},{16,8},{20,12},{24,0},{28,4},{1,25},{... | collective-permute-start | bytes 786440 | tf_op jit(solution)/shard_map/ppermute | solution.py:48
  229.5 34.9 %collective-permute-start.56 = (bf16[128,1024]{1,0:T(8,128)(2,1)S(1)}, bf16[128,1024]{1,0:T(8,128)(2,1)S(1)}, u32[]{:S(2)}, u32[]{:S(2)}) collective-permute-start(bf16[128,1024]{1,0:T(8,128)(2,1)S(1)} %copy-done.107), channel_id=1, source_target_pairs={{0,16},{4,20},{8,24},{12,28},{16,0},{20,4},{24,8},{28,12},{1,17},{... | collective-permute-start | bytes 786440 | tf_op jit(solution)/shard_map/ppermute | solution.py:48
  254.7 48.3 %collective-permute-start.65 = (bf16[1024,128]{1,0:T(8,128)(2,1)}, bf16[1024,128]{1,0:T(8,128)(2,1)}, u32[]{:S(2)}, u32[]{:S(2)}) collective-permute-start(bf16[1024,128]{1,0:T(8,128)(2,1)} %get-tuple-element.85), channel_id=1, source_target_pairs={{0,4},{4,0},{8,12},{12,8},{16,20},{20,16},{24,28},{28,24},{1,5},{5... | collective-permute-start | bytes 786440 | tf_op jit(solution)/shard_map/ppermute | solution.py:48
  273.3 27.8 %collective-permute-start.64 = (bf16[1024,128]{1,0:T(8,128)(2,1)}, bf16[1024,128]{1,0:T(8,128)(2,1)}, u32[]{:S(2)}, u32[]{:S(2)}) collective-permute-start(bf16[1024,128]{1,0:T(8,128)(2,1)} %get-tuple-element.85), channel_id=1, source_target_pairs={{0,24},{4,28},{8,16},{12,20},{16,8},{20,12},{24,0},{28,4},{1,25},{... | collective-permute-start | bytes 786440 | tf_op jit(solution)/shard_map/ppermute | solution.py:48
  277.0 21.9 %collective-permute-start.63 = (bf16[1024,128]{1,0:T(8,128)(2,1)}, bf16[1024,128]{1,0:T(8,128)(2,1)}, u32[]{:S(2)}, u32[]{:S(2)}) collective-permute-start(bf16[1024,128]{1,0:T(8,128)(2,1)} %get-tuple-element.85), channel_id=1, source_target_pairs={{0,16},{4,20},{8,24},{12,28},{16,0},{20,4},{24,8},{28,12},{1,17},{... | collective-permute-start | bytes 786440 | tf_op jit(solution)/shard_map/ppermute | solution.py:48
  294.1 23.3 %collective-permute-start.61 = (bf16[128,1024]{1,0:T(8,128)(2,1)S(1)}, bf16[128,1024]{1,0:T(8,128)(2,1)S(1)}, u32[]{:S(2)}, u32[]{:S(2)}) collective-permute-start(bf16[128,1024]{1,0:T(8,128)(2,1)S(1)} %copy-done.104), channel_id=1, source_target_pairs={{0,4},{4,0},{8,12},{12,8},{16,20},{20,16},{24,28},{28,24},{1,5},{5... | collective-permute-start | bytes 786440 | tf_op jit(solution)/shard_map/ppermute | solution.py:48
  303.0 30.6 %collective-permute-start.68 = (bf16[1024,128]{1,0:T(8,128)(2,1)}, bf16[1024,128]{1,0:T(8,128)(2,1)S(1)}, u32[]{:S(2)}, u32[]{:S(2)}) collective-permute-start(bf16[1024,128]{1,0:T(8,128)(2,1)} %collective-permute-done.64), channel_id=1, source_target_pairs={{0,4},{4,0},{8,12},{12,8},{16,20},{20,16},{24,28},{28,24},{1,5},{5... | collective-permute-start | bytes 786440 | tf_op jit(solution)/shard_map/ppermute | solution.py:48
  339.6 26.1 %collective-permute-start.117 = (bf16[1024,512]{1,0:T(8,128)(2,1)S(1)}, bf16[1024,512]{1,0:T(8,128)(2,1)S(1)}, u32[]{:S(2)}, u32[]{:S(2)}) collective-permute-start(bf16[1024,512]{1,0:T(8,128)(2,1)S(1)} %convolution_convert_fusion), channel_id=1, source_target_pairs={{0,4},{4,0},{8,12},{12,8},{16,20},{20,16},{24,28},{28,24},{1,5},{5... | collective-permute-start | bytes 3145736 | tf_op jit(solution)/shard_map/ppermute | solution.py:48
  345.9 41.6 %collective-permute-start.109 = (bf16[512,1024]{1,0:T(8,128)(2,1)S(1)}, bf16[512,1024]{1,0:T(8,128)(2,1)S(1)}, u32[]{:S(2)}, u32[]{:S(2)}) collective-permute-start(bf16[512,1024]{1,0:T(8,128)(2,1)S(1)} %convolution_convert_fusion.2), channel_id=1, source_target_pairs={{0,4},{4,0},{8,12},{12,8},{16,20},{20,16},{24,28},{28,24},{1,5},{5... | collective-permute-start | bytes 3145736 | tf_op jit(solution)/shard_map/ppermute | solution.py:48
  346.9 45.2 %collective-permute-start.70 = (bf16[256,1024]{1,0:T(8,128)(2,1)S(1)}, bf16[256,1024]{1,0:T(8,128)(2,1)S(1)}, u32[]{:S(2)}, u32[]{:S(2)}) collective-permute-start(bf16[256,1024]{1,0:T(8,128)(2,1)S(1)} %fusion.74), channel_id=1, source_target_pairs={{0,2},{1,3},{2,0},{3,1},{4,6},{5,7},{6,4},{7,5},{8,10},{9,11},{10,... | collective-permute-start | bytes 1572872 | tf_op jit(solution)/shard_map/ppermute | solution.py:48
  348.6 41.4 %collective-permute-start.74 = (bf16[256,1024]{1,0:T(8,128)(2,1)S(1)}, bf16[256,1024]{1,0:T(8,128)(2,1)S(1)}, u32[]{:S(2)}, u32[]{:S(2)}) collective-permute-start(bf16[256,1024]{1,0:T(8,128)(2,1)S(1)} %fusion.73), channel_id=1, source_target_pairs={{0,2},{1,3},{2,0},{3,1},{4,6},{5,7},{6,4},{7,5},{8,10},{9,11},{10,... | collective-permute-start | bytes 1572872 | tf_op jit(solution)/shard_map/ppermute | solution.py:48
  366.9 31.2 %collective-permute-start.118 = (bf16[1024,128]{1,0:T(8,128)(2,1)S(1)}, bf16[1024,128]{1,0:T(8,128)(2,1)S(1)}, u32[]{:S(2)}, u32[]{:S(2)}) collective-permute-start(bf16[1024,128]{1,0:T(8,128)(2,1)S(1)} %get-tuple-element.58), channel_id=1, source_target_pairs={{0,8},{4,12},{8,0},{12,4},{16,24},{20,28},{24,16},{28,20},{1,9},{5... | collective-permute-start | bytes 786440 | tf_op jit(solution)/shard_map/ppermute | solution.py:48
  368.8 31.8 %collective-permute-start.120 = (bf16[1024,128]{1,0:T(8,128)(2,1)S(1)}, bf16[1024,128]{1,0:T(8,128)(2,1)S(1)}, u32[]{:S(2)}, u32[]{:S(2)}) collective-permute-start(bf16[1024,128]{1,0:T(8,128)(2,1)S(1)} %get-tuple-element.59), channel_id=1, source_target_pairs={{0,24},{4,28},{8,16},{12,20},{16,8},{20,12},{24,0},{28,4},{1,25},{... | collective-permute-start | bytes 786440 | tf_op jit(solution)/shard_map/ppermute | solution.py:48
  390.1 24.8 %collective-permute-start.110 = (bf16[128,1024]{1,0:T(8,128)(2,1)S(1)}, bf16[128,1024]{1,0:T(8,128)(2,1)S(1)}, u32[]{:S(2)}, u32[]{:S(2)}) collective-permute-start(bf16[128,1024]{1,0:T(8,128)(2,1)S(1)} %get-tuple-element.64), channel_id=1, source_target_pairs={{0,8},{4,12},{8,0},{12,4},{16,24},{20,28},{24,16},{28,20},{1,9},{5... | collective-permute-start | bytes 786440 | tf_op jit(solution)/shard_map/ppermute | solution.py:48
  400.5 24.1 %collective-permute-start.111 = (bf16[128,1024]{1,0:T(8,128)(2,1)S(1)}, bf16[128,1024]{1,0:T(8,128)(2,1)S(1)}, u32[]{:S(2)}, u32[]{:S(2)}) collective-permute-start(bf16[128,1024]{1,0:T(8,128)(2,1)S(1)} %get-tuple-element.66), channel_id=1, source_target_pairs={{0,16},{4,20},{8,24},{12,28},{16,0},{20,4},{24,8},{28,12},{1,17},{... | collective-permute-start | bytes 786440 | tf_op jit(solution)/shard_map/ppermute | solution.py:48
  430.4 28.4 %collective-permute-start.77 = (bf16[256,1024]{1,0:T(8,128)(2,1)}, bf16[256,1024]{1,0:T(8,128)(2,1)}, u32[]{:S(2)}, u32[]{:S(2)}) collective-permute-start(bf16[256,1024]{1,0:T(8,128)(2,1)} %fusion.72), channel_id=1, source_target_pairs={{0,2},{1,3},{2,0},{3,1},{4,6},{5,7},{6,4},{7,5},{8,10},{9,11},{10,... | collective-permute-start | bytes 1572872 | tf_op jit(solution)/shard_map/ppermute | solution.py:48
  476.3 26.3 %collective-permute-start.113 = (bf16[1024,512]{1,0:T(8,128)(2,1)}, bf16[1024,512]{1,0:T(8,128)(2,1)}, u32[]{:S(2)}, u32[]{:S(2)}) collective-permute-start(bf16[1024,512]{1,0:T(8,128)(2,1)} %convolution_convert_fusion.1), channel_id=1, source_target_pairs={{0,4},{4,0},{8,12},{12,8},{16,20},{20,16},{24,28},{28,24},{1,5},{5... | collective-permute-start | bytes 3145736 | tf_op jit(solution)/shard_map/ppermute | solution.py:48
  486.3 38.3 %collective-permute-start.105 = (bf16[512,1024]{1,0:T(8,128)(2,1)}, bf16[512,1024]{1,0:T(8,128)(2,1)}, u32[]{:S(2)}, u32[]{:S(2)}) collective-permute-start(bf16[512,1024]{1,0:T(8,128)(2,1)} %convolution_convert_fusion.3), channel_id=1, source_target_pairs={{0,4},{4,0},{8,12},{12,8},{16,20},{20,16},{24,28},{28,24},{1,5},{5... | collective-permute-start | bytes 3145736 | tf_op jit(solution)/shard_map/ppermute | solution.py:48
  489.1 37.7 %collective-permute-start.80 = (bf16[256,1024]{1,0:T(8,128)(2,1)S(1)}, bf16[256,1024]{1,0:T(8,128)(2,1)S(1)}, u32[]{:S(2)}, u32[]{:S(2)}) collective-permute-start(bf16[256,1024]{1,0:T(8,128)(2,1)S(1)} %fusion.71), channel_id=1, source_target_pairs={{0,2},{1,3},{2,0},{3,1},{4,6},{5,7},{6,4},{7,5},{8,10},{9,11},{10,... | collective-permute-start | bytes 1572872 | tf_op jit(solution)/shard_map/ppermute | solution.py:48
  505.8 26.6 %collective-permute-start.114 = (bf16[1024,128]{1,0:T(8,128)(2,1)S(1)}, bf16[1024,128]{1,0:T(8,128)(2,1)S(1)}, u32[]{:S(2)}, u32[]{:S(2)}) collective-permute-start(bf16[1024,128]{1,0:T(8,128)(2,1)S(1)} %get-tuple-element.55), channel_id=1, source_target_pairs={{0,8},{4,12},{8,0},{12,4},{16,24},{20,28},{24,16},{28,20},{1,9},{5... | collective-permute-start | bytes 786440 | tf_op jit(solution)/shard_map/ppermute | solution.py:48
  505.9 28.4 %collective-permute-start.116 = (bf16[1024,128]{1,0:T(8,128)(2,1)S(1)}, bf16[1024,128]{1,0:T(8,128)(2,1)S(1)}, u32[]{:S(2)}, u32[]{:S(2)}) collective-permute-start(bf16[1024,128]{1,0:T(8,128)(2,1)S(1)} %get-tuple-element.56), channel_id=1, source_target_pairs={{0,24},{4,28},{8,16},{12,20},{16,8},{20,12},{24,0},{28,4},{1,25},{... | collective-permute-start | bytes 786440 | tf_op jit(solution)/shard_map/ppermute | solution.py:48
  507.6 26.7 %collective-permute-start.115 = (bf16[1024,128]{1,0:T(8,128)(2,1)S(1)}, bf16[1024,128]{1,0:T(8,128)(2,1)S(1)}, u32[]{:S(2)}, u32[]{:S(2)}) collective-permute-start(bf16[1024,128]{1,0:T(8,128)(2,1)S(1)} %get-tuple-element.57), channel_id=1, source_target_pairs={{0,16},{4,20},{8,24},{12,28},{16,0},{20,4},{24,8},{28,12},{1,17},{... | collective-permute-start | bytes 786440 | tf_op jit(solution)/shard_map/ppermute | solution.py:48
  570.4 27.2 %collective-permute-start.89 = (bf16[512,768]{1,0:T(8,128)(2,1)}, bf16[512,768]{1,0:T(8,128)(2,1)}, u32[]{:S(2)}, u32[]{:S(2)}) collective-permute-start(bf16[512,768]{1,0:T(8,128)(2,1)} %convolution_convert_fusion.5), channel_id=1, source_target_pairs={{0,4},{4,0},{8,12},{12,8},{16,20},{20,16},{24,28},{28,24},{1,5},{5... | collective-permute-start | bytes 2359304 | tf_op jit(solution)/shard_map/ppermute | solution.py:48
  577.9 26.3 %collective-permute-start.98 = (bf16[256,128]{1,0:T(8,128)(2,1)}, bf16[256,128]{1,0:T(8,128)(2,1)}, u32[]{:S(2)}, u32[]{:S(2)}) collective-permute-start(bf16[256,128]{1,0:T(8,128)(2,1)} %get-tuple-element.101), channel_id=1, source_target_pairs={{0,8},{4,12},{8,0},{12,4},{16,24},{20,28},{24,16},{28,20},{1,9},{5... | collective-permute-start | bytes 196616 | tf_op jit(solution)/shard_map/ppermute | solution.py:48
  577.9 26.3 %collective-permute-start.100 = (bf16[256,128]{1,0:T(8,128)(2,1)}, bf16[256,128]{1,0:T(8,128)(2,1)}, u32[]{:S(2)}, u32[]{:S(2)}) collective-permute-start(bf16[256,128]{1,0:T(8,128)(2,1)} %get-tuple-element.102), channel_id=1, source_target_pairs={{0,24},{4,28},{8,16},{12,20},{16,8},{20,12},{24,0},{28,4},{1,25},{... | collective-permute-start | bytes 196616 | tf_op jit(solution)/shard_map/ppermute | solution.py:48
  579.5 24.6 %collective-permute-start.99 = (bf16[256,128]{1,0:T(8,128)(2,1)}, bf16[256,128]{1,0:T(8,128)(2,1)}, u32[]{:S(2)}, u32[]{:S(2)}) collective-permute-start(bf16[256,128]{1,0:T(8,128)(2,1)} %get-tuple-element.103), channel_id=1, source_target_pairs={{0,16},{4,20},{8,24},{12,28},{16,0},{20,4},{24,8},{28,12},{1,17},{... | collective-permute-start | bytes 196616 | tf_op jit(solution)/shard_map/ppermute | solution.py:48
  593.7 40.0 %all-to-all-start.2 = ((bf16[8,38,1024]{2,1,0:T(8,128)(2,1)}), bf16[8,38,1024]{2,1,0:T(8,128)(2,1)S(1)}, u32[]{:S(2)}, u32[]{:S(2)}) async-start(bf16[8,38,1024]{2,1,0:T(8,128)(2,1)} %pad_maximum_fusion.26), calls=%async_computation.2 | async-start | bytes 1310720 | tf_op jit(solution)/shard_map/all_to_all | solution.py:162
  604.1 28.1 %collective-permute-start.91 = (bf16[128,768]{1,0:T(8,128)(2,1)S(1)}, bf16[128,768]{1,0:T(8,128)(2,1)S(1)}, u32[]{:S(2)}, u32[]{:S(2)}) collective-permute-start(bf16[128,768]{1,0:T(8,128)(2,1)S(1)} %get-tuple-element.69), channel_id=1, source_target_pairs={{0,16},{4,20},{8,24},{12,28},{16,0},{20,4},{24,8},{28,12},{1,17},{... | collective-permute-start | bytes 589832 | tf_op jit(solution)/shard_map/ppermute | solution.py:48
  (322 other events, 3560.1 us)

commit v2 on v1

v2 whole, which is shorter than its diff:
```python
import functools

import jax
import jax.numpy as jnp
from jax import lax
from jax.experimental import pallas as pl
from jax.experimental.pallas import tpu as pltpu
from jax.sharding import PartitionSpec as P

epsilon = 1e-06
level_ends = (1, 5, 14, 30, 55, 91, 155, 255, 424, 680)
wide = jnp.float32
low = jnp.bfloat16
root = 0.7978845608028654
cubic = 0.044715


def matmul(left, right):
    return jnp.dot(left, right, preferred_element_type=wide)


def contract_rows(left, right):
    return lax.dot_general(left, right, (((0,), (0,)), ((), ())), preferred_element_type=wide)


def contract_last(left, right):
    return lax.dot_general(left, right, (((1,), (1,)), ((), ())), preferred_element_type=wide)


def swap(value, axis, offset):
    size = lax.axis_size(axis)
    return lax.ppermute(value, axis, [(i, i ^ offset) for i in range(size)])


def tie(value, *others):
    return lax.optimization_barrier((value, others))[0]


slow_groups = [[0, 2, 4, 6], [1, 3, 5, 7]]


def paired(groups):
    return groups == 8


def own_order(groups):
    here = lax.axis_index("dp")
    if not paired(groups):
        return jnp.arange(groups, dtype=jnp.int32)
    place = jnp.arange(groups, dtype=jnp.int32)
    return (lax.rem(here // 2 + 4 - place % 4, 4) * 2 + (here % 2 ^ place // 4)).astype(jnp.int32)


def straight(block):
    return [lax.ppermute(block, "dp", [(i, (i + 2 * back) % 8) for i in range(8)]) for back in (1, 2, 3)]


def columns_of(piece, out, first):
    depth, width = piece.shape
    for index in range(width // 128):
        out[first + index * depth : first + (index + 1) * depth, :] = piece[:, index * 128 : (index + 1) * 128]


def pack_mix_kernel(qkv, proj, *refs, layer):
    out = refs[-1]
    columns_of(qkv[...], out, 0)
    first = qkv.shape[0] * qkv.shape[1] // 128
    out[first : first + proj.shape[1], :] = proj[layer]
    if len(refs) > 1:
        out[first + proj.shape[1] :, :] = refs[0][layer]


def pack_mix(qkv, proj, layer, *more):
    height = qkv.shape[0] * qkv.shape[1] // 128 + proj.shape[1] + sum(value.shape[1] for value in more)
    return call(functools.partial(pack_mix_kernel, layer=layer), [((height, 128), low)], qkv, proj, *more)[0]


def pack_fc1_kernel(fc1, out, *, layer):
    columns_of(fc1[layer], out, 0)


def pack_fc1(fc1, layer):
    height = fc1.shape[1] * fc1.shape[2] // 128
    return call(functools.partial(pack_fc1_kernel, layer=layer), [((height, 128), low)], fc1)[0]


def stack_kernel(*refs):
    out = refs[-1]
    size = refs[0].shape[0]
    for index, ref in enumerate(refs[:-1]):
        out[index * size : (index + 1) * size, :] = ref[...]


def stack(blocks):
    size = blocks[0].shape[0]
    return call(stack_kernel, [((size * len(blocks), 128), low)], *blocks)[0]


def put_block(read, place, outs, parts):
    first = 0
    for out, (depth, columns, axis) in zip(outs, parts):
        for index in range(columns):
            piece = read(first, depth)
            first += depth
            if axis == 0:
                out[place * depth : (place + 1) * depth, index * 128 : (index + 1) * 128] = piece
            else:
                out[:, place * 128 : (place + 1) * 128] = piece


def join_kernel(*refs, sources, parts):
    outs = refs[-len(parts) :]
    for place, (ref, base) in enumerate(sources):
        put_block(lambda first, depth: refs[ref][base + first : base + first + depth, :], place, outs, parts)


def pair_kernel(order, here, there, *outs, parts):
    size = here.shape[0] // 4
    for place in range(8):
        base = (order[place] // 2) * size
        blocks = there if place // 4 else here
        put_block(
            lambda first, depth: blocks[pl.ds(pl.multiple_of(base + first, 128), depth), :], place, outs, parts
        )


def join_pair(here, there, order, parts):
    return call(functools.partial(pair_kernel, parts=parts), joined_shapes(8, parts), order, here, there, scalars=1)


def order_kernel(order, blocks, *outs, parts):
    size = blocks.shape[0] // order.shape[0]
    for place in range(order.shape[0]):
        base = order[place] * size
        put_block(
            lambda first, depth: blocks[pl.ds(pl.multiple_of(base + first, 128), depth), :], place, outs, parts
        )


def joined_shapes(count, parts):
    return [((depth, 128 * count) if axis else (depth * count, columns * 128), low) for depth, columns, axis in parts]


def join(arrays, sources, parts):
    return call(
        functools.partial(join_kernel, sources=sources, parts=parts), joined_shapes(len(sources), parts), *arrays
    )


def join_ordered(blocks, order, parts):
    return call(
        functools.partial(order_kernel, parts=parts), joined_shapes(order.shape[0], parts), order, blocks, scalars=1
    )


def unpack_kernel(order, to_rows, arrived, out, kept):
    kept[...] = matmul(to_rows[...], arrived[...]).astype(low)
    span = out.shape[1] // order.shape[0]
    for place in range(order.shape[0]):
        out[:, place * span : (place + 1) * span] = kept[:, pl.ds(pl.multiple_of(order[place] * span, span), span)]


def unpack(to_rows, arrived, order):
    if not paired(order.shape[0]):
        return matmul(to_rows, arrived).astype(low)
    shape = (to_rows.shape[0], arrived.shape[1])
    return call(
        unpack_kernel, [(shape, low)], order, to_rows, arrived, scratch=[pltpu.VMEM(shape, low)], scalars=1
    )[0]


def repack_kernel(order, to_rows, value, out, kept):
    rows, span = out.shape[0], out.shape[1] // order.shape[0]
    for place in range(order.shape[0]):
        at = pl.ds(pl.multiple_of(order[place] * span, span), span)
        kept[:, at] = value[:rows, place * span : (place + 1) * span].astype(low)
    out[...] = contract_rows(to_rows[...], kept[...]).astype(low)


def repack(to_rows, value, order):
    shape = (to_rows.shape[0], value.shape[1])
    if not paired(order.shape[0]):
        return matmul(to_rows.T, value[: shape[0]].astype(low)).astype(low)
    return call(
        repack_kernel, [(shape, low)], order, to_rows, value, scratch=[pltpu.VMEM(shape, low)], scalars=1
    )[0]


def collect_kernel(*refs, offsets):
    out = refs[-1]
    lines, width = out.shape[0], out.shape[1] // 6
    for part, (ref, first) in enumerate(zip(refs[:-1], offsets)):
        out[:, part * width : (part + 1) * width] = ref[:lines, first : first + width]


def collect(parts, width):
    return call(
        functools.partial(collect_kernel, offsets=[first for _, first in parts]),
        [((8, 6 * width), wide)],
        *[value for value, _ in parts],
    )[0]


def unspread_kernel(order, own, other, out):
    count, _, columns = out.shape
    blocks = columns // 128
    for part in range(6):
        for place in range(count):
            first = (part * count + place) * 128
            block = order[place] + part * count
            at = pl.ds(pl.multiple_of(lax.rem(block, blocks) * 128, 128), 128)
            out[block // blocks, :, at] = (own[:, first : first + 128] + other[:, first : first + 128]).astype(low)


def unspread(own, other, order, items, columns):
    count = order.shape[0]
    if paired(count):
        return call(unspread_kernel, [((count, own.shape[0], columns), low)], order, own, other, scalars=1)[0][:, :items]
    return jnp.swapaxes((own + other).astype(low)[:items].reshape(items, count, columns), 0, 1)


def spread_kernel(order, arrived, out):
    count, lines, columns = arrived.shape
    layers, parts, items, _ = out.shape
    blocks = columns // 128
    for part in range(parts):
        for place in range(count):
            block = order[place] + part * count
            source = block // blocks
            at = pl.ds(pl.multiple_of(lax.rem(block, blocks) * 128, 128), 128)
            rows = arrived[source, :, at].astype(wide)
            total = rows[: lines // 2] + rows[lines // 2 :]
            for layer in range(layers):
                out[layer, part, :, place * 128 : (place + 1) * 128] = total[layer * items : (layer + 1) * items]


def spread(arrived, order, layers, items, width):
    count, lines, columns = arrived.shape
    if paired(count):
        return call(spread_kernel, [((layers, 6, items, width), wide)], order, arrived, scalars=1)[0]
    halves = arrived.astype(wide).reshape(count, 2, layers, items, columns)
    whole = jnp.transpose(halves[:, 0] + halves[:, 1], (1, 2, 0, 3)).reshape(layers, items, 6, width)
    return jnp.swapaxes(whole, 1, 2)


def fold_kernel(slow, kept, arrived, out):
    span = out.shape[2]
    for back in range(4):
        columns = slice(back * span, (back + 1) * span)
        out[lax.rem(slow[0] + 4 - back, 4)] = (kept[:, columns] + arrived[:, columns].astype(wide)).astype(low)


def fold(kept, arrived, slow):
    height, half = kept.shape
    return call(fold_kernel, [((4, height, half // 4), low)], slow, kept, arrived, scalars=1)[0]


class Sums:
    def __init__(self, kept, sent):
        self.kept = kept
        self.arrived = swap(sent, "dp", 1)

    def fold(self, along, marker):
        if along:
            slow = (lax.axis_index("dp") // 2).astype(jnp.int32).reshape(1)
            blocks = fold(self.kept, tie(self.arrived, marker), slow)
            self.blocks = lax.psum_scatter(
                blocks, "dp", scatter_dimension=0, axis_index_groups=slow_groups, tiled=True
            )
            return
        self.blocks = None
        total = self.kept + tie(self.arrived, marker).astype(wide)
        span = total.shape[1] // 4
        self.parts = [total[:, i * span : (i + 1) * span] for i in range(4)]
        for back in (1, 2, 3):
            pairs = [(i, (i + 8 - 2 * back) % 8) for i in range(8)]
            self.parts[back] = lax.ppermute(self.parts[back].astype(low), "dp", pairs)

    def total(self, marker):
        if self.blocks is not None:
            return tie(self.blocks, marker).reshape(self.blocks.shape[1:]).astype(wide)
        parts = [tie(part, marker) for part in self.parts]
        return parts[0] + parts[1].astype(wide) + parts[2].astype(wide) + parts[3].astype(wide)


class WholeSums:
    def __init__(self, blocks):
        self.arrived = blocks
        self.result = lax.psum_scatter(blocks, "dp", scatter_dimension=0, tiled=True)

    def fold(self):
        pass

    def total(self, marker):
        return tie(self.result, marker).reshape(self.result.shape[1:]).astype(wide)


def gather_cores(part_own, part_other):
    return (part_own + swap(part_other, "shard", 1).astype(wide)).astype(low)


def route(dest, rows):
    table = dest[:, 0, :]
    groups = table.shape[0]
    capacity = rows // groups
    here = lax.axis_index("dp")
    own = lax.dynamic_index_in_dim(table, here, 0, keepdims=False)
    pack = own // rows
    index = jnp.arange(rows, dtype=jnp.int32)
    earlier = index[None, :] < index[:, None]
    rank = jnp.sum((earlier & (pack[None, :] == pack[:, None])).astype(jnp.int32), axis=1)
    slot = pack * capacity + rank
    to_slots = (slot[None, :] == index[:, None]).astype(low)
    mine = table // rows == here
    rank_in = jnp.sum((earlier[None] & mine[:, None, :]).astype(jnp.int32), axis=2)
    slot_in = jnp.arange(groups, dtype=jnp.int32)[:, None] * capacity + rank_in
    slot_in = jnp.where(mine, slot_in, rows).reshape(-1)
    row_in = (table % rows).reshape(-1)
    by_row = (row_in[None, :] == index[:, None]).astype(low)
    by_slot = (slot_in[None, :] == index[:, None]).astype(low)
    to_rows = contract_last(by_row, by_slot).astype(low)
    return to_slots, to_rows


def exchange(value, groups):
    return lax.all_to_all(value, "dp", split_axis=0, concat_axis=0, tiled=True)


def pack_layout(lengths, place):
    ends = jnp.cumsum(lengths)
    starts = ends - lengths
    member = jnp.sum((place[:, None] >= ends[None, :]).astype(jnp.int32), axis=1)
    onehot = member[:, None] == jnp.arange(lengths.shape[0], dtype=jnp.int32)[None, :]
    start = jnp.sum(jnp.where(onehot, starts[None, :], jnp.int32(0)), axis=1)
    bounds = jnp.array(level_ends, dtype=jnp.int32)
    level = jnp.sum(((place - start)[:, None] >= bounds[None, :]).astype(jnp.int32), axis=1)
    return member, level


grant = 24
small = pl.CostEstimate(flops=1000000000, bytes_accessed=1000000, transcendentals=0)
stripe = 64


def call(kernel, outs, *operands, scratch=(), scalars=0):
    spec = pl.BlockSpec(memory_space=pltpu.VMEM)
    return pl.pallas_call(
        kernel,
        out_shape=[jax.ShapeDtypeStruct(shape, kind) for shape, kind in outs],
        in_specs=[pl.BlockSpec(memory_space=pltpu.SMEM)] * scalars + [spec] * (len(operands) - scalars),
        out_specs=[spec] * len(outs),
        scratch_shapes=list(scratch),
        cost_estimate=small,
        compiler_params=pltpu.CompilerParams(vmem_limit_bytes=grant << 20),
    )(*operands)


def pick(member, table):
    items = table.shape[0]
    result = table[items - 1 : items, :]
    for item in range(items - 2, -1, -1):
        result = jnp.where(member == item, table[item : item + 1, :], result)
    return result


def normed(value):
    centered = value - jnp.mean(value, axis=-1, keepdims=True)
    inverse = lax.rsqrt(jnp.mean(centered * centered, axis=-1, keepdims=True) + epsilon)
    return centered * inverse, inverse


def stripes(rows, body):
    @pl.loop(0, rows // stripe)
    def _(index):
        first = pl.multiple_of(index * stripe, stripe)
        body(pl.ds(first, stripe), pl.ds(pl.multiple_of(lax.rem(first + rows // 2, rows), stripe), stripe))


def enter_kernel(value, mods, member, out, *, scale, shift):
    def body(at, _):
        who = member[at, :]
        unit, _inverse = normed(value[at, :])
        out[at, :] = (unit * (1.0 + pick(who, mods[scale])) + pick(who, mods[shift])).astype(low)

    stripes(value.shape[0], body)


def enter(value, mods, member, scale, shift):
    return call(
        functools.partial(enter_kernel, scale=scale, shift=shift), [(value.shape, low)], value, mods, member
    )[0]


def step_kernel(value, here, there, mods_gain, mods, member, out, low_out, *, gain, scale, shift):
    def body(at, across):
        who = member[at, :]
        branch = here[at, :].astype(wide) + there[across, :].astype(wide)
        total = value[at, :] + pick(who, mods_gain[gain]) * branch
        out[at, :] = total
        unit, _inverse = normed(total)
        low_out[at, :] = (unit * (1.0 + pick(who, mods[scale])) + pick(who, mods[shift])).astype(low)

    stripes(value.shape[0], body)


def step(value, here, there, mods_gain, mods, member, gain, scale, shift):
    return call(
        functools.partial(step_kernel, gain=gain, scale=scale, shift=shift),
        [(value.shape, wide), (value.shape, low)],
        value, here, there, mods_gain, mods, member,
    )


def leave_kernel(value, here, there, mods, member, out, *, gain):
    def body(at, across):
        branch = here[at, :].astype(wide) + there[across, :].astype(wide)
        out[at, :] = value[at, :] + pick(member[at, :], mods[gain]) * branch

    stripes(value.shape[0], body)


def leave(value, here, there, mods, member, gain):
    return call(
        functools.partial(leave_kernel, gain=gain), [(value.shape, wide)], value, here, there, mods, member
    )[0]


def mlp_kernel(own, other, fc1, fc2, part_own, part_other, hidden_out, act_out):
    half = own.shape[0]
    for place, source, target in ((0, own, part_own), (1, other, part_other)):
        @pl.loop(0, half // 128)
        def _(index):
            at = pl.ds(pl.multiple_of(index * 128, 128), 128)
            put = pl.ds(pl.multiple_of(place * half + index * 128, 128), 128)
            hidden = matmul(source[at, :], fc1[...])
            hidden_out[put, :] = hidden
            activated = (0.5 * hidden * (1.0 + jnp.tanh(root * (hidden + cubic * hidden * hidden * hidden)))).astype(low)
            act_out[put, :] = activated
            target[at, :] = matmul(activated, fc2[...]).astype(target.dtype)


def mlp(own, other, fc1, fc2):
    half, width = own.shape
    units = fc1.shape[1]
    return call(
        mlp_kernel,
        [((half, width), wide), ((half, width), low), ((2 * half, units), wide), ((2 * half, units), low)],
        own, other, fc1, fc2,
    )


def mlp_back_kernel(own, other, hidden_in, fc1, fc2, part_own, part_other, grad_out):
    half = own.shape[0]
    for place, source, target in ((0, own, part_own), (1, other, part_other)):
        @pl.loop(0, half // 128)
        def _(index):
            at = pl.ds(pl.multiple_of(index * 128, 128), 128)
            put = pl.ds(pl.multiple_of(place * half + index * 128, 128), 128)
            grad_activated = contract_last(source[at, :], fc2[...])
            hidden = hidden_in[put, :]
            square = hidden * hidden
            bent = jnp.tanh(root * (hidden + cubic * hidden * square))
            slope = 0.5 * (1.0 + bent) + 0.5 * hidden * (1.0 - bent * bent) * (root * (1.0 + 3.0 * cubic * square))
            grad_hidden = (grad_activated * slope).astype(low)
            grad_out[put, :] = grad_hidden
            target[at, :] = contract_last(grad_hidden, fc1[...]).astype(target.dtype)


def mlp_back(own, other, hidden, fc1, fc2):
    half, width = own.shape
    return call(
        mlp_back_kernel,
        [((half, width), wide), ((half, width), low), (hidden.shape, low)],
        own, other, hidden, fc1, fc2,
    )


def heads_of(shape, heads):
    lane = lax.broadcasted_iota(jnp.int32, shape, 1)
    span = shape[1] // heads
    return [(lane >= head * span) & (lane < (head + 1) * span) for head in range(heads)]


def head_sums(value, masks):
    return [jnp.sum(jnp.where(mask, value, 0.0), axis=1, keepdims=True) for mask in masks]


def by_head(columns, masks):
    result = columns[-1]
    for column, mask in zip(columns[-2::-1], masks[-2::-1]):
        result = jnp.where(mask, column, result)
    return result


def allowed_at(member, level, member_row, level_row, at):
    return (member[at, :] == member_row[...]) & (level_row[...] <= level[at, :])


def attend_kernel(
    own, other, qkv, proj, scale, member, level, member_row, level_row,
    part_own, part_other, raw_out, heads_out, inverse_out, queries, keys, values, *, heads,
):
    half = own.shape[0]
    span = qkv.shape[1] // 3
    block = 128
    for place, source in ((0, own), (1, other)):
        @pl.loop(0, half // block)
        def _(index):
            at = pl.ds(pl.multiple_of(index * block, block), block)
            put = pl.ds(pl.multiple_of(place * half + index * block, block), block)
            projected = matmul(source[at, :], qkv[...])
            raw_out[put, :] = projected
            masks = heads_of((block, span), heads)
            query, key = projected[:, :span], projected[:, span : 2 * span]
            query_sums, key_sums = head_sums(query * query, masks), head_sums(key * key, masks)
            query_scale = by_head(
                [lax.rsqrt(total + epsilon) * jnp.exp(scale[:, head : head + 1]) for head, total in enumerate(query_sums)], masks
            )
            key_scale = by_head([lax.rsqrt(total + epsilon) for total in key_sums], masks)
            queries[put, :] = (query * query_scale).astype(low)
            keys[put, :] = (key * key_scale).astype(low)
            values[put, :] = projected[:, 2 * span :].astype(low)

    rows = 2 * half
    for place, target in ((0, part_own), (1, part_other)):
        @pl.loop(0, half // block)
        def _(index):
            at = pl.ds(pl.multiple_of(index * block, block), block)
            put = pl.ds(pl.multiple_of(place * half + index * block, block), block)
            allowed = allowed_at(member, level, member_row, level_row, put)
            query = queries[put, :]
            masks = heads_of((block, span), heads)
            wide_masks = heads_of((rows, span), heads)
            outputs = jnp.zeros((block, span), wide)
            inverses = []
            for head in range(heads):
                scores = contract_last(jnp.where(masks[head], query, jnp.zeros_like(query)), keys[...])
                raised = jnp.where(allowed, jnp.exp(scores - jnp.exp(scale[:, head : head + 1])), 0.0)
                inverse = 1.0 / jnp.sum(raised, axis=1, keepdims=True)
                inverses.append(inverse)
                weights = (raised * inverse).astype(low)
                outputs = outputs + matmul(weights, jnp.where(wide_masks[head], values[...], jnp.zeros((), low)))
            inverse_out[put, :] = jnp.concatenate(inverses, axis=1)
            outputs = outputs.astype(low)
            heads_out[put, :] = outputs
            target[at, :] = matmul(outputs, proj[...]).astype(target.dtype)


def attend(own, other, qkv, proj, scale, layout, heads):
    half, width = own.shape
    rows, span = 2 * half, qkv.shape[1] // 3
    return call(
        functools.partial(attend_kernel, heads=heads),
        [
            ((half, width), wide),
            ((half, width), low),
            ((rows, 3 * span), wide),
            ((rows, span), low),
            ((rows, heads), wide),
        ],
        own, other, qkv, proj, scale, *layout,
        scratch=[pltpu.VMEM((rows, span), low)] * 3,
    )


def attend_back_kernel(
    own, other, raw, inverse_in, qkv, proj, scale, member, level, member_row, level_row,
    part_own, part_other, grad_out, log_out,
    queries, keys, values, grads, grad_queries, key_sums_t, value_sums_t, *, heads,
):
    half = own.shape[0]
    rows = 2 * half
    span = qkv.shape[1] // 3
    block = 128
    for place, source in ((0, own), (1, other)):
        @pl.loop(0, half // block)
        def _(index):
            at = pl.ds(pl.multiple_of(index * block, block), block)
            put = pl.ds(pl.multiple_of(place * half + index * block, block), block)
            grads[put, :] = contract_last(source[at, :], proj[...]).astype(low)
            masks = heads_of((block, span), heads)
            query, key = raw[put, :span], raw[put, span : 2 * span]
            query_sums, key_sums = head_sums(query * query, masks), head_sums(key * key, masks)
            query_scale = by_head(
                [lax.rsqrt(total + epsilon) * jnp.exp(scale[:, head : head + 1]) for head, total in enumerate(query_sums)], masks
            )
            key_scale = by_head([lax.rsqrt(total + epsilon) for total in key_sums], masks)
            queries[put, :] = (query * query_scale).astype(low)
            keys[put, :] = (key * key_scale).astype(low)
            values[put, :] = raw[put, 2 * span :].astype(low)

    key_sums_t[...] = jnp.zeros_like(key_sums_t)
    value_sums_t[...] = jnp.zeros_like(value_sums_t)
    deep = span // heads
    step_rows = 256

    @pl.loop(0, rows // step_rows)
    def _(index):
        put = pl.ds(pl.multiple_of(index * step_rows, step_rows), step_rows)
        allowed = allowed_at(member, level, member_row, level_row, put)
        query, grad = queries[put, :], grads[put, :]
        query_t, grad_t = query.astype(wide).T.astype(low), grad.astype(wide).T.astype(low)
        masks = heads_of((step_rows, span), heads)
        wide_masks = heads_of((rows, span), heads)
        outputs = jnp.zeros((step_rows, span), wide)
        for head in range(heads):
            scores = contract_last(jnp.where(masks[head], query, jnp.zeros_like(query)), keys[...])
            raised = jnp.where(allowed, jnp.exp(scores - jnp.exp(scale[:, head : head + 1])), 0.0)
            weights = raised * inverse_in[put, head : head + 1]
            grad_weights = contract_last(jnp.where(masks[head], grad, jnp.zeros_like(grad)), values[...])
            inner = jnp.sum(weights * grad_weights, axis=1, keepdims=True)
            grad_scores = (weights * (grad_weights - inner)).astype(low)
            outputs = outputs + matmul(grad_scores, jnp.where(wide_masks[head], keys[...], jnp.zeros((), low)))
            these = slice(head * deep, (head + 1) * deep)
            key_sums_t[these, :] += matmul(query_t[these, :], grad_scores)
            value_sums_t[these, :] += matmul(grad_t[these, :], weights.astype(low))
        grad_queries[put, :] = outputs

    log_out[...] = jnp.zeros_like(log_out)
    raw_keys = key_sums_t[...].T
    raw_values = value_sums_t[...].T
    grad_out[:, 2 * span :] = raw_values.astype(low)
    key_sums = raw_keys
    for place, target in ((0, part_own), (1, part_other)):
        for index in range(half // block):
            put = slice(place * half + index * block, place * half + (index + 1) * block)
            at = slice(index * block, (index + 1) * block)
            masks = heads_of((block, span), heads)
            query, key = raw[put, :span], raw[put, span : 2 * span]
            grad_query, grad_key = grad_queries[put, :], key_sums[put, :]
            inverse_q = [lax.rsqrt(total + epsilon) for total in head_sums(query * query, masks)]
            inverse_k = [lax.rsqrt(total + epsilon) for total in head_sums(key * key, masks)]
            dots_q, dots_k = head_sums(query * grad_query, masks), head_sums(key * grad_key, masks)
            rises = [jnp.exp(scale[:, head : head + 1]) for head in range(heads)]
            logs = [a * d * i for a, d, i in zip(rises, dots_q, inverse_q)]
            log_out[...] += jnp.concatenate([jnp.sum(x, axis=0, keepdims=True) for x in logs], axis=1)
            first = by_head([a * i for a, i in zip(rises, inverse_q)], masks)
            second = by_head([a * d * i * i * i for a, d, i in zip(rises, dots_q, inverse_q)], masks)
            grad_out[put, :span] = (grad_query * first - query * second).astype(low)
            first = by_head(inverse_k, masks)
            second = by_head([d * i * i * i for d, i in zip(dots_k, inverse_k)], masks)
            grad_out[put, span : 2 * span] = (grad_key * first - key * second).astype(low)
            target[at, :] = contract_last(grad_out[put, :], qkv[...]).astype(target.dtype)


def attend_back(own, other, raw, inverse, qkv, proj, scale, layout, heads):
    half, width = own.shape
    rows, span = 2 * half, qkv.shape[1] // 3
    return call(
        functools.partial(attend_back_kernel, heads=heads),
        [((half, width), wide), ((half, width), low), ((rows, 3 * span), low), ((1, heads), wide)],
        own, other, raw, inverse, qkv, proj, scale, *layout,
        scratch=[pltpu.VMEM((rows, span), low)] * 4
        + [pltpu.VMEM((rows, span), wide), pltpu.VMEM((span, rows), wide), pltpu.VMEM((span, rows), wide)],
    )


def step_back_kernel(
    value, here, there, grad, mods, mods_gain, branch_here, branch_there, member, choose,
    grad_out, low_out, sums_out, terms, *, scale, gain,
):
    width = value.shape[1]

    def body(at, across):
        who = member[at, :]
        unit, inverse = normed(value[at, :])
        arrived = here[at, :].astype(wide) + there[across, :].astype(wide)
        scaled = arrived * (1.0 + pick(who, mods[scale]))
        total = grad[at, :] + inverse * (
            scaled
            - jnp.mean(scaled, axis=-1, keepdims=True)
            - unit * jnp.mean(scaled * unit, axis=-1, keepdims=True)
        )
        grad_out[at, :] = total
        terms[at, : width] = (arrived * unit).astype(low)
        terms[at, width : 2 * width] = arrived.astype(low)
        if gain is not None:
            branch = branch_here[at, :].astype(wide) + branch_there[across, :].astype(wide)
            terms[at, 2 * width :] = (total * branch).astype(low)
            low_out[at, :] = (total * pick(who, mods_gain[gain])).astype(low)

    stripes(value.shape[0], body)
    sums_out[...] = matmul(choose[...], terms[...])


def last_back_kernel(value, here, there, grad, mods, member, choose, grad_out, sums_out, terms, *, scale):
    step_back_kernel(
        value, here, there, grad, mods, None, None, None, member, choose,
        grad_out, None, sums_out, terms, scale=scale, gain=None,
    )


def step_back(value, here, there, grad, mods, member, choose, scale, before=None):
    rows, width = value.shape
    lines = choose.shape[0]
    if before is None:
        return call(
            functools.partial(last_back_kernel, scale=scale),
            [((rows, width), wide), ((lines, 2 * width), wide)],
            value, here, there, grad, mods, member, choose,
            scratch=[pltpu.VMEM((rows, 2 * width), low)],
        )
    mods_gain, gain, branch_here, branch_there = before
    return call(
        functools.partial(step_back_kernel, scale=scale, gain=gain),
        [((rows, width), wide), ((rows, width), low), ((lines, 3 * width), wide)],
        value, here, there, grad, mods, mods_gain, branch_here, branch_there, member, choose,
        scratch=[pltpu.VMEM((rows, 3 * width), low)],
    )


def first_back_kernel(grad, here, there, mods, member, choose, low_out, sums_out, terms, *, gain):
    def body(at, across):
        branch = here[at, :].astype(wide) + there[across, :].astype(wide)
        terms[at, :] = (grad[at, :] * branch).astype(low)
        low_out[at, :] = (grad[at, :] * pick(member[at, :], mods[gain])).astype(low)

    stripes(grad.shape[0], body)
    sums_out[...] = matmul(choose[...], terms[...])


def first_back(grad, here, there, mods, member, choose, gain):
    rows, width = grad.shape
    return call(
        functools.partial(first_back_kernel, gain=gain),
        [((rows, width), low), ((choose.shape[0], width), wide)],
        grad, here, there, mods, member, choose,
        scratch=[pltpu.VMEM((rows, width), low)],
    )


def gradient_kernel(*refs):
    kept, sent = refs[-2:]
    rest = refs[:-2]
    half = kept.shape[1]
    block = 256
    first = 0
    for factor, own, other in [rest[i : i + 3] for i in range(0, len(rest), 3)]:
        rows = own.shape[0]
        base = first

        @pl.loop(0, factor.shape[1] // block)
        def _(index):
            at = pl.ds(pl.multiple_of(index * block, block), block)
            put = pl.ds(pl.multiple_of(base + index * block, block), block)
            turned = factor[:, at].T
            kept[put, :] = matmul(turned[:, :rows], own[:, :half]) + matmul(turned[:, rows:], other[:, :half])
            sent[put, :] = (
                matmul(turned[:, :rows], own[:, half:]) + matmul(turned[:, rows:], other[:, half:])
            ).astype(low)

        first += factor.shape[1]


def silu_of(value):
    return value / (1.0 + jnp.exp(-value))


def condition_kernel(classes, table, ada, cond_out, part_out):
    count = table.shape[0]
    hits = (classes[...] == lax.broadcasted_iota(jnp.int32, (classes.shape[0], count), 1)).astype(low)
    cond = matmul(hits, table[...])
    cond_out[...] = cond
    cond_low = silu_of(cond).astype(low)
    for layer in range(ada.shape[0]):
        part_out[layer] = matmul(cond_low, ada[layer])


def condition(classes, table, ada):
    count, width = classes.shape[0], table.shape[1]
    layers, _, columns = ada.shape
    return call(
        condition_kernel, [((count, width), wide), ((layers, count, columns), wide)], classes, table, ada
    )


def condition_back_kernel(*refs):
    cond, ada = refs[:2]
    grads, (ada_out, silu_out) = refs[2:-2], refs[-2:]
    cond_low = silu_of(cond[...]).astype(low)
    total = jnp.zeros(cond.shape, wide)
    for layer, grad in enumerate(grads):
        ada_out[layer] = contract_rows(cond_low, grad[...])
        total = total + contract_last(grad[...], ada[layer])
    silu_out[...] = total


def condition_back(cond, ada, grads):
    return call(condition_back_kernel, [(ada.shape, wide), (cond.shape, wide)], cond, ada, *grads)


def table_kernel(classes, cond, grad, out):
    value = cond[...]
    gate = 1.0 / (1.0 + jnp.exp(-value))
    slope = gate * (1.0 + value * (1.0 - gate))
    count = out.shape[0]
    hits = (classes[...] == lax.broadcasted_iota(jnp.int32, (count, classes.shape[1]), 0)).astype(wide)
    out[...] = jnp.dot(hits, grad[...] * slope, precision=lax.Precision.HIGHEST, preferred_element_type=wide)


def table_back(classes, cond, grad, count):
    return call(table_kernel, [((count, cond.shape[1]), wide)], classes, cond, grad)[0]


def gradient_blocks_kernel(order, *refs):
    out = refs[-1]
    rest = refs[:-1]
    count, _, span = out.shape
    block = 256
    first = 0
    for factor, own, other in [rest[i : i + 3] for i in range(0, len(rest), 3)]:
        rows = own.shape[0]
        base = first

        @pl.loop(0, factor.shape[1] // block)
        def _(index):
            at = pl.ds(pl.multiple_of(index * block, block), block)
            put = pl.ds(pl.multiple_of(base + index * block, block), block)
            turned = factor[:, at].T
            half = own.shape[1] // 2
            for side in range(2):
                columns = slice(side * half, (side + 1) * half)
                product = (matmul(turned[:, :rows], own[:, columns]) + matmul(turned[:, rows:], other[:, columns])).astype(low)
                for index_in in range(count // 2):
                    place = side * (count // 2) + index_in
                    out[order[place], put, :] = product[:, index_in * span : (index_in + 1) * span]

        first += factor.shape[1]


def gradient_blocks(order, *pairs):
    height = sum(left.shape[1] for left, _ in pairs)
    width = pairs[0][1][0].shape[1]
    count = order.shape[0]
    operands = [value for left, sides in pairs for value in (left, *sides)]
    if not paired(count):
        whole = [contract_rows(left, jnp.concatenate(sides, axis=0)) for left, sides in pairs]
        whole = jnp.concatenate(whole, axis=0).reshape(height, count, width // count)
        return jnp.swapaxes(whole, 0, 1).astype(low)
    return call(gradient_blocks_kernel, [((count, height, width // count), low)], order, *operands, scalars=1)[0]


def gradients(*pairs):
    height = sum(left.shape[1] for left, _ in pairs)
    half = pairs[0][1][0].shape[1] // 2
    operands = [value for left, sides in pairs for value in (left, *sides)]
    return call(gradient_kernel, [((height, half), wide), ((height, half), low)], *operands)


def on_device(
    tokens,
    out_grad,
    dest,
    lengths,
    classes,
    class_table,
    w_ada,
    w_qkv,
    head_scale,
    w_proj,
    w_fc1,
    w_fc2,
):
    rows, width = tokens.shape
    groups, shards = lax.axis_size("dp"), lax.axis_size("shard")
    layers = w_ada.shape[0]
    pack = rows * shards
    heads_here = head_scale.shape[1]
    items = lengths.shape[1]
    slots = rows // groups
    columns = w_ada.shape[2]
    me = lax.axis_index("shard")

    near = paired(groups)
    depth, span = w_qkv.shape[1], w_qkv.shape[3]
    flat = [w_qkv[layer].reshape(depth, -1) for layer in range(layers)]
    order = own_order(groups)
    def along(block):
        return lax.all_gather(block, "dp", axis=0, tiled=True, axis_index_groups=slow_groups)

    if near:
        mix_a = along(pack_mix(flat[0], w_proj, 0))

    if near:
        known = classes
        for offset in (1, 2, 4):
            known = jnp.concatenate([known, swap(known, "dp", offset)], axis=0)
        index = jnp.arange(groups, dtype=jnp.int32)
        found = (index[:, None] ^ index[None, :]) == lax.axis_index("dp")
        known = jnp.sum(jnp.where(found[:, :, None], known[None], 0), axis=1)
    else:
        known = lax.all_gather(classes, "dp", axis=0, tiled=True)
    all_classes = known.reshape(-1)

    def whole(own, hops, there, other, first, parts):
        size = own.shape[0]
        sources = [(0, 0), (1, 0), (2, 0), (3, 0), (4, first)] + [(5, i * size) for i in range(3)]
        return join([own, *hops, other, there], sources, parts)

    mix_parts = [(depth, 3 * span // 128, 0), (w_proj.shape[1], 1, 1)]
    fc1_parts = [(depth, w_fc1.shape[2] // 128, 0)]
    fc2_parts = [(w_fc2.shape[1], 1, 1)]
    if near:
        fc1_a = tie(pack_fc1(w_fc1, 0), all_classes)
        fc2_b = tie(w_fc2[0], all_classes)
        hops_a = straight(fc1_a)
        other_ab = swap(stack([fc1_a, fc2_b]), "dp", 1)
        mix_c, fc1_d, fc2_e = (
            along(tie(block, all_classes)) for block in (pack_mix(flat[1], w_proj, 1), pack_fc1(w_fc1, 1), w_fc2[1])
        )

    to_slots, to_rows = route(dest, rows)
    arrived = exchange(matmul(to_slots, tokens).astype(low).reshape(groups, slots, width), groups)
    packed = unpack(to_rows, arrived.reshape(rows, width), order)
    carried = jnp.concatenate([packed, swap(packed, "shard", 2)], axis=0).astype(wide)

    cond, part = condition(all_classes[:, None], class_table, w_ada)
    part = part + swap(part, "shard", 1)
    part = part + swap(part, "shard", 2)
    part = jnp.swapaxes(part.reshape(layers, groups, items, columns), 0, 1)
    upper = lax.reduce_precision(part, 8, 7)
    halves = jnp.stack([upper.astype(low), (part - upper).astype(low)], axis=1)
    halves = exchange(tie(halves.reshape(groups, 2 * layers * items, columns), packed), groups)
    modulation = spread(halves, order, layers, items, width)
    if near:
        modulation = tie(modulation, *hops_a, other_ab)
        there_m = swap(mix_a, "dp", 1)
        there_a = swap(stack(hops_a), "dp", 1)
        hops_b = straight(tie(fc2_b, modulation))

    def arrive(marker):
        grads_out = matmul(to_slots, tie(out_grad, marker)).astype(low).reshape(groups, slots, width)
        grads_out = exchange(grads_out, groups)
        grad_packed = unpack(to_rows, grads_out.reshape(rows, width), order)
        return jnp.concatenate([grad_packed, swap(grad_packed, "shard", 2)], axis=0).astype(wide)

    place = jnp.concatenate(
        [(me ^ offset) * rows + jnp.arange(rows, dtype=jnp.int32) for offset in (0, 2, 1, 3)]
    )
    member, level = pack_layout(lengths[0], place)
    layout = (member[:, None], level[:, None], member[None, :], level[None, :])
    here_member = member[: 2 * rows, None]
    choose = (jnp.arange(16, dtype=jnp.int32)[:, None] == member[None, : 2 * rows]).astype(low)
    scales = [head_scale[layer][None, :] for layer in range(layers)]
    mods = [modulation[layer] for layer in range(layers)]

    weights = [None] * layers
    saved = []
    first_low = enter(carried, mods[0], here_member, 2, 4)
    for layer in range(layers):
        if not near:
            qkv_full = lax.all_gather(flat[layer], "dp", axis=0, tiled=True)
            proj_full = lax.all_gather(w_proj[layer], "dp", axis=1, tiled=True)
            fc1_full = lax.all_gather(w_fc1[layer], "dp", axis=0, tiled=True)
            fc2_full = lax.all_gather(w_fc2[layer], "dp", axis=1, tiled=True)
        elif layer == 0:
            qkv_full, proj_full = join_pair(mix_a, there_m, order, mix_parts)
        else:
            qkv_full, proj_full = join_pair(mix_c, there_c, order, mix_parts)
        first = (first_low, swap(first_low, "shard", 1))
        if near and layer == 0:
            first = (first[0], tie(first[1], *hops_b))
            there_b = swap(stack(hops_b), "dp", 1)
        part_own, part_other, raw, heads_low, inverse = attend(
            *first, qkv_full, proj_full, scales[layer], layout, heads_here
        )
        here = gather_cores(part_own, part_other)
        if layer == 0:
            grad_carried = arrive(here)
        if near:
            here = tie(here, there_a if layer == 0 else there_d)
        there = swap(here, "shard", 2)
        if near and layer == 1:
            there_e = swap(tie(fc2_e, here), "dp", 1)
        attended = (here, there)
        middle, second_low = step(carried, *attended, mods[layer], mods[layer], here_member, 0, 3, 5)
        second = (second_low, swap(second_low, "shard", 1))
        if near and layer == 0:
            (fc1_full,) = whole(fc1_a, hops_a, there_a, other_ab, 0, fc1_parts)
            (fc2_full,) = whole(fc2_b, hops_b, there_b, other_ab, fc1_a.shape[0], fc2_parts)
        elif near:
            (fc1_full,) = join_pair(fc1_d, there_d, order, fc1_parts)
            (fc2_full,) = join_pair(fc2_e, there_e, order, fc2_parts)
        weights[layer] = (qkv_full, proj_full, fc1_full, fc2_full)
        part_own, part_other, hidden, activated = mlp(*second, fc1_full, fc2_full)
        here = gather_cores(part_own, part_other)
        there = swap(here, "shard", 2)
        if near and layer == 0:
            there_c = swap(tie(mix_c, here), "dp", 1)
        if layer == 0:
            there, grad_carried = lax.optimization_barrier((there, grad_carried))
        if near and layer == 0:
            there_d = swap(tie(fc1_d, there), "dp", 1)
        branch = (here, there)
        saved.append((carried, middle, first, raw, heads_low, inverse, attended, second, hidden, activated, branch))
        if layer + 1 < layers:
            carried, first_low = step(middle, *branch, mods[layer], mods[layer + 1], here_member, 1, 2, 4)
        else:
            carried = leave(middle, *branch, mods[layer], here_member, 1)

    mixed_out = repack(to_rows, carried, order).reshape(groups, slots, width)

    def give(layer):
        sums = collect(mod_sums[layer], width)
        return unspread(sums, swap(sums, "shard", 1), order, items, columns)

    layer_sums = [None] * layers
    scale_grads = [None] * layers
    mod_sums = [[None] * 6 for _ in range(layers)]
    grad_low, sums = first_back(grad_carried, *saved[-1][-1], mods[-1], here_member, choose, 1)
    mod_sums[-1][1] = (sums, 0)
    for layer in range(layers - 1, -1, -1):
        qkv_full, proj_full, fc1_full, fc2_full = weights[layer]
        carried_in, middle, first, raw, heads_low, inverse, attended, second, hidden, activated, branch = saved[layer]
        grad_branch = (grad_low, swap(grad_low, "shard", 1))
        if near:
            terms = gradients((activated, grad_branch))
            sums_fc2 = Sums(*terms)
            hidden = tie(hidden, *terms)
        part_own, part_other, grad_hidden = mlp_back(*grad_branch, hidden, fc1_full, fc2_full)
        here = gather_cores(part_own, part_other)
        there = swap(here, "shard", 2)
        if near:
            terms = gradients((tie(grad_hidden, here), second))
            there = tie(there, *terms, *([mixed_out] if layer else []))
            sums_fc1 = Sums(*terms)
            before = sums_fc2 if layer else layer_sums[1][0]
            there = tie(there, before.arrived)
            before.fold(True, there)
        else:
            sums_fc2 = WholeSums(gradient_blocks(order, (activated, grad_branch)))
            sums_fc1 = WholeSums(gradient_blocks(order, (grad_hidden, second)))
        grad_middle, grad_low, sums = step_back(
            middle, here, there, grad_carried, mods[layer], here_member, choose, 3, (mods[layer], 0, *attended)
        )
        mod_sums[layer][3], mod_sums[layer][5], mod_sums[layer][0] = ((sums, i * width) for i in range(3))
        grad_attended = (grad_low, swap(grad_low, "shard", 1))
        part_own, part_other, grad_projected, scale_grads[layer] = attend_back(
            *grad_attended, raw, inverse, qkv_full, proj_full, scales[layer], layout, heads_here
        )
        here = gather_cores(part_own, part_other)
        there = swap(here, "shard", 2)
        if near:
            terms = gradients((tie(heads_low, here), grad_attended), (grad_projected, first))
            there = tie(there, *terms)
            sums_attn = Sums(*terms)
            before = sums_fc1 if layer else sums_fc2
            there = tie(there, before.arrived)
            before.fold(True, there)
        else:
            blocks_attn = gradient_blocks(order, (heads_low, grad_attended), (grad_projected, first))
            sums_attn = WholeSums(blocks_attn)
        if layer > 0:
            grad_carried, grad_low, sums = step_back(
                carried_in, here, there, grad_middle, mods[layer], here_member, choose, 2, (mods[layer - 1], 1, *saved[layer - 1][-1])
            )
            mod_sums[layer - 1][1] = (sums, 2 * width)
        else:
            grad_carried, sums = step_back(carried_in, here, there, grad_middle, mods[layer], here_member, choose, 2)
        mod_sums[layer][2], mod_sums[layer][4] = (sums, 0), (sums, width)
        layer_sums[layer] = (sums_attn, sums_fc1, sums_fc2)
    if near:
        layer_sums[0][1].fold(True, grad_carried)
        layer_sums[0][0].fold(False, grad_carried)

    grads_back = repack(to_rows, grad_carried, order).reshape(groups, slots, width)
    sent = jnp.stack([give(layer) for layer in range(layers)], axis=1).reshape(groups, layers * items * columns)
    if sent.shape[1] % width:
        back = exchange(jnp.concatenate([mixed_out, grads_back], axis=1), groups)
        mods_back = exchange(sent, groups)
    else:
        sent = sent.reshape(groups, -1, width)
        back = exchange(jnp.concatenate([mixed_out, grads_back, sent], axis=1), groups)
        mods_back = back[:, 2 * slots :]
    mixed_back, grads_back = back[:, :slots], back[:, slots : 2 * slots]
    mods_back = mods_back.reshape(groups, layers, items, columns)
    mods_back = [mods_back[:, layer] for layer in range(layers)]

    mixed = contract_rows(to_slots, mixed_back.reshape(rows, width)).astype(low)
    tokens_grad = contract_rows(to_slots, grads_back.reshape(rows, width)).astype(low)
    ada_grad, grad_silu = condition_back(
        cond, w_ada, [back.reshape(groups * items, columns) for back in mods_back]
    )
    logs = jnp.pad(jnp.stack(scale_grads).reshape(1, -1), ((0, 7), (0, cond.shape[1] - layers * heads_here)))
    summed = jnp.concatenate([grad_silu, logs], axis=0)
    if paired(groups):
        for offset in (1, 2, 4):
            summed = summed + swap(summed, "dp", offset)
    else:
        summed = lax.psum(summed, "dp")
    grad_silu = summed[: cond.shape[0]]
    scale_grad = summed[cond.shape[0], : layers * heads_here].reshape(layers, heads_here)
    table_grad = table_back(all_classes[None, :], cond, grad_silu, class_table.shape[0])
    spanned = w_proj.shape[1]
    layer_grads = []
    for layer in range(layers):
        attn, fc1, fc2 = (sums.total(grad_carried) for sums in layer_sums[layer])
        layer_grads.append((attn[spanned:].T.reshape(w_qkv.shape[1:]), attn[:spanned], fc1.T, fc2))
    qkv_grad, proj_grad, fc1_grad, fc2_grad = (
        jnp.stack([layer_grads[layer][i] for layer in range(layers)]) for i in range(4)
    )
    return (
        mixed,
        tokens_grad,
        table_grad,
        ada_grad,
        qkv_grad,
        scale_grad,
        proj_grad,
        fc1_grad,
        fc2_grad,
    )


def solution(mesh):
    placed = (
        P(("dp", "shard"), None),
        P(("dp", "shard"), None),
        P(None, "shard", None),
        P("dp", None),
        P("dp", None),
        P(None, "shard"),
        P(None, "shard", "dp"),
        P(None, "dp", None, "shard"),
        P(None, "shard"),
        P(None, "shard", "dp"),
        P(None, "dp", "shard"),
        P(None, "shard", "dp"),
    )
    return jax.shard_map(
        on_device,
        mesh=mesh,
        in_specs=placed,
        out_specs=(
            P(("dp", "shard"), None),
            P(("dp", "shard"), None),
            P(None, "shard"),
            P(None, "shard", "dp"),
            P(None, "dp", None, "shard"),
            P(None, "shard"),
            P(None, "shard", "dp"),
            P(None, "dp", "shard"),
            P(None, "shard", "dp"),
        ),
        check_vma=False,
    )
```

time: 659 us -> 568 us (0.86)
  Pallas kernels: 0 us -> 138 us
  matrix products: 79.2 us -> 4.08 us
  starting transfers between devices: 144 us -> 82.6 us
  waiting for transfers between devices: 279 us -> 235 us
  other arithmetic: 47.7 us -> 19 us
  local copies, waits for them, and re-layouts: 81.7 us -> 67.2 us
    pallas_call x0 -> x54, Pallas kernels: none -> 138 us  [call(): pl.pallas_call(kernel, out_shape=[jax.ShapeDtypeStruct(shape, kind) for s...]
    ppermute x121 -> x49, waiting for transfers between devices: 279 us -> 187 us  [swap(): return lax.ppermute(value, axis, [(i, i ^ offset) for i in range(size)])]
    ppermute x121 -> x49, starting transfers between devices: 129 us -> 41 us  [swap(): return lax.ppermute(value, axis, [(i, i ^ offset) for i in range(size)])]
    ppermute x0 -> x9, waiting for transfers between devices: none -> 38.5 us  [the longest x6 38.5 us: straight(): lax.ppermute(block, 'dp', [(i, (i + 2 * back) % 8) for i in range(8)])]
    dot_general x25 -> x0, matrix products: 26.5 us -> none  [the longest x12 12.4 us: item_sums(): lax.dot_general(choose, value, (((0,), (0,)), ((), ())), precision=lax.Pr...]
    dot_general x18 -> x2, matrix products: 22.3 us -> 1.95 us  [contract_rows(): lax.dot_general(left, right, (((0,), (0,)), ((), ())), preferred_element_...]
    dot_general x19 -> x2, matrix products: 16.1 us -> 1.85 us  [matmul(): return jnp.dot(left, right, preferred_element_type=wide)]
    dot_general x11 -> x1, matrix products: 14.2 us -> 0.28 us  [contract_last(): lax.dot_general(left, right, (((1,), (1,)), ((), ())), preferred_element_...]
  transfers between devices with their start and end apart: 124 -> 71, of which waited for: 52 -> 39; matrix products, arithmetic and copies ran while one was open for 26% -> 6% of each run, Pallas kernels for 0% -> 22%
where the time goes in v2:
time: 568 us; the launch traced here: 563 us
  waiting for transfers between devices  235 us (41%)
  Pallas kernels  138 us (24%)
  starting transfers between devices  82.6 us (15%)
  local copies, waits for them, and re-layouts  67.2 us (12%)
  other arithmetic  19 us (3%)
  between operations  16.1 us (3%)
    ppermute x49, waiting for transfers between devices, swap(): return lax.ppermute(value, axis, [(i, i ^ offset) for i in range(size)])  187 us
    pallas_call x54, Pallas kernels, call(): pl.pallas_call(kernel, out_shape=[jax.ShapeDtypeStruct(shape, kind) for s...  138 us
    unnamed x334, local copies, waits for them, and re-layouts  52.8 us
    ppermute x49, starting transfers between devices, swap(): return lax.ppermute(value, axis, [(i, i ^ offset) for i in range(size)])  41 us
    ppermute x6, waiting for transfers between devices, straight(): lax.ppermute(block, 'dp', [(i, (i + 2 * back) % 8) for i in range(8)])  38.5 us
    all_to_all x4, starting transfers between devices, exchange(): return lax.all_to_all(value, 'dp', split_axis=0, concat_axis=0, tiled=True)  19.1 us
    all_gather x4, starting transfers between devices, along(): lax.all_gather(block, 'dp', axis=0, tiled=True, axis_index_groups=slow_gr...  11.5 us
  transfers between devices with their start and end apart: 71, of which 39 were waited for; matrix products, arithmetic and copies ran while one was open for 6% of the time, Pallas kernels for 22%

profile of v2, /device:TPU:0, one launch (start us, length us, event | category | flops | bytes accessed | tf_op | source)
XLA Modules:
  0.0 562.5 jit_solution(11590906858912093539)
XLA Ops:
  7.2 3.0 collective-permute-start.1
  12.7 4.9 all-to-all-start
  26.0 2.8 collective-permute-start.3
  44.1 5.9 %all-to-all-start.1 = ((bf16[8,16,768]{2,1,0:T(8,128)(2,1)}), bf16[8,16,768]{2,1,0:T(8,128)(2,1)S(1)}, u32[]{:S(2)}, u32[]{:S(2)}) async-start(bf16[8,16,768]{2,1,0:T(8,128)(2,1)} %reshape.286), calls=%async_computation.1 | async-start | bytes 393216 | tf_op jit(solution)/shard_map/all_to_all | solution.py:326
  50.1 3.8 collective-permute-start.8
  60.7 18.6 %collective-permute-done.7.refs_1_.refs_2_ = bf16[1024,128]{1,0:T(8,128)(2,1)S(1)} collective-permute-done((bf16[1024,128]{1,0:T(8,128)(2,1)S(1)}, bf16[1024,128]{1,0:T(8,128)(2,1)S(1)}, u32[]{:S(2)}, u32[]{:S(2)}) %collective-permute-start.7) | collective-permute-done | bytes 262176 | tf_op jit(solution)/shard_map/ppermute | solution.py:55
  87.5 6.7 %collective-permute-done.13.refs_2_.refs_3_ = bf16[1024,128]{1,0:T(8,128)(2,1)S(1)} collective-permute-done((bf16[1024,128]{1,0:T(8,128)(2,1)S(1)}, bf16[1024,128]{1,0:T(8,128)(2,1)S(1)}, u32[]{:S(2)}, u32[]{:S(2)}) %collective-permute-start.13) | collective-permute-done | bytes 262176 | tf_op jit(solution)/shard_map/ppermute | solution.py:55
  95.6 12.7 %collective-permute-done.12.refs_1_.refs_2_ = bf16[1024,128]{1,0:T(8,128)(2,1)S(1)} collective-permute-done((bf16[1024,128]{1,0:T(8,128)(2,1)S(1)}, bf16[1024,128]{1,0:T(8,128)(2,1)S(1)}, u32[]{:S(2)}, u32[]{:S(2)}) %collective-permute-start.12) | collective-permute-done | bytes 262176 | tf_op jit(solution)/shard_map/ppermute | solution.py:55
  112.7 10.9 %shard_map.204 = (f32[256,1024]{1,0:T(8,128)S(1)}, bf16[256,1024]{1,0:T(8,128)(2,1)}, f32[512,768]{1,0:T(8,128)S(1)}, bf16[512,256]{1,0:T(8,128)(2,1)S(1)}, f32[512,4]{1,0:T(8,128)S(1)}) custom-call(bf16[256,1024]{1,0:T(8,128)(2,1)} %shard_map.201.own.refs_4_, bf16[256,1024]{1,0:T(8,128)(2,1)} %collective-permute-done.10.other.refs_5_, ...), custom_call_target="tpu_custom_call" | custom-call | flops 1000000000 | bytes 1000000 | tf_op jit(solution)/shard_map/pallas_call | solution.py:347
  127.3 11.4 %all-gather.9.cloned.1.call-start = ((), (), s32[]{:S(2)}) async-start(), calls=%async_computation.11 | async-start | bytes 1310720 | tf_op jit(solution)/shard_map/all_gather | solution.py:879
  143.6 11.0 %collective-permute-done.17.there.branch_there = bf16[256,1024]{1,0:T(8,128)(2,1)S(1)} collective-permute-done((bf16[256,1024]{1,0:T(8,128)(2,1)S(1)}, bf16[256,1024]{1,0:T(8,128)(2,1)S(1)}, u32[]{:S(2)}, u32[]{:S(2)}) %collective-permute-start.17) | collective-permute-done | bytes 524320 | tf_op jit(solution)/shard_map/ppermute | solution.py:32
  165.5 6.1 %shard_map.210 = (f32[256,1024]{1,0:T(8,128)S(1)}, bf16[256,1024]{1,0:T(8,128)(2,1)}, f32[512,1024]{1,0:T(8,128)S(1)}, bf16[512,1024]{1,0:T(8,128)(2,1)S(1)}) custom-call(bf16[256,1024]{1,0:T(8,128)(2,1)} %get-tuple-element.139.own.refs_1_, bf16[256,1024]{1,0:T(8,128)(2,1)} %collective-permute-done.18.other.refs_2_, bf16[1024,1024]{1,0:T(8,128)(2,1)S(1)} %shard_map.207.fc1, ...), custom_call_target="tpu_custom_call" | custom-call | flops 1000000000 | bytes 1000000 | tf_op jit(solution)/shard_map/pallas_call | solution.py:347
  175.1 4.1 all-to-all-start.2
  183.8 7.8 %all-to-all-done.2 = bf16[8,16,1024]{2,1,0:T(8,128)(2,1)} async-done(((bf16[8,16,1024]{2,1,0:T(8,128)(2,1)}), bf16[8,16,1024]{2,1,0:T(8,128)(2,1)}, u32[]{:S(2)}, u32[]{:S(2)}) %all-to-all-start.2) | async-done | bytes 262176 | tf_op jit(solution)/shard_map/all_to_all | solution.py:326
  195.2 6.7 %collective-permute-done.22 = bf16[128,1024]{1,0:T(8,128)(2,1)} collective-permute-done((bf16[128,1024]{1,0:T(8,128)(2,1)S(1)}, bf16[128,1024]{1,0:T(8,128)(2,1)}, u32[]{:S(2)}, u32[]{:S(2)}) %collective-permute-start.22) | collective-permute-done | bytes 262176 | tf_op jit(solution)/shard_map/ppermute | solution.py:32
  206.0 3.6 shard_map.212
  215.1 10.0 %shard_map.215 = (f32[256,1024]{1,0:T(8,128)S(1)}, bf16[256,1024]{1,0:T(8,128)(2,1)S(1)}, f32[512,768]{1,0:T(8,128)S(1)}, bf16[512,256]{1,0:T(8,128)(2,1)S(1)}, f32[512,4]{1,0:T(8,128)S(1)}) custom-call(bf16[256,1024]{1,0:T(8,128)(2,1)} %get-tuple-element.145.own.refs_4_, bf16[256,1024]{1,0:T(8,128)(2,1)} %collective-permute-done.23.other.refs_5_, ...), custom_call_target="tpu_custom_call" | custom-call | flops 1000000000 | bytes 1000000 | tf_op jit(solution)/shard_map/pallas_call | solution.py:347
  228.1 8.3 %collective-permute-done.26.there = bf16[4096,128]{1,0:T(8,128)(2,1)S(1)} collective-permute-done((bf16[4096,128]{1,0:T(8,128)(2,1)}, bf16[4096,128]{1,0:T(8,128)(2,1)S(1)}, u32[]{:S(2)}, u32[]{:S(2)}) %collective-permute-start.26) | collective-permute-done | bytes 1048608 | tf_op jit(solution)/shard_map/ppermute | solution.py:32
  240.5 10.9 %collective-permute-done.27.there.branch_there = bf16[256,1024]{1,0:T(8,128)(2,1)} collective-permute-done((bf16[256,1024]{1,0:T(8,128)(2,1)}, bf16[256,1024]{1,0:T(8,128)(2,1)}, u32[]{:S(2)}, u32[]{:S(2)}) %collective-permute-start.27) | collective-permute-done | bytes 524320 | tf_op jit(solution)/shard_map/ppermute | solution.py:32
  253.5 2.9 shard_map.217
  257.6 6.1 %collective-permute-done.29.there = bf16[4096,128]{1,0:T(8,128)(2,1)S(1)} collective-permute-done((bf16[4096,128]{1,0:T(8,128)(2,1)}, bf16[4096,128]{1,0:T(8,128)(2,1)S(1)}, u32[]{:S(2)}, u32[]{:S(2)}) %collective-permute-start.29) | collective-permute-done | bytes 1048608 | tf_op jit(solution)/shard_map/ppermute | solution.py:32
  264.9 3.3 shard_map.220
  270.9 13.4 %collective-permute-done.31.there = bf16[256,1024]{1,0:T(8,128)(2,1)S(1)} collective-permute-done((bf16[256,1024]{1,0:T(8,128)(2,1)S(1)}, bf16[256,1024]{1,0:T(8,128)(2,1)S(1)}, u32[]{:S(2)}, u32[]{:S(2)}) %collective-permute-start.31) | collective-permute-done | bytes 524320 | tf_op jit(solution)/shard_map/ppermute | solution.py:32
  289.1 6.5 %shard_map.225 = (f32[256,1024]{1,0:T(8,128)S(1)}, bf16[256,1024]{1,0:T(8,128)(2,1)S(1)}, bf16[512,1024]{1,0:T(8,128)(2,1)S(1)}) custom-call(bf16[256,1024]{1,0:T(8,128)(2,1)S(1)} %get-tuple-element.162.refs_1_.own, bf16[256,1024]{1,0:T(8,128)(2,1)S(1)} %collective-permute-done.32.refs_2_.other, f32[512,1024]{1,0:T(8,128)S(1)} %get-tuple-element.167.hidden_in, ...), custom_call_target="tpu_custom_call" | custom-call | flops 1000000000 | bytes 1000000 | tf_op jit(solution)/shard_map/pallas_call | solution.py:347
  304.7 7.1 %collective-permute-done.34.there = bf16[256,1024]{1,0:T(8,128)(2,1)S(1)} collective-permute-done((bf16[256,1024]{1,0:T(8,128)(2,1)S(1)}, bf16[256,1024]{1,0:T(8,128)(2,1)S(1)}, u32[]{:S(2)}, u32[]{:S(2)}) %collective-permute-start.34) | collective-permute-done | bytes 524320 | tf_op jit(solution)/shard_map/ppermute | solution.py:32
  311.8 9.5 %collective-permute-done.35.arrived = bf16[1024,512]{1,0:T(8,128)(2,1)S(1)} collective-permute-done((bf16[1024,512]{1,0:T(8,128)(2,1)S(1)}, bf16[1024,512]{1,0:T(8,128)(2,1)S(1)}, u32[]{:S(2)}, u32[]{:S(2)}) %collective-permute-start.35) | collective-permute-done | bytes 1048608 | tf_op jit(solution)/shard_map/ppermute | solution.py:32
  321.2 4.1 shard_map.227
  332.6 10.9 %shard_map.228 = (f32[256,1024]{1,0:T(8,128)S(1)}, bf16[256,1024]{1,0:T(8,128)(2,1)S(1)}, bf16[512,768]{1,0:T(8,128)(2,1)S(1)}, f32[1,4]{1,0:T(1,128)S(1)}) custom-call(bf16[256,1024]{1,0:T(8,128)(2,1)} %get-tuple-element.176.own.refs_1_, bf16[256,1024]{1,0:T(8,128)(2,1)} %collective-permute-done.36.other.refs_2_, f32[512,768]{1,0:T(8,128)S(1)} %copy-done.26, ...), custom_call_target="tpu_custom_call" | custom-call | flops 1000000000 | bytes 1000000 | tf_op jit(solution)/shard_map/pallas_call | solution.py:347
  346.4 3.5 shard_map.229
  352.2 7.7 %collective-permute-done.38.there = bf16[256,1024]{1,0:T(8,128)(2,1)S(1)} collective-permute-done((bf16[256,1024]{1,0:T(8,128)(2,1)S(1)}, bf16[256,1024]{1,0:T(8,128)(2,1)S(1)}, u32[]{:S(2)}, u32[]{:S(2)}) %collective-permute-start.38) | collective-permute-done | bytes 524320 | tf_op jit(solution)/shard_map/ppermute | solution.py:32
  359.8 9.5 %collective-permute-done.39.arrived = bf16[1024,512]{1,0:T(8,128)(2,1)S(1)} collective-permute-done((bf16[1024,512]{1,0:T(8,128)(2,1)S(1)}, bf16[1024,512]{1,0:T(8,128)(2,1)S(1)}, u32[]{:S(2)}, u32[]{:S(2)}) %collective-permute-start.39) | collective-permute-done | bytes 1048608 | tf_op jit(solution)/shard_map/ppermute | solution.py:32
  369.3 3.8 shard_map.230
  378.1 2.9 shard_map.231
  381.1 2.7 copy-done.8
  383.9 7.6 %shard_map.232 = (f32[256,1024]{1,0:T(8,128)S(1)}, bf16[256,1024]{1,0:T(8,128)(2,1)S(1)}, bf16[512,1024]{1,0:T(8,128)(2,1)S(1)}) custom-call(bf16[256,1024]{1,0:T(8,128)(2,1)} %get-tuple-element.189.refs_1_.own, bf16[256,1024]{1,0:T(8,128)(2,1)S(1)} %collective-permute-done.40.refs_2_.other, f32[512,1024]{1,0:T(8,128)S(1)} %copy-done.8, ...), custom_call_target="tpu_custom_call" | custom-call | flops 1000000000 | bytes 1000000 | tf_op jit(solution)/shard_map/pallas_call | solution.py:347
  394.2 4.2 shard_map.233
  399.7 8.1 %collective-permute-done.42.there = bf16[256,1024]{1,0:T(8,128)(2,1)S(1)} collective-permute-done((bf16[256,1024]{1,0:T(8,128)(2,1)S(1)}, bf16[256,1024]{1,0:T(8,128)(2,1)S(1)}, u32[]{:S(2)}, u32[]{:S(2)}) %collective-permute-start.42) | collective-permute-done | bytes 524320 | tf_op jit(solution)/shard_map/ppermute | solution.py:32
  407.9 9.3 %collective-permute-done.43.arrived = bf16[1024,512]{1,0:T(8,128)(2,1)S(1)} collective-permute-done((bf16[1024,512]{1,0:T(8,128)(2,1)S(1)}, bf16[1024,512]{1,0:T(8,128)(2,1)S(1)}, u32[]{:S(2)}, u32[]{:S(2)}) %collective-permute-start.43) | collective-permute-done | bytes 1048608 | tf_op jit(solution)/shard_map/ppermute | solution.py:32
  428.2 9.5 %shard_map.235 = (f32[256,1024]{1,0:T(8,128)S(1)}, bf16[256,1024]{1,0:T(8,128)(2,1)S(1)}, bf16[512,768]{1,0:T(8,128)(2,1)S(1)}, f32[1,4]{1,0:T(1,128)S(1)}) custom-call(bf16[256,1024]{1,0:T(8,128)(2,1)S(1)} %get-tuple-element.204.own.refs_1_, bf16[256,1024]{1,0:T(8,128)(2,1)S(1)} %collective-permute-done.44.other.refs_2_, f32[512,768]{1,0:T(8,128)S(1)} %copy-done.22, ...), custom_call_target="tpu_custom_call" | custom-call | flops 1000000000 | bytes 1000000 | tf_op jit(solution)/shard_map/pallas_call | solution.py:347
  440.8 4.2 shard_map.236
  445.0 8.8 %collective-permute-done.46.there = bf16[256,1024]{1,0:T(8,128)(2,1)S(1)} collective-permute-done((bf16[256,1024]{1,0:T(8,128)(2,1)S(1)}, bf16[256,1024]{1,0:T(8,128)(2,1)S(1)}, u32[]{:S(2)}, u32[]{:S(2)}) %collective-permute-start.46) | collective-permute-done | bytes 524320 | tf_op jit(solution)/shard_map/ppermute | solution.py:32
  454.7 8.7 %collective-permute-done.47.arrived = bf16[1024,512]{1,0:T(8,128)(2,1)S(1)} collective-permute-done((bf16[1024,512]{1,0:T(8,128)(2,1)S(1)}, bf16[1024,512]{1,0:T(8,128)(2,1)S(1)}, u32[]{:S(2)}, u32[]{:S(2)}) %collective-permute-start.47) | collective-permute-done | bytes 1048608 | tf_op jit(solution)/shard_map/ppermute | solution.py:32
  477.4 4.2 all-to-all-start.3
  481.7 15.7 %collective-permute-done.53 = bf16[1024,512]{1,0:T(8,128)(2,1)} collective-permute-done((bf16[1024,512]{1,0:T(8,128)(2,1)}, bf16[1024,512]{1,0:T(8,128)(2,1)}, u32[]{:S(2)}, u32[]{:S(2)}) %collective-permute-start.53) | collective-permute-done | bytes 1048608 | tf_op jit(solution)/shard_map/ppermute | solution.py:32
  497.4 3.0 fusion.22
  505.0 16.0 %collective-permute-done.57.arrived = bf16[1024,512]{1,0:T(8,128)(2,1)S(1)} collective-permute-done((bf16[1024,512]{1,0:T(8,128)(2,1)}, bf16[1024,512]{1,0:T(8,128)(2,1)S(1)}, u32[]{:S(2)}, u32[]{:S(2)}) %collective-permute-start.57) | collective-permute-done | bytes 1048608 | tf_op jit(solution)/shard_map/ppermute | solution.py:32
  536.9 5.1 collective-permute-done.51
  543.1 6.6 %collective-permute-done.52 = f32[40,256]{1,0:T(8,128)S(1)} collective-permute-done((f32[40,256]{1,0:T(8,128)S(1)}, f32[40,256]{1,0:T(8,128)S(1)}, u32[]{:S(2)}, u32[]{:S(2)}) %collective-permute-start.52) | collective-permute-done | bytes 40992 | tf_op jit(solution)/shard_map/ppermute | solution.py:32
  (585 shorter events, 192.4 us)
Async XLA Ops:
  7.2 15.0 %collective-permute-start.1 = (s32[1,4]{1,0:T(1,128)}, s32[1,4]{1,0:T(1,128)S(1)}, u32[]{:S(2)}, u32[]{:S(2)}) collective-permute-start(s32[1,4]{1,0:T(1,128)} %param.17), channel_id=1, source_target_pairs={{0,4},{4,0},{8,12},{12,8},{16,20},{20,16},{24,28},{28,24},{1,5},{5... | collective-permute-start | bytes 56 | tf_op jit(solution)/shard_map/ppermute | solution.py:32
  12.7 28.1 %all-to-all-start = ((bf16[8,16,1024]{2,1,0:T(8,128)(2,1)}), bf16[8,16,1024]{2,1,0:T(8,128)(2,1)S(1)}, u32[]{:S(2)}, u32[]{:S(2)}) async-start(bf16[8,16,1024]{2,1,0:T(8,128)(2,1)} %bitcast.3), calls=%async_computation | async-start | bytes 524288 | tf_op jit(solution)/shard_map/all_to_all | solution.py:326
  17.6 38.8 %all-gather.5.cloned.1.call-start = ((), (), s32[]{:S(2)}) async-start(), calls=%async_computation.9 | async-start | bytes 1310720 | tf_op jit(solution)/shard_map/all_gather | solution.py:879
  36.2 43.1 %collective-permute-start.9 = (bf16[2048,128]{1,0:T(8,128)(2,1)}, bf16[2048,128]{1,0:T(8,128)(2,1)S(1)}, u32[]{:S(2)}, u32[]{:S(2)}) collective-permute-start(bf16[2048,128]{1,0:T(8,128)(2,1)} %shard_map.200), channel_id=1, source_target_pairs={{0,4},{4,0},{8,12},{12,8},{16,20},{20,16},{24,28},{28,24},{1,5},{5... | collective-permute-start | bytes 1572872 | tf_op jit(solution)/shard_map/ppermute | solution.py:32
  41.7 13.6 %collective-permute-start = (bf16[128,1024]{1,0:T(8,128)(2,1)S(1)}, bf16[128,1024]{1,0:T(8,128)(2,1)}, u32[]{:S(2)}, u32[]{:S(2)}) collective-permute-start(bf16[128,1024]{1,0:T(8,128)(2,1)S(1)} %shard_map.196), channel_id=1, source_target_pairs={{0,2},{1,3},{2,0},{3,1},{4,6},{5,7},{6,4},{7,5},{8,10},{9,11},{10,... | collective-permute-start | bytes 786440 | tf_op jit(solution)/shard_map/ppermute | solution.py:32
  44.1 15.0 %all-to-all-start.1 = ((bf16[8,16,768]{2,1,0:T(8,128)(2,1)}), bf16[8,16,768]{2,1,0:T(8,128)(2,1)S(1)}, u32[]{:S(2)}, u32[]{:S(2)}) async-start(bf16[8,16,768]{2,1,0:T(8,128)(2,1)} %reshape.286), calls=%async_computation.1 | async-start | bytes 393216 | tf_op jit(solution)/shard_map/all_to_all | solution.py:326
  50.0 131.8 %all-gather.7.cloned.1.call-start = ((), (), s32[]{:S(2)}) async-start(), calls=%async_computation.10 | async-start | bytes 1310720 | tf_op jit(solution)/shard_map/all_gather | solution.py:879
  50.1 10.5 %collective-permute-start.8 = (bf16[1024,128]{1,0:T(8,128)(2,1)S(1)}, bf16[1024,128]{1,0:T(8,128)(2,1)S(1)}, u32[]{:S(2)}, u32[]{:S(2)}) collective-permute-start(bf16[1024,128]{1,0:T(8,128)(2,1)S(1)} %shard_map.199.refs_0_), channel_id=1, source_target_pairs={{0,24},{4,28},{8,0},{12,4},{16,8},{20,12},{24,16},{28,20},{1,25},{... | collective-permute-start | bytes 786440 | tf_op jit(solution)/shard_map/ppermute | solution.py:55
  53.9 25.3 %collective-permute-start.7 = (bf16[1024,128]{1,0:T(8,128)(2,1)S(1)}, bf16[1024,128]{1,0:T(8,128)(2,1)S(1)}, u32[]{:S(2)}, u32[]{:S(2)}) collective-permute-start(bf16[1024,128]{1,0:T(8,128)(2,1)S(1)} %shard_map.199.refs_0_), channel_id=1, source_target_pairs={{0,16},{4,20},{8,24},{12,28},{16,0},{20,4},{24,8},{28,12},{1,17},{... | collective-permute-start | bytes 786440 | tf_op jit(solution)/shard_map/ppermute | solution.py:55
  53.9 25.3 %collective-permute-start.6 = (bf16[1024,128]{1,0:T(8,128)(2,1)S(1)}, bf16[1024,128]{1,0:T(8,128)(2,1)S(1)}, u32[]{:S(2)}, u32[]{:S(2)}) collective-permute-start(bf16[1024,128]{1,0:T(8,128)(2,1)S(1)} %shard_map.199.refs_0_), channel_id=1, source_target_pairs={{0,8},{4,12},{8,16},{12,20},{16,24},{20,28},{24,0},{28,4},{1,9},{5... | collective-permute-start | bytes 786440 | tf_op jit(solution)/shard_map/ppermute | solution.py:55
  56.4 53.3 %collective-permute-start.14 = (bf16[4096,128]{1,0:T(8,128)(2,1)}, bf16[4096,128]{1,0:T(8,128)(2,1)}, u32[]{:S(2)}, u32[]{:S(2)}) collective-permute-start(bf16[4096,128]{1,0:T(8,128)(2,1)} %all-gather.5.cloned.1.call-done.here), channel_id=1, source_target_pairs={{0,4},{4,0},{8,12},{12,8},{16,20},{20,16},{24,28},{28,24},{1,5},{5... | collective-permute-start | bytes 3145736 | tf_op jit(solution)/shard_map/ppermute | solution.py:32
  81.7 28.0 %collective-permute-start.10 = (bf16[256,1024]{1,0:T(8,128)(2,1)}, bf16[256,1024]{1,0:T(8,128)(2,1)}, u32[]{:S(2)}, u32[]{:S(2)}) collective-permute-start(bf16[256,1024]{1,0:T(8,128)(2,1)} %shard_map.201.own.refs_4_), channel_id=1, source_target_pairs={{0,1},{1,0},{2,3},{3,2},{4,5},{5,4},{6,7},{7,6},{8,9},{9,8},{10,11... | collective-permute-start | bytes 1572872 | tf_op jit(solution)/shard_map/ppermute | solution.py:32
  84.2 10.0 %collective-permute-start.13 = (bf16[1024,128]{1,0:T(8,128)(2,1)S(1)}, bf16[1024,128]{1,0:T(8,128)(2,1)S(1)}, u32[]{:S(2)}, u32[]{:S(2)}) collective-permute-start(bf16[1024,128]{1,0:T(8,128)(2,1)S(1)} %get-tuple-element.131.refs_1_.refs_0_), channel_id=1, source_target_pairs={{0,24},{4,28},{8,0},{12,4},{16,8},{20,12},{24,16},{28,20},{1,25},{... | collective-permute-start | bytes 786440 | tf_op jit(solution)/shard_map/ppermute | solution.py:55
  84.2 24.1 %collective-permute-start.12 = (bf16[1024,128]{1,0:T(8,128)(2,1)S(1)}, bf16[1024,128]{1,0:T(8,128)(2,1)S(1)}, u32[]{:S(2)}, u32[]{:S(2)}) collective-permute-start(bf16[1024,128]{1,0:T(8,128)(2,1)S(1)} %get-tuple-element.131.refs_1_.refs_0_), channel_id=1, source_target_pairs={{0,16},{4,20},{8,24},{12,28},{16,0},{20,4},{24,8},{28,12},{1,17},{... | collective-permute-start | bytes 786440 | tf_op jit(solution)/shard_map/ppermute | solution.py:55
  84.5 24.5 %collective-permute-start.11 = (bf16[1024,128]{1,0:T(8,128)(2,1)S(1)}, bf16[1024,128]{1,0:T(8,128)(2,1)S(1)}, u32[]{:S(2)}, u32[]{:S(2)}) collective-permute-start(bf16[1024,128]{1,0:T(8,128)(2,1)S(1)} %get-tuple-element.131.refs_1_.refs_0_), channel_id=1, source_target_pairs={{0,8},{4,12},{8,16},{12,20},{16,24},{20,28},{24,0},{28,4},{1,9},{5... | collective-permute-start | bytes 786440 | tf_op jit(solution)/shard_map/ppermute | solution.py:55
  94.2 46.1 %collective-permute-start.16 = (bf16[3072,128]{1,0:T(8,128)(2,1)}, bf16[3072,128]{1,0:T(8,128)(2,1)}, u32[]{:S(2)}, u32[]{:S(2)}) collective-permute-start(bf16[3072,128]{1,0:T(8,128)(2,1)} %shard_map.205), channel_id=1, source_target_pairs={{0,4},{4,0},{8,12},{12,8},{16,20},{20,16},{24,28},{28,24},{1,5},{5... | collective-permute-start | bytes 2359304 | tf_op jit(solution)/shard_map/ppermute | solution.py:32
  126.4 12.3 %collective-permute-start.15 = (bf16[256,1024]{1,0:T(8,128)(2,1)}, bf16[256,1024]{1,0:T(8,128)(2,1)}, u32[]{:S(2)}, u32[]{:S(2)}) collective-permute-start(bf16[256,1024]{1,0:T(8,128)(2,1)} %get-tuple-element.136), channel_id=1, source_target_pairs={{0,1},{1,0},{2,3},{3,2},{4,5},{5,4},{6,7},{7,6},{8,9},{9,8},{10,11... | collective-permute-start | bytes 1572872 | tf_op jit(solution)/shard_map/ppermute | solution.py:32
  127.3 83.4 %all-gather.9.cloned.1.call-start = ((), (), s32[]{:S(2)}) async-start(), calls=%async_computation.11 | async-start | bytes 1310720 | tf_op jit(solution)/shard_map/all_gather | solution.py:879
  140.3 14.4 %collective-permute-start.17 = (bf16[256,1024]{1,0:T(8,128)(2,1)S(1)}, bf16[256,1024]{1,0:T(8,128)(2,1)S(1)}, u32[]{:S(2)}, u32[]{:S(2)}) collective-permute-start(bf16[256,1024]{1,0:T(8,128)(2,1)S(1)} %add_convert_fusion.7.here.branch_here), channel_id=1, source_target_pairs={{0,2},{1,3},{2,0},{3,1},{4,6},{5,7},{6,4},{7,5},{8,10},{9,11},{10,... | collective-permute-start | bytes 1572872 | tf_op jit(solution)/shard_map/ppermute | solution.py:32
  141.8 21.8 %collective-permute-start.19 = (bf16[3072,128]{1,0:T(8,128)(2,1)}, bf16[3072,128]{1,0:T(8,128)(2,1)}, u32[]{:S(2)}, u32[]{:S(2)}) collective-permute-start(bf16[3072,128]{1,0:T(8,128)(2,1)} %shard_map.208), channel_id=1, source_target_pairs={{0,4},{4,0},{8,12},{12,8},{16,20},{20,16},{24,28},{28,24},{1,5},{5... | collective-permute-start | bytes 2359304 | tf_op jit(solution)/shard_map/ppermute | solution.py:32
  175.1 16.5 %all-to-all-start.2 = ((bf16[8,16,1024]{2,1,0:T(8,128)(2,1)}), bf16[8,16,1024]{2,1,0:T(8,128)(2,1)}, u32[]{:S(2)}, u32[]{:S(2)}) async-start(bf16[8,16,1024]{2,1,0:T(8,128)(2,1)} %bitcast.108), calls=%async_computation.2 | async-start | bytes 524288 | tf_op jit(solution)/shard_map/all_to_all | solution.py:326
  179.2 59.8 %all-gather.11.cloned.1.call-start = ((), (), s32[]{:S(2)}) async-start(), calls=%async_computation.12 | async-start | bytes 1310720 | tf_op jit(solution)/shard_map/all_gather | solution.py:879
  181.2 21.7 %collective-permute-start.21 = (bf16[256,1024]{1,0:T(8,128)(2,1)}, bf16[256,1024]{1,0:T(8,128)(2,1)}, u32[]{:S(2)}, u32[]{:S(2)}) collective-permute-start(bf16[256,1024]{1,0:T(8,128)(2,1)} %add_convert_fusion.6.here.branch_here), channel_id=1, source_target_pairs={{0,2},{1,3},{2,0},{3,1},{4,6},{5,7},{6,4},{7,5},{8,10},{9,11},{10,... | collective-permute-start | bytes 1572872 | tf_op jit(solution)/shard_map/ppermute | solution.py:32
  181.8 30.3 %collective-permute-start.24 = (bf16[4096,128]{1,0:T(8,128)(2,1)}, bf16[4096,128]{1,0:T(8,128)(2,1)}, u32[]{:S(2)}, u32[]{:S(2)}) collective-permute-start(bf16[4096,128]{1,0:T(8,128)(2,1)} %all-gather.7.cloned.1.call-done.here), channel_id=1, source_target_pairs={{0,4},{4,0},{8,12},{12,8},{16,20},{20,16},{24,28},{28,24},{1,5},{5... | collective-permute-start | bytes 3145736 | tf_op jit(solution)/shard_map/ppermute | solution.py:32
  195.1 309.9 %reduce-scatter.14.cloned.1.call-start = ((), (), s32[]{:S(2)}) async-start(), calls=%async_computation.17 | async-start | bytes 1310720 | tf_op jit(solution)/shard_map/reduce_scatter | solution.py:267
  210.6 25.8 %collective-permute-start.26 = (bf16[4096,128]{1,0:T(8,128)(2,1)}, bf16[4096,128]{1,0:T(8,128)(2,1)S(1)}, u32[]{:S(2)}, u32[]{:S(2)}) collective-permute-start(bf16[4096,128]{1,0:T(8,128)(2,1)} %all-gather.9.cloned.1.call-done.here), channel_id=1, source_target_pairs={{0,4},{4,0},{8,12},{12,8},{16,20},{20,16},{24,28},{28,24},{1,5},{5... | collective-permute-start | bytes 3145736 | tf_op jit(solution)/shard_map/ppermute | solution.py:32
  237.5 13.9 %collective-permute-start.27 = (bf16[256,1024]{1,0:T(8,128)(2,1)}, bf16[256,1024]{1,0:T(8,128)(2,1)}, u32[]{:S(2)}, u32[]{:S(2)}) collective-permute-start(bf16[256,1024]{1,0:T(8,128)(2,1)} %add_convert_fusion.5.here.branch_here), channel_id=1, source_target_pairs={{0,2},{1,3},{2,0},{3,1},{4,6},{5,7},{6,4},{7,5},{8,10},{9,11},{10,... | collective-permute-start | bytes 1572872 | tf_op jit(solution)/shard_map/ppermute | solution.py:32
  239.0 24.7 %collective-permute-start.29 = (bf16[4096,128]{1,0:T(8,128)(2,1)}, bf16[4096,128]{1,0:T(8,128)(2,1)S(1)}, u32[]{:S(2)}, u32[]{:S(2)}) collective-permute-start(bf16[4096,128]{1,0:T(8,128)(2,1)} %all-gather.11.cloned.1.call-done.here), channel_id=1, source_target_pairs={{0,4},{4,0},{8,12},{12,8},{16,20},{20,16},{24,28},{28,24},{1,5},{5... | collective-permute-start | bytes 3145736 | tf_op jit(solution)/shard_map/ppermute | solution.py:32
  270.4 14.0 %collective-permute-start.31 = (bf16[256,1024]{1,0:T(8,128)(2,1)S(1)}, bf16[256,1024]{1,0:T(8,128)(2,1)S(1)}, u32[]{:S(2)}, u32[]{:S(2)}) collective-permute-start(bf16[256,1024]{1,0:T(8,128)(2,1)S(1)} %add_convert_fusion.4.here), channel_id=1, source_target_pairs={{0,2},{1,3},{2,0},{3,1},{4,6},{5,7},{6,4},{7,5},{8,10},{9,11},{10,... | collective-permute-start | bytes 1572872 | tf_op jit(solution)/shard_map/ppermute | solution.py:32
  295.8 25.4 %collective-permute-start.35 = (bf16[1024,512]{1,0:T(8,128)(2,1)S(1)}, bf16[1024,512]{1,0:T(8,128)(2,1)S(1)}, u32[]{:S(2)}, u32[]{:S(2)}) collective-permute-start(bf16[1024,512]{1,0:T(8,128)(2,1)S(1)} %get-tuple-element.166), channel_id=1, source_target_pairs={{0,4},{4,0},{8,12},{12,8},{16,20},{20,16},{24,28},{28,24},{1,5},{5... | collective-permute-start | bytes 3145736 | tf_op jit(solution)/shard_map/ppermute | solution.py:32
  297.7 14.0 %collective-permute-start.34 = (bf16[256,1024]{1,0:T(8,128)(2,1)S(1)}, bf16[256,1024]{1,0:T(8,128)(2,1)S(1)}, u32[]{:S(2)}, u32[]{:S(2)}) collective-permute-start(bf16[256,1024]{1,0:T(8,128)(2,1)S(1)} %add_convert_fusion.3.here), channel_id=1, source_target_pairs={{0,2},{1,3},{2,0},{3,1},{4,6},{5,7},{6,4},{7,5},{8,10},{9,11},{10,... | collective-permute-start | bytes 1572872 | tf_op jit(solution)/shard_map/ppermute | solution.py:32
  328.3 176.6 %reduce-scatter.10.cloned.1.call-start = ((), (), s32[]{:S(2)}) async-start(), calls=%async_computation.15 | async-start | bytes 1310720 | tf_op jit(solution)/shard_map/reduce_scatter | solution.py:267
  343.8 25.5 %collective-permute-start.39 = (bf16[1024,512]{1,0:T(8,128)(2,1)S(1)}, bf16[1024,512]{1,0:T(8,128)(2,1)S(1)}, u32[]{:S(2)}, u32[]{:S(2)}) collective-permute-start(bf16[1024,512]{1,0:T(8,128)(2,1)S(1)} %copy-done.110), channel_id=1, source_target_pairs={{0,4},{4,0},{8,12},{12,8},{16,20},{20,16},{24,28},{28,24},{1,5},{5... | collective-permute-start | bytes 3145736 | tf_op jit(solution)/shard_map/ppermute | solution.py:32
  345.8 14.0 %collective-permute-start.38 = (bf16[256,1024]{1,0:T(8,128)(2,1)S(1)}, bf16[256,1024]{1,0:T(8,128)(2,1)S(1)}, u32[]{:S(2)}, u32[]{:S(2)}) collective-permute-start(bf16[256,1024]{1,0:T(8,128)(2,1)S(1)} %add_convert_fusion.2.here), channel_id=1, source_target_pairs={{0,2},{1,3},{2,0},{3,1},{4,6},{5,7},{6,4},{7,5},{8,10},{9,11},{10,... | collective-permute-start | bytes 1572872 | tf_op jit(solution)/shard_map/ppermute | solution.py:32
  376.2 147.7 %reduce-scatter.6.cloned.1.call-start = ((), (), s32[]{:S(2)}) async-start(), calls=%async_computation.13 | async-start | bytes 1310720 | tf_op jit(solution)/shard_map/reduce_scatter | solution.py:267
  391.9 25.3 %collective-permute-start.43 = (bf16[1024,512]{1,0:T(8,128)(2,1)S(1)}, bf16[1024,512]{1,0:T(8,128)(2,1)S(1)}, u32[]{:S(2)}, u32[]{:S(2)}) collective-permute-start(bf16[1024,512]{1,0:T(8,128)(2,1)S(1)} %copy-done.108), channel_id=1, source_target_pairs={{0,4},{4,0},{8,12},{12,8},{16,20},{20,16},{24,28},{28,24},{1,5},{5... | collective-permute-start | bytes 3145736 | tf_op jit(solution)/shard_map/ppermute | solution.py:32
  393.7 14.2 %collective-permute-start.42 = (bf16[256,1024]{1,0:T(8,128)(2,1)S(1)}, bf16[256,1024]{1,0:T(8,128)(2,1)S(1)}, u32[]{:S(2)}, u32[]{:S(2)}) collective-permute-start(bf16[256,1024]{1,0:T(8,128)(2,1)S(1)} %add_convert_fusion.1.here), channel_id=1, source_target_pairs={{0,2},{1,3},{2,0},{3,1},{4,6},{5,7},{6,4},{7,5},{8,10},{9,11},{10,... | collective-permute-start | bytes 1572872 | tf_op jit(solution)/shard_map/ppermute | solution.py:32
  418.5 133.8 %reduce-scatter.12.cloned.1.call-start = ((), (), s32[]{:S(2)}) async-start(), calls=%async_computation.16 | async-start | bytes 1310720 | tf_op jit(solution)/shard_map/reduce_scatter | solution.py:267
  437.9 25.4 %collective-permute-start.47 = (bf16[1024,512]{1,0:T(8,128)(2,1)S(1)}, bf16[1024,512]{1,0:T(8,128)(2,1)S(1)}, u32[]{:S(2)}, u32[]{:S(2)}) collective-permute-start(bf16[1024,512]{1,0:T(8,128)(2,1)S(1)} %copy-done.104), channel_id=1, source_target_pairs={{0,4},{4,0},{8,12},{12,8},{16,20},{20,16},{24,28},{28,24},{1,5},{5... | collective-permute-start | bytes 3145736 | tf_op jit(solution)/shard_map/ppermute | solution.py:32
  439.8 14.0 %collective-permute-start.46 = (bf16[256,1024]{1,0:T(8,128)(2,1)S(1)}, bf16[256,1024]{1,0:T(8,128)(2,1)S(1)}, u32[]{:S(2)}, u32[]{:S(2)}) collective-permute-start(bf16[256,1024]{1,0:T(8,128)(2,1)S(1)} %add_convert_fusion.here), channel_id=1, source_target_pairs={{0,2},{1,3},{2,0},{3,1},{4,6},{5,7},{6,4},{7,5},{8,10},{9,11},{10,... | collective-permute-start | bytes 1572872 | tf_op jit(solution)/shard_map/ppermute | solution.py:32
  440.4 24.4 %collective-permute-start.49 = (f32[8,6144]{1,0:T(8,128)S(1)}, f32[8,6144]{1,0:T(8,128)S(1)}, u32[]{:S(2)}, u32[]{:S(2)}) collective-permute-start(f32[8,6144]{1,0:T(8,128)S(1)} %shard_map.241.own), channel_id=1, source_target_pairs={{0,1},{1,0},{2,3},{3,2},{4,5},{5,4},{6,7},{7,6},{8,9},{9,8},{10,11... | collective-permute-start | bytes 589832 | tf_op jit(solution)/shard_map/ppermute | solution.py:32
  467.4 30.0 %collective-permute-start.53 = (bf16[1024,512]{1,0:T(8,128)(2,1)}, bf16[1024,512]{1,0:T(8,128)(2,1)}, u32[]{:S(2)}, u32[]{:S(2)}) collective-permute-start(bf16[1024,512]{1,0:T(8,128)(2,1)} %get-tuple-element.213), channel_id=1, source_target_pairs={{0,4},{4,0},{8,12},{12,8},{16,20},{20,16},{24,28},{28,24},{1,5},{5... | collective-permute-start | bytes 3145736 | tf_op jit(solution)/shard_map/ppermute | solution.py:32
  470.7 50.2 %collective-permute-start.57 = (bf16[1024,512]{1,0:T(8,128)(2,1)}, bf16[1024,512]{1,0:T(8,128)(2,1)S(1)}, u32[]{:S(2)}, u32[]{:S(2)}) collective-permute-start(bf16[1024,512]{1,0:T(8,128)(2,1)} %get-tuple-element.200), channel_id=1, source_target_pairs={{0,4},{4,0},{8,12},{12,8},{16,20},{20,16},{24,28},{28,24},{1,5},{5... | collective-permute-start | bytes 3145736 | tf_op jit(solution)/shard_map/ppermute | solution.py:32
  477.4 51.6 %all-to-all-start.3 = ((bf16[8,38,1024]{2,1,0:T(8,128)(2,1)}), bf16[8,38,1024]{2,1,0:T(8,128)(2,1)}, u32[]{:S(2)}, u32[]{:S(2)}) async-start(bf16[8,38,1024]{2,1,0:T(8,128)(2,1)} %pad_maximum_fusion.1), calls=%async_computation.3 | async-start | bytes 1310720 | tf_op jit(solution)/shard_map/all_to_all | solution.py:326
  481.6 70.7 %reduce-scatter.8.cloned.1.call-start = ((), (), s32[]{:S(2)}) async-start(), calls=%async_computation.14 | async-start | bytes 1310720 | tf_op jit(solution)/shard_map/reduce_scatter | solution.py:267
  501.2 25.8 %collective-permute-start.54 = (bf16[1024,128]{1,0:T(8,128)(2,1)}, bf16[1024,128]{1,0:T(8,128)(2,1)S(1)}, u32[]{:S(2)}, u32[]{:S(2)}) collective-permute-start(bf16[1024,128]{1,0:T(8,128)(2,1)} %get-tuple-element.272), channel_id=1, source_target_pairs={{0,24},{4,28},{8,0},{12,4},{16,8},{20,12},{24,16},{28,20},{1,25},{... | collective-permute-start | bytes 786440 | tf_op jit(solution)/shard_map/ppermute | solution.py:277
  501.9 25.1 %collective-permute-start.56 = (bf16[1024,128]{1,0:T(8,128)(2,1)S(1)}, bf16[1024,128]{1,0:T(8,128)(2,1)S(1)}, u32[]{:S(2)}, u32[]{:S(2)}) collective-permute-start(bf16[1024,128]{1,0:T(8,128)(2,1)S(1)} %get-tuple-element.273), channel_id=1, source_target_pairs={{0,8},{4,12},{8,16},{12,20},{16,24},{20,28},{24,0},{28,4},{1,9},{5... | collective-permute-start | bytes 786440 | tf_op jit(solution)/shard_map/ppermute | solution.py:277
  503.4 23.6 %collective-permute-start.55 = (bf16[1024,128]{1,0:T(8,128)(2,1)S(1)}, bf16[1024,128]{1,0:T(8,128)(2,1)S(1)}, u32[]{:S(2)}, u32[]{:S(2)}) collective-permute-start(bf16[1024,128]{1,0:T(8,128)(2,1)S(1)} %get-tuple-element.274), channel_id=1, source_target_pairs={{0,16},{4,20},{8,24},{12,28},{16,0},{20,4},{24,8},{28,12},{1,17},{... | collective-permute-start | bytes 786440 | tf_op jit(solution)/shard_map/ppermute | solution.py:277
  (188 other events, 1745.0 us)
Sparse Core Ops, SparseCore 0:
  20.6 29.2 all-gather.4
  127.4 26.6 all-gather.6
  158.9 29.2 all-gather.8
  195.2 25.8 all-gather.10
  328.5 26.6 reduce-scatter.13
  376.3 26.5 reduce-scatter.9
  418.6 26.4 reduce-scatter.5
  464.9 30.1 reduce-scatter.11
  524.0 28.1 reduce-scatter.7

commit v3 on v2

--- a/solution.py
+++ b/solution.py
@@ -82,6 +82,15 @@
 def pack_fc1(fc1, layer):
     height = fc1.shape[1] * fc1.shape[2] // 128
     return call(functools.partial(pack_fc1_kernel, layer=layer), [((height, 128), low)], fc1)[0]
+
+
+def pack_pair_kernel(fc1, fc2, out, *, layer):
+    columns_of(fc1[layer], out, 0)
+    out[fc2.shape[1] :, :] = fc2[layer]
+
+
+def pack_pair(fc1, fc2, layer):
+    return call(functools.partial(pack_pair_kernel, layer=layer), [((2 * fc2.shape[1], 128), low)], fc1, fc2)[0]
 
 
 def stack_kernel(*refs):
@@ -247,7 +256,7 @@
     span = out.shape[2]
     for back in range(4):
         columns = slice(back * span, (back + 1) * span)
-        out[lax.rem(slow[0] + 4 - back, 4)] = (kept[:, columns] + arrived[:, columns].astype(wide)).astype(low)
+        out[lax.rem(slow[0] + 4 - back, 4)] = (kept[:, columns].astype(wide) + arrived[:, columns].astype(wide)).astype(low)
 
 
 def fold(kept, arrived, slow):
@@ -267,9 +276,9 @@
             self.blocks = lax.psum_scatter(
                 blocks, "dp", scatter_dimension=0, axis_index_groups=slow_groups, tiled=True
             )
-            return
+            return tie(marker, blocks)
         self.blocks = None
-        total = self.kept + tie(self.arrived, marker).astype(wide)
+        total = self.kept.astype(wide) + tie(self.arrived, marker).astype(wide)
         span = total.shape[1] // 4
         self.parts = [total[:, i * span : (i + 1) * span] for i in range(4)]
         for back in (1, 2, 3):
@@ -295,8 +304,15 @@
         return tie(self.result, marker).reshape(self.result.shape[1:]).astype(wide)
 
 
-def gather_cores(part_own, part_other):
-    return (part_own + swap(part_other, "shard", 1).astype(wide)).astype(low)
+def gather_cores_kernel(own, first, second, out):
+    half = first.shape[0]
+    out[:half, :] = (own[:half, :] + first[...].astype(wide)).astype(low)
+    out[half:, :] = (own[half:, :] + second[...].astype(wide)).astype(low)
+
+
+def gather_cores(part_own, parts_other):
+    arrived = [swap(part, "shard", 1) for part in parts_other]
+    return call(gather_cores_kernel, [(part_own.shape, low)], part_own, *arrived)[0]
 
 
 def route(dest, rows):
@@ -338,11 +354,10 @@
 
 
 grant = 24
-small = pl.CostEstimate(flops=1000000000, bytes_accessed=1000000, transcendentals=0)
 stripe = 64
 
 
-def call(kernel, outs, *operands, scratch=(), scalars=0):
+def call(kernel, outs, *operands, scratch=(), scalars=0, cost=1):
     spec = pl.BlockSpec(memory_space=pltpu.VMEM)
     return pl.pallas_call(
         kernel,
@@ -350,7 +365,7 @@
         in_specs=[pl.BlockSpec(memory_space=pltpu.SMEM)] * scalars + [spec] * (len(operands) - scalars),
         out_specs=[spec] * len(outs),
         scratch_shapes=list(scratch),
-        cost_estimate=small,
+        cost_estimate=pl.CostEstimate(flops=cost, bytes_accessed=1, transcendentals=0),
         compiler_params=pltpu.CompilerParams(vmem_limit_bytes=grant << 20),
     )(*operands)
 
@@ -425,18 +440,32 @@
     )[0]
 
 
-def mlp_kernel(own, other, fc1, fc2, part_own, part_other, hidden_out, act_out):
+def put_part(targets, at, value):
+    if len(targets) == 1:
+        targets[0][at, :] = value.astype(targets[0].dtype)
+        return
+    half = targets[0].shape[0]
+    for index, target in enumerate(targets):
+        first, last = max(at.start, index * half), min(at.stop, (index + 1) * half)
+        if first < last:
+            target[first - index * half : last - index * half, :] = value[first - at.start : last - at.start].astype(target.dtype)
+
+
+def mlp_kernel(own, other, fc1, fc2, part_own, part_a, part_b, slope_out, act_out):
     half = own.shape[0]
-    for place, source, target in ((0, own, part_own), (1, other, part_other)):
-        @pl.loop(0, half // 128)
-        def _(index):
-            at = pl.ds(pl.multiple_of(index * 128, 128), 128)
-            put = pl.ds(pl.multiple_of(place * half + index * 128, 128), 128)
+    for place, source, target in ((0, own, (part_own,)), (1, other, (part_a, part_b))):
+        for index in range(half // 256):
+            at = slice(index * 256, (index + 1) * 256)
+            put = slice(place * half + index * 256, place * half + (index + 1) * 256)
             hidden = matmul(source[at, :], fc1[...])
-            hidden_out[put, :] = hidden
-            activated = (0.5 * hidden * (1.0 + jnp.tanh(root * (hidden + cubic * hidden * hidden * hidden)))).astype(low)
+            square = hidden * hidden
+            bent = jnp.tanh(hidden * (root + (root * cubic) * square))
+            share = 0.5 + 0.5 * bent
+            activated = (hidden * share).astype(low)
+            slope = share + (hidden * (1.0 - bent * bent)) * (0.5 * root + (1.5 * root * cubic) * square)
+            slope_out[put, :] = slope.astype(low)
             act_out[put, :] = activated
-            target[at, :] = matmul(activated, fc2[...]).astype(target.dtype)
+            put_part(target, at, matmul(activated, fc2[...]))
 
 
 def mlp(own, other, fc1, fc2):
@@ -444,34 +473,29 @@
     units = fc1.shape[1]
     return call(
         mlp_kernel,
-        [((half, width), wide), ((half, width), low), ((2 * half, units), wide), ((2 * half, units), low)],
+        [((half, width), wide), ((half // 2, width), low), ((half // 2, width), low), ((2 * half, units), low), ((2 * half, units), low)],
         own, other, fc1, fc2,
     )
 
 
-def mlp_back_kernel(own, other, hidden_in, fc1, fc2, part_own, part_other, grad_out):
+def mlp_back_kernel(own, other, slope, fc1, fc2, part_own, part_a, part_b, grad_out):
     half = own.shape[0]
-    for place, source, target in ((0, own, part_own), (1, other, part_other)):
-        @pl.loop(0, half // 128)
-        def _(index):
-            at = pl.ds(pl.multiple_of(index * 128, 128), 128)
-            put = pl.ds(pl.multiple_of(place * half + index * 128, 128), 128)
+    for place, source, target in ((0, own, (part_own,)), (1, other, (part_a, part_b))):
+        for index in range(half // 256):
+            at = slice(index * 256, (index + 1) * 256)
+            put = slice(place * half + index * 256, place * half + (index + 1) * 256)
             grad_activated = contract_last(source[at, :], fc2[...])
-            hidden = hidden_in[put, :]
-            square = hidden * hidden
-            bent = jnp.tanh(root * (hidden + cubic * hidden * square))
-            slope = 0.5 * (1.0 + bent) + 0.5 * hidden * (1.0 - bent * bent) * (root * (1.0 + 3.0 * cubic * square))
-            grad_hidden = (grad_activated * slope).astype(low)
+            grad_hidden = (grad_activated * slope[put, :].astype(wide)).astype(low)
             grad_out[put, :] = grad_hidden
-            target[at, :] = contract_last(grad_hidden, fc1[...]).astype(target.dtype)
-
-
-def mlp_back(own, other, hidden, fc1, fc2):
+            put_part(target, at, contract_last(grad_hidden, fc1[...]))
+
+
+def mlp_back(own, other, slope, fc1, fc2):
     half, width = own.shape
     return call(
         mlp_back_kernel,
-        [((half, width), wide), ((half, width), low), (hidden.shape, low)],
-        own, other, hidden, fc1, fc2,
+        [((half, width), wide), ((half // 2, width), low), ((half // 2, width), low), (slope.shape, low)],
+        own, other, slope, fc1, fc2,
     )
 
 
@@ -498,35 +522,33 @@
 
 def attend_kernel(
     own, other, qkv, proj, scale, member, level, member_row, level_row,
-    part_own, part_other, raw_out, heads_out, inverse_out, queries, keys, values, *, heads,
+    part_own, part_a, part_b, kept, inverse_out, *, heads,
 ):
     half = own.shape[0]
     span = qkv.shape[1] // 3
-    block = 128
+    block = 256
+    queries, keys, values, heads_out = (kept.at[:, i * span : (i + 1) * span] for i in range(4))
     for place, source in ((0, own), (1, other)):
         @pl.loop(0, half // block)
         def _(index):
             at = pl.ds(pl.multiple_of(index * block, block), block)
             put = pl.ds(pl.multiple_of(place * half + index * block, block), block)
             projected = matmul(source[at, :], qkv[...])
-            raw_out[put, :] = projected
             masks = heads_of((block, span), heads)
             query, key = projected[:, :span], projected[:, span : 2 * span]
-            query_sums, key_sums = head_sums(query * query, masks), head_sums(key * key, masks)
-            query_scale = by_head(
-                [lax.rsqrt(total + epsilon) * jnp.exp(scale[:, head : head + 1]) for head, total in enumerate(query_sums)], masks
-            )
-            key_scale = by_head([lax.rsqrt(total + epsilon) for total in key_sums], masks)
-            queries[put, :] = (query * query_scale).astype(low)
-            keys[put, :] = (key * key_scale).astype(low)
+            inverse_q = [lax.rsqrt(total + epsilon) for total in head_sums(query * query, masks)]
+            inverse_k = [lax.rsqrt(total + epsilon) for total in head_sums(key * key, masks)]
+            rises = [jnp.exp(scale[:, head : head + 1]) for head in range(heads)]
+            queries[put, :] = (query * by_head([i * a for i, a in zip(inverse_q, rises)], masks)).astype(low)
+            keys[put, :] = (key * by_head(inverse_k, masks)).astype(low)
             values[put, :] = projected[:, 2 * span :].astype(low)
+            inverse_out[put, : 2 * heads] = jnp.concatenate(inverse_q + inverse_k, axis=1)
 
     rows = 2 * half
-    for place, target in ((0, part_own), (1, part_other)):
-        @pl.loop(0, half // block)
-        def _(index):
-            at = pl.ds(pl.multiple_of(index * block, block), block)
-            put = pl.ds(pl.multiple_of(place * half + index * block, block), block)
+    for place, target in ((0, (part_own,)), (1, (part_a, part_b))):
+        for index in range(half // block):
+            at = slice(index * block, (index + 1) * block)
+            put = slice(place * half + index * block, place * half + (index + 1) * block)
             allowed = allowed_at(member, level, member_row, level_row, put)
             query = queries[put, :]
             masks = heads_of((block, span), heads)
@@ -540,10 +562,10 @@
                 inverses.append(inverse)
                 weights = (raised * inverse).astype(low)
                 outputs = outputs + matmul(weights, jnp.where(wide_masks[head], values[...], jnp.zeros((), low)))
-            inverse_out[put, :] = jnp.concatenate(inverses, axis=1)
+            inverse_out[put, 2 * heads :] = jnp.concatenate(inverses, axis=1)
             outputs = outputs.astype(low)
             heads_out[put, :] = outputs
-            target[at, :] = matmul(outputs, proj[...]).astype(target.dtype)
+            put_part(target, at, matmul(outputs, proj[...]))
 
 
 def attend(own, other, qkv, proj, scale, layout, heads):
@@ -551,44 +573,23 @@
     rows, span = 2 * half, qkv.shape[1] // 3
     return call(
         functools.partial(attend_kernel, heads=heads),
-        [
-            ((half, width), wide),
-            ((half, width), low),
-            ((rows, 3 * span), wide),
-            ((rows, span), low),
-            ((rows, heads), wide),
-        ],
+        [((half, width), wide), ((half // 2, width), low), ((half // 2, width), low)] + [((rows, 4 * span), low), ((rows, 3 * heads), wide)],
         own, other, qkv, proj, scale, *layout,
-        scratch=[pltpu.VMEM((rows, span), low)] * 3,
     )
 
 
 def attend_back_kernel(
-    own, other, raw, inverse_in, qkv, proj, scale, member, level, member_row, level_row,
-    part_own, part_other, grad_out, log_out,
-    queries, keys, values, grads, grad_queries, key_sums_t, value_sums_t, *, heads,
+    own, other, kept, inverse_in, qkv, proj, scale, member, level, member_row, level_row,
+    part_own, part_a, part_b, grad_out, log_out,
+    grads, grad_queries, key_sums_t, value_sums_t, *, heads,
 ):
     half = own.shape[0]
     rows = 2 * half
     span = qkv.shape[1] // 3
-    block = 128
-    for place, source in ((0, own), (1, other)):
-        @pl.loop(0, half // block)
-        def _(index):
-            at = pl.ds(pl.multiple_of(index * block, block), block)
-            put = pl.ds(pl.multiple_of(place * half + index * block, block), block)
-            grads[put, :] = contract_last(source[at, :], proj[...]).astype(low)
-            masks = heads_of((block, span), heads)
-            query, key = raw[put, :span], raw[put, span : 2 * span]
-            query_sums, key_sums = head_sums(query * query, masks), head_sums(key * key, masks)
-            query_scale = by_head(
-                [lax.rsqrt(total + epsilon) * jnp.exp(scale[:, head : head + 1]) for head, total in enumerate(query_sums)], masks
-            )
-            key_scale = by_head([lax.rsqrt(total + epsilon) for total in key_sums], masks)
-            queries[put, :] = (query * query_scale).astype(low)
-            keys[put, :] = (key * key_scale).astype(low)
-            values[put, :] = raw[put, 2 * span :].astype(low)
-
+    block = 256
+    queries, keys, values = (kept.at[:, i * span : (i + 1) * span] for i in range(3))
+    grads[:half, :] = contract_last(own[...], proj[...]).astype(low)
+    grads[half:, :] = contract_last(other[...], proj[...]).astype(low)
     key_sums_t[...] = jnp.zeros_like(key_sums_t)
     value_sums_t[...] = jnp.zeros_like(value_sums_t)
     deep = span // heads
@@ -606,7 +607,7 @@
         for head in range(heads):
             scores = contract_last(jnp.where(masks[head], query, jnp.zeros_like(query)), keys[...])
             raised = jnp.where(allowed, jnp.exp(scores - jnp.exp(scale[:, head : head + 1])), 0.0)
-            weights = raised * inverse_in[put, head : head + 1]
+            weights = raised * inverse_in[put, 2 * heads + head : 2 * heads + head + 1]
             grad_weights = contract_last(jnp.where(masks[head], grad, jnp.zeros_like(grad)), values[...])
             inner = jnp.sum(weights * grad_weights, axis=1, keepdims=True)
             grad_scores = (weights * (grad_weights - inner)).astype(low)
@@ -617,41 +618,37 @@
         grad_queries[put, :] = outputs
 
     log_out[...] = jnp.zeros_like(log_out)
-    raw_keys = key_sums_t[...].T
-    raw_values = value_sums_t[...].T
-    grad_out[:, 2 * span :] = raw_values.astype(low)
-    key_sums = raw_keys
-    for place, target in ((0, part_own), (1, part_other)):
+    grad_keys = key_sums_t[...].T
+    grad_out[:, 2 * span :] = value_sums_t[...].T.astype(low)
+    rises = [jnp.exp(scale[:, head : head + 1]) for head in range(heads)]
+    for place, target in ((0, (part_own,)), (1, (part_a, part_b))):
         for index in range(half // block):
             put = slice(place * half + index * block, place * half + (index + 1) * block)
             at = slice(index * block, (index + 1) * block)
             masks = heads_of((block, span), heads)
-            query, key = raw[put, :span], raw[put, span : 2 * span]
-            grad_query, grad_key = grad_queries[put, :], key_sums[put, :]
-            inverse_q = [lax.rsqrt(total + epsilon) for total in head_sums(query * query, masks)]
-            inverse_k = [lax.rsqrt(total + epsilon) for total in head_sums(key * key, masks)]
+            query, key = queries[put, :].astype(wide), keys[put, :].astype(wide)
+            grad_query, grad_key = grad_queries[put, :], grad_keys[put, :]
+            inverse = [inverse_in[put, i : i + 1] for i in range(2 * heads)]
             dots_q, dots_k = head_sums(query * grad_query, masks), head_sums(key * grad_key, masks)
-            rises = [jnp.exp(scale[:, head : head + 1]) for head in range(heads)]
-            logs = [a * d * i for a, d, i in zip(rises, dots_q, inverse_q)]
-            log_out[...] += jnp.concatenate([jnp.sum(x, axis=0, keepdims=True) for x in logs], axis=1)
-            first = by_head([a * i for a, i in zip(rises, inverse_q)], masks)
-            second = by_head([a * d * i * i * i for a, d, i in zip(rises, dots_q, inverse_q)], masks)
+            log_out[...] += jnp.concatenate([jnp.sum(x, axis=0, keepdims=True) for x in dots_q], axis=1)
+            first = by_head([a * i for a, i in zip(rises, inverse[:heads])], masks)
+            second = by_head([d * i / a for a, d, i in zip(rises, dots_q, inverse[:heads])], masks)
             grad_out[put, :span] = (grad_query * first - query * second).astype(low)
-            first = by_head(inverse_k, masks)
-            second = by_head([d * i * i * i for d, i in zip(dots_k, inverse_k)], masks)
+            first = by_head(inverse[heads:], masks)
+            second = by_head([d * i for d, i in zip(dots_k, inverse[heads:])], masks)
             grad_out[put, span : 2 * span] = (grad_key * first - key * second).astype(low)
-            target[at, :] = contract_last(grad_out[put, :], qkv[...]).astype(target.dtype)
-
-
-def attend_back(own, other, raw, inverse, qkv, proj, scale, layout, heads):
+            put_part(target, at, contract_last(grad_out[put, :], qkv[...]))
+
+
+def attend_back(own, other, kept, qkv, proj, scale, layout, heads):
     half, width = own.shape
     rows, span = 2 * half, qkv.shape[1] // 3
     return call(
         functools.partial(attend_back_kernel, heads=heads),
-        [((half, width), wide), ((half, width), low), ((rows, 3 * span), low), ((1, heads), wide)],
-        own, other, raw, inverse, qkv, proj, scale, *layout,
-        scratch=[pltpu.VMEM((rows, span), low)] * 4
-        + [pltpu.VMEM((rows, span), wide), pltpu.VMEM((span, rows), wide), pltpu.VMEM((span, rows), wide)],
+        [((half, width), wide), ((half // 2, width), low), ((half // 2, width), low), ((rows, 3 * span), low), ((1, heads), wide)],
+        own, other, *kept, qkv, proj, scale, *layout,
+        scratch=[pltpu.VMEM((rows, span), low), pltpu.VMEM((rows, span), wide)]
+        + [pltpu.VMEM((span, rows), wide), pltpu.VMEM((span, rows), wide)],
     )
 
 
@@ -729,27 +726,18 @@
     )
 
 
-def gradient_kernel(*refs):
+def gradient_kernel(*refs, spans):
     kept, sent = refs[-2:]
     rest = refs[:-2]
     half = kept.shape[1]
-    block = 256
     first = 0
-    for factor, own, other in [rest[i : i + 3] for i in range(0, len(rest), 3)]:
+    for (begin, end), factor, own, other in [(spans[i // 3], *rest[i : i + 3]) for i in range(0, len(rest), 3)]:
         rows = own.shape[0]
-        base = first
-
-        @pl.loop(0, factor.shape[1] // block)
-        def _(index):
-            at = pl.ds(pl.multiple_of(index * block, block), block)
-            put = pl.ds(pl.multiple_of(base + index * block, block), block)
-            turned = factor[:, at].T
-            kept[put, :] = matmul(turned[:, :rows], own[:, :half]) + matmul(turned[:, rows:], other[:, :half])
-            sent[put, :] = (
-                matmul(turned[:, :rows], own[:, half:]) + matmul(turned[:, rows:], other[:, half:])
-            ).astype(low)
-
-        first += factor.shape[1]
+        put = slice(first, first + end - begin)
+        turned = factor[:, begin:end].T
+        kept[put, :] = (matmul(turned[:, :rows], own[:, :half]) + matmul(turned[:, rows:], other[:, :half])).astype(low)
+        sent[put, :] = (matmul(turned[:, :rows], own[:, half:]) + matmul(turned[:, rows:], other[:, half:])).astype(low)
+        first += end - begin
 
 
 def silu_of(value):
@@ -841,10 +829,14 @@
 
 
 def gradients(*pairs):
-    height = sum(left.shape[1] for left, _ in pairs)
+    pairs = [(left if isinstance(left, tuple) else (left, 0, left.shape[1]), sides) for left, sides in pairs]
+    spans = [(first, last) for (_, first, last), _ in pairs]
+    height = sum(last - first for first, last in spans)
     half = pairs[0][1][0].shape[1] // 2
-    operands = [value for left, sides in pairs for value in (left, *sides)]
-    return call(gradient_kernel, [((height, half), wide), ((height, half), low)], *operands)
+    operands = [value for (left, _, _), sides in pairs for value in (left, *sides)]
+    return call(
+        functools.partial(gradient_kernel, spans=spans), [((height, half), low), ((height, half), low)], *operands
+    )
 
 
 def on_device(
@@ -878,61 +870,68 @@
     def along(block):
         return lax.all_gather(block, "dp", axis=0, tiled=True, axis_index_groups=slow_groups)
 
+    def ring(block, marker=None):
+        block = block if marker is None else tie(block, marker)
+        return lax.ppermute(block, "dp", [(i, (i + 2) % 8) for i in range(8)])
+
+    def whole(own, hops, there, other, first, parts):
+        size = own.shape[0]
+        sources = [(0, 0), (1, 0), (2, 0), (3, 0), (4, first)] + [(5, i * size) for i in range(3)]
+        return join([own, *hops, other, there], sources, parts)
+
+    mix_parts = [(depth, 3 * span // 128, 0), (w_proj.shape[1], 1, 1)]
+    fc1_parts = [(depth, w_fc1.shape[2] // 128, 0)]
+    fc2_parts = [(w_fc2.shape[1], 1, 1)]
     if near:
         mix_a = along(pack_mix(flat[0], w_proj, 0))
-
-    if near:
-        known = classes
+        fc1_a, mix_c, fc1_d, fc2_e = (
+            along(block) for block in (pack_fc1(w_fc1, 0), pack_mix(flat[1], w_proj, 1), pack_fc1(w_fc1, 1), w_fc2[1])
+        )
+
+    def gather_classes(known):
         for offset in (1, 2, 4):
             known = jnp.concatenate([known, swap(known, "dp", offset)], axis=0)
+        return known
+
+    if near:
+        known = gather_classes(classes)
         index = jnp.arange(groups, dtype=jnp.int32)
         found = (index[:, None] ^ index[None, :]) == lax.axis_index("dp")
         known = jnp.sum(jnp.where(found[:, :, None], known[None], 0), axis=1)
     else:
         known = lax.all_gather(classes, "dp", axis=0, tiled=True)
     all_classes = known.reshape(-1)
-
-    def whole(own, hops, there, other, first, parts):
-        size = own.shape[0]
-        sources = [(0, 0), (1, 0), (2, 0), (3, 0), (4, first)] + [(5, i * size) for i in range(3)]
-        return join([own, *hops, other, there], sources, parts)
-
-    mix_parts = [(depth, 3 * span // 128, 0), (w_proj.shape[1], 1, 1)]
-    fc1_parts = [(depth, w_fc1.shape[2] // 128, 0)]
-    fc2_parts = [(w_fc2.shape[1], 1, 1)]
+    to_slots, to_rows = route(dest, rows)
+    leaving = [matmul(to_slots, value).astype(low).reshape(groups, slots, width) for value in (tokens, out_grad)]
+    arrived = exchange(jnp.where(all_classes[0] >= 0, jnp.concatenate(leaving, axis=1), 0), groups)
+
+    def sum_pack(part):
+        part = part + swap(part, "shard", 1)
+        return part + swap(part, "shard", 2)
+
+    cond, part = condition(all_classes[:, None], class_table, w_ada)
+    part = sum_pack(part)
     if near:
-        fc1_a = tie(pack_fc1(w_fc1, 0), all_classes)
-        fc2_b = tie(w_fc2[0], all_classes)
-        hops_a = straight(fc1_a)
-        other_ab = swap(stack([fc1_a, fc2_b]), "dp", 1)
-        mix_c, fc1_d, fc2_e = (
-            along(tie(block, all_classes)) for block in (pack_mix(flat[1], w_proj, 1), pack_fc1(w_fc1, 1), w_fc2[1])
-        )
-
-    to_slots, to_rows = route(dest, rows)
-    arrived = exchange(matmul(to_slots, tokens).astype(low).reshape(groups, slots, width), groups)
-    packed = unpack(to_rows, arrived.reshape(rows, width), order)
-    carried = jnp.concatenate([packed, swap(packed, "shard", 2)], axis=0).astype(wide)
-
-    cond, part = condition(all_classes[:, None], class_table, w_ada)
-    part = part + swap(part, "shard", 1)
-    part = part + swap(part, "shard", 2)
+        there_m = swap(tie(mix_a, part), "dp", 1)
     part = jnp.swapaxes(part.reshape(layers, groups, items, columns), 0, 1)
     upper = lax.reduce_precision(part, 8, 7)
     halves = jnp.stack([upper.astype(low), (part - upper).astype(low)], axis=1)
-    halves = exchange(tie(halves.reshape(groups, 2 * layers * items, columns), packed), groups)
+    halves = exchange(halves.reshape(groups, 2 * layers * items, columns), groups)
+    packed = unpack(to_rows, arrived[:, :slots].reshape(rows, width), order)
+    carried = jnp.concatenate([packed, swap(packed, "shard", 2)], axis=0).astype(wide)
+    grad_packed = unpack(to_rows, arrived[:, slots:].reshape(rows, width), order)
     modulation = spread(halves, order, layers, items, width)
     if near:
-        modulation = tie(modulation, *hops_a, other_ab)
-        there_m = swap(mix_a, "dp", 1)
-        there_a = swap(stack(hops_a), "dp", 1)
-        hops_b = straight(tie(fc2_b, modulation))
-
-    def arrive(marker):
-        grads_out = matmul(to_slots, tie(out_grad, marker)).astype(low).reshape(groups, slots, width)
-        grads_out = exchange(grads_out, groups)
-        grad_packed = unpack(to_rows, grads_out.reshape(rows, width), order)
-        return jnp.concatenate([grad_packed, swap(grad_packed, "shard", 2)], axis=0).astype(wide)
+        own_b = tie(w_fc2[0], modulation)
+        hops_b = straight(own_b)
+        other_b = swap(own_b, "dp", 1)
+    def across_cores(value):
+        return swap(value, "shard", 1)
+
+    def sum_pack_rows(part_own, parts_other, *meanwhile):
+        here = gather_cores(part_own, parts_other)
+        there = swap(here, "shard", 2)
+        return here, there
 
     place = jnp.concatenate(
         [(me ^ offset) * rows + jnp.arange(rows, dtype=jnp.int32) for offset in (0, 2, 1, 3)]
@@ -953,50 +952,49 @@
             proj_full = lax.all_gather(w_proj[layer], "dp", axis=1, tiled=True)
             fc1_full = lax.all_gather(w_fc1[layer], "dp", axis=0, tiled=True)
             fc2_full = lax.all_gather(w_fc2[layer], "dp", axis=1, tiled=True)
-        elif layer == 0:
-            qkv_full, proj_full = join_pair(mix_a, there_m, order, mix_parts)
-        else:
-            qkv_full, proj_full = join_pair(mix_c, there_c, order, mix_parts)
-        first = (first_low, swap(first_low, "shard", 1))
         if near and layer == 0:
-            first = (first[0], tie(first[1], *hops_b))
-            there_b = swap(stack(hops_b), "dp", 1)
-        part_own, part_other, raw, heads_low, inverse = attend(
+            there_a = swap(tie(fc1_a, first_low), "dp", 1)
+        elif near:
+            there_d = swap(tie(fc1_d, first_low), "dp", 1)
+        first = (first_low, across_cores(first_low))
+        if near:
+            mix, mix_there = (mix_c, there_c) if layer else (mix_a, there_m)
+            qkv_full, proj_full = join_pair(mix, tie(mix_there, first_low), order, mix_parts)
+        part_own, part_a, part_b, *kept = attend(
             *first, qkv_full, proj_full, scales[layer], layout, heads_here
         )
-        here = gather_cores(part_own, part_other)
-        if layer == 0:
-            grad_carried = arrive(here)
+        if near and layer == 0:
+            part_a = tie(part_a, *hops_b, other_b)
+            there_b = swap(tie(stack(hops_b), part_a), "dp", 1)
+        elif near:
+            there_e = swap(tie(fc2_e, part_a), "dp", 1)
+        if layer == 1:
+            part_a = tie(part_a, grad_there)
+        here, there = sum_pack_rows(part_own, (part_a, part_b))
         if near:
-            here = tie(here, there_a if layer == 0 else there_d)
-        there = swap(here, "shard", 2)
-        if near and layer == 1:
-            there_e = swap(tie(fc2_e, here), "dp", 1)
+            there = tie(there, there_d if layer else there_a)
         attended = (here, there)
         middle, second_low = step(carried, *attended, mods[layer], mods[layer], here_member, 0, 3, 5)
-        second = (second_low, swap(second_low, "shard", 1))
+        second = (second_low, across_cores(second_low))
+        if near:
+            fc1, fc1_there = (fc1_d, there_d) if layer else (fc1_a, there_a)
+            (fc1_full,) = join_pair(fc1, tie(fc1_there, second_low), order, fc1_parts)
+            if layer == 0:
+                (fc2_full,) = whole(own_b, hops_b, tie(there_b, second_low), other_b, 0, fc2_parts)
+            else:
+                (fc2_full,) = join_pair(fc2_e, tie(there_e, second_low), order, fc2_parts)
+        weights[layer] = (qkv_full, proj_full, fc1_full, fc2_full)
+        part_own, part_a, part_b, slope, activated = mlp(*second, fc1_full, fc2_full)
         if near and layer == 0:
-            (fc1_full,) = whole(fc1_a, hops_a, there_a, other_ab, 0, fc1_parts)
-            (fc2_full,) = whole(fc2_b, hops_b, there_b, other_ab, fc1_a.shape[0], fc2_parts)
-        elif near:
-            (fc1_full,) = join_pair(fc1_d, there_d, order, fc1_parts)
-            (fc2_full,) = join_pair(fc2_e, there_e, order, fc2_parts)
-        weights[layer] = (qkv_full, proj_full, fc1_full, fc2_full)
-        part_own, part_other, hidden, activated = mlp(*second, fc1_full, fc2_full)
-        here = gather_cores(part_own, part_other)
-        there = swap(here, "shard", 2)
-        if near and layer == 0:
-            there_c = swap(tie(mix_c, here), "dp", 1)
-        if layer == 0:
-            there, grad_carried = lax.optimization_barrier((there, grad_carried))
-        if near and layer == 0:
-            there_d = swap(tie(fc1_d, there), "dp", 1)
-        branch = (here, there)
-        saved.append((carried, middle, first, raw, heads_low, inverse, attended, second, hidden, activated, branch))
+            there_c = swap(tie(mix_c, part_a), "dp", 1)
+        branch = sum_pack_rows(part_own, (part_a, part_b))
+        saved.append((carried, middle, first, kept, attended, second, slope, activated, branch))
         if layer + 1 < layers:
+            grad_there = swap(tie(grad_packed, branch[1]), "shard", 2)
             carried, first_low = step(middle, *branch, mods[layer], mods[layer + 1], here_member, 1, 2, 4)
         else:
             carried = leave(middle, *branch, mods[layer], here_member, 1)
+    grad_carried = jnp.concatenate([grad_packed, grad_there], axis=0).astype(wide)
 
     mixed_out = repack(to_rows, carried, order).reshape(groups, slots, width)
 
@@ -1011,22 +1009,25 @@
     mod_sums[-1][1] = (sums, 0)
     for layer in range(layers - 1, -1, -1):
         qkv_full, proj_full, fc1_full, fc2_full = weights[layer]
-        carried_in, middle, first, raw, heads_low, inverse, attended, second, hidden, activated, branch = saved[layer]
-        grad_branch = (grad_low, swap(grad_low, "shard", 1))
+        carried_in, middle, first, kept, attended, second, slope, activated, branch = saved[layer]
+        other = across_cores(grad_low)
+        if near and layer == 0:
+            other = tie(other, layer_sums[1][1].arrived)
+            other = layer_sums[1][1].fold(True, other)
+        grad_branch = (grad_low, other)
         if near:
             terms = gradients((activated, grad_branch))
             sums_fc2 = Sums(*terms)
-            hidden = tie(hidden, *terms)
-        part_own, part_other, grad_hidden = mlp_back(*grad_branch, hidden, fc1_full, fc2_full)
-        here = gather_cores(part_own, part_other)
-        there = swap(here, "shard", 2)
+            slope = tie(slope, *terms)
+        part_own, part_a, part_b, grad_hidden = mlp_back(*grad_branch, slope, fc1_full, fc2_full)
+        if near and layer == 0:
+            part_a = tie(part_a, layer_sums[1][0].arrived)
+            part_a = layer_sums[1][0].fold(True, part_a)
+        here, there = sum_pack_rows(part_own, (part_a, part_b))
         if near:
             terms = gradients((tie(grad_hidden, here), second))
-            there = tie(there, *terms, *([mixed_out] if layer else []))
             sums_fc1 = Sums(*terms)
-            before = sums_fc2 if layer else layer_sums[1][0]
-            there = tie(there, before.arrived)
-            before.fold(True, there)
+            there = tie(there, *terms, *([layer_sums[1][2].blocks] if layer == 0 else [mixed_out]))
         else:
             sums_fc2 = WholeSums(gradient_blocks(order, (activated, grad_branch)))
             sums_fc1 = WholeSums(gradient_blocks(order, (grad_hidden, second)))
@@ -1034,22 +1035,31 @@
             middle, here, there, grad_carried, mods[layer], here_member, choose, 3, (mods[layer], 0, *attended)
         )
         mod_sums[layer][3], mod_sums[layer][5], mod_sums[layer][0] = ((sums, i * width) for i in range(3))
-        grad_attended = (grad_low, swap(grad_low, "shard", 1))
-        part_own, part_other, grad_projected, scale_grads[layer] = attend_back(
-            *grad_attended, raw, inverse, qkv_full, proj_full, scales[layer], layout, heads_here
+        other = across_cores(grad_low)
+        if near and layer == 0:
+            other = tie(other, sums_fc2.arrived, layer_sums[1][1].blocks)
+            other = sums_fc2.fold(True, other)
+        grad_attended = (grad_low, other)
+        part_own, part_a, part_b, grad_projected, scale_grads[layer] = attend_back(
+            *grad_attended, kept, qkv_full, proj_full, scales[layer], layout, heads_here
         )
-        here = gather_cores(part_own, part_other)
-        there = swap(here, "shard", 2)
+        if near and layer == 0:
+            terms = gradients(((kept[0], 3 * span, 4 * span), grad_attended), (grad_projected, first))
+            part_a = tie(part_a, *terms)
+        elif near:
+            part_a = tie(part_a, sums_fc2.arrived)
+            part_a = sums_fc2.fold(True, part_a)
+        here, there = sum_pack_rows(part_own, (part_a, part_b))
         if near:
-            terms = gradients((tie(heads_low, here), grad_attended), (grad_projected, first))
+            if layer > 0:
+                terms = gradients(((tie(kept[0], here), 3 * span, 4 * span), grad_attended), (grad_projected, first))
             there = tie(there, *terms)
+            if layer == 0:
+                there = tie(there, sums_fc1.arrived, layer_sums[1][0].blocks)
+                there = sums_fc1.fold(True, there)
             sums_attn = Sums(*terms)
-            before = sums_fc1 if layer else sums_fc2
-            there = tie(there, before.arrived)
-            before.fold(True, there)
         else:
-            blocks_attn = gradient_blocks(order, (heads_low, grad_attended), (grad_projected, first))
-            sums_attn = WholeSums(blocks_attn)
+            sums_attn = WholeSums(gradient_blocks(order, (kept[0][:, 3 * span :], grad_attended), (grad_projected, first)))
         if layer > 0:
             grad_carried, grad_low, sums = step_back(
                 carried_in, here, there, grad_middle, mods[layer], here_member, choose, 2, (mods[layer - 1], 1, *saved[layer - 1][-1])
@@ -1060,7 +1070,7 @@
         mod_sums[layer][2], mod_sums[layer][4] = (sums, 0), (sums, width)
         layer_sums[layer] = (sums_attn, sums_fc1, sums_fc2)
     if near:
-        layer_sums[0][1].fold(True, grad_carried)
+        grad_carried = tie(grad_carried, layer_sums[0][0].arrived)
         layer_sums[0][0].fold(False, grad_carried)
 
     grads_back = repack(to_rows, grad_carried, order).reshape(groups, slots, width)
@@ -1094,7 +1104,7 @@
     spanned = w_proj.shape[1]
     layer_grads = []
     for layer in range(layers):
-        attn, fc1, fc2 = (sums.total(grad_carried) for sums in layer_sums[layer])
+        attn, fc1, fc2 = (sums.total(scale_grad) for sums in layer_sums[layer])
         layer_grads.append((attn[spanned:].T.reshape(w_qkv.shape[1:]), attn[:spanned], fc1.T, fc2))
     qkv_grad, proj_grad, fc1_grad, fc2_grad = (
         jnp.stack([layer_grads[layer][i] for layer in range(layers)]) for i in range(4)

time: 568 us -> 514 us (0.905)
  Pallas kernels: 138 us -> 101 us
  waiting for transfers between devices: 235 us -> 207 us
  local copies, waits for them, and re-layouts: 67.2 us -> 86.1 us
  other arithmetic: 19 us -> 12.2 us
    ppermute x6 -> x3, waiting for transfers between devices: 38.5 us -> 0.01 us  [straight(): lax.ppermute(block, 'dp', [(i, (i + 2 * back) % 8) for i in range(8)])]
    pallas_call x54 -> x60, Pallas kernels: 138 us -> 101 us  [call(): pl.pallas_call(kernel, out_shape=[jax.ShapeDtypeStruct(shape, kind) for s...]
    ppermute x49 -> x57, waiting for transfers between devices: 187 us -> 160 us  [swap(): return lax.ppermute(value, axis, [(i, i ^ offset) for i in range(size)])]
    all_to_all x4 -> x3, waiting for transfers between devices: 9.02 us -> 35.5 us  [exchange(): return lax.all_to_all(value, 'dp', split_axis=0, concat_axis=0, tiled=True)]
    unnamed x334 -> x350, local copies, waits for them, and re-layouts: 52.8 us -> 74.6 us
    all_gather x4 -> x5, waiting for transfers between devices: 0.03 us -> 11.6 us  [along(): lax.all_gather(block, 'dp', axis=0, tiled=True, axis_index_groups=slow_gr...]
    all_gather x4 -> x5, starting transfers between devices: 11.5 us -> 0.2 us  [along(): lax.all_gather(block, 'dp', axis=0, tiled=True, axis_index_groups=slow_gr...]
    ppermute x49 -> x57, starting transfers between devices: 41 us -> 51.6 us  [swap(): return lax.ppermute(value, axis, [(i, i ^ offset) for i in range(size)])]
  transfers between devices with their start and end apart: 71 -> 76, of which waited for: 39 -> 43; matrix products, arithmetic and copies ran while one was open for 6% -> 5% of each run, Pallas kernels for 22% -> 18%
where the time goes in v3:
time: 514 us; the launch traced here: 508 us
  waiting for transfers between devices  207 us (40%)
  Pallas kernels  101 us (20%)
  local copies, waits for them, and re-layouts  86.1 us (17%)
  starting transfers between devices  81.9 us (16%)
  between operations  16.5 us (3%)
  other arithmetic  12.2 us (2%)
    ppermute x57, waiting for transfers between devices, swap(): return lax.ppermute(value, axis, [(i, i ^ offset) for i in range(size)])  160 us
    pallas_call x60, Pallas kernels, call(): pl.pallas_call(kernel, out_shape=[jax.ShapeDtypeStruct(shape, kind) for s...  101 us
    unnamed x350, local copies, waits for them, and re-layouts  74.6 us
    ppermute x57, starting transfers between devices, swap(): return lax.ppermute(value, axis, [(i, i ^ offset) for i in range(size)])  51.6 us
    all_to_all x3, waiting for transfers between devices, exchange(): return lax.all_to_all(value, 'dp', split_axis=0, concat_axis=0, tiled=True)  35.5 us
    all_to_all x3, starting transfers between devices, exchange(): return lax.all_to_all(value, 'dp', split_axis=0, concat_axis=0, tiled=True)  15 us
    ppermute x3, starting transfers between devices, straight(): lax.ppermute(block, 'dp', [(i, (i + 2 * back) % 8) for i in range(8)])  11.9 us
    all_gather x5, waiting for transfers between devices, along(): lax.all_gather(block, 'dp', axis=0, tiled=True, axis_index_groups=slow_gr...  11.6 us
  transfers between devices with their start and end apart: 76, of which 43 were waited for; matrix products, arithmetic and copies ran while one was open for 5% of the time, Pallas kernels for 18%

profile of v3, /device:TPU:0, one launch (start us, length us, event | category | flops | bytes accessed | tf_op | source)
XLA Modules:
  0.0 507.6 jit_solution(18144509436846718405)
XLA Ops:
  12.4 3.0 collective-permute-start
  21.1 2.7 collective-permute-start.2
  23.8 2.2 collective-permute-done.2
  27.4 5.6 %all-to-all-start = ((bf16[8,32,1024]{2,1,0:T(8,128)(2,1)}), bf16[8,32,1024]{2,1,0:T(8,128)(2,1)S(1)}, u32[]{:S(2)}, u32[]{:S(2)}) async-start(bf16[8,32,1024]{2,1,0:T(8,128)(2,1)} %maximum_select_fusion), calls=%async_computation | async-start | bytes 1048576 | tf_op jit(solution)/shard_map/all_to_all | solution.py:342
  36.9 5.5 %collective-permute-done.5 = f32[2,32,768]{2,1,0:T(8,128)S(1)} collective-permute-done((f32[2,32,768]{2,1,0:T(8,128)S(1)}, f32[2,32,768]{2,1,0:T(8,128)S(1)}, u32[]{:S(2)}, u32[]{:S(2)}) %collective-permute-start.5) | collective-permute-done | bytes 196640 | tf_op jit(solution)/shard_map/ppermute | solution.py:32
  43.4 9.2 %all-to-all-done = bf16[8,32,1024]{2,1,0:T(8,128)(2,1)S(1)} async-done(((bf16[8,32,1024]{2,1,0:T(8,128)(2,1)}), bf16[8,32,1024]{2,1,0:T(8,128)(2,1)S(1)}, u32[]{:S(2)}, u32[]{:S(2)}) %all-to-all-start) | async-done | bytes 524320 | tf_op jit(solution)/shard_map/all_to_all | solution.py:342
  52.6 3.5 all-to-all-start.1
  61.5 2.6 all-to-all-done.1.arrived
  69.2 3.3 collective-permute-start.10
  72.5 11.6 %all-gather.9.cloned.1.call-done.here = bf16[4096,128]{1,0:T(8,128)(2,1)} async-done(((bf16[1024,128]{1,0:T(8,128)(2,1)}), bf16[4096,128]{1,0:T(8,128)(2,1)}) %all-gather.9.cloned.1.call-update) | async-done | bytes 1048592 | tf_op jit(solution)/shard_map/all_gather | solution.py:871
  84.1 8.6 %collective-permute-start.8 = (bf16[1024,128]{1,0:T(8,128)(2,1)}, bf16[1024,128]{1,0:T(8,128)(2,1)}, u32[]{:S(2)}, u32[]{:S(2)}) collective-permute-start(bf16[1024,128]{1,0:T(8,128)(2,1)} %get-tuple-element.147.refs_0_), channel_id=1, source_target_pairs={{0,8},{4,12},{8,16},{12,20},{16,24},{20,28},{24,0},{28,4},{1,9},{5... | collective-permute-start | bytes 786440 | tf_op jit(solution)/shard_map/ppermute | solution.py:55
  93.7 2.2 collective-permute-start.15
  101.8 4.2 shard_map.202
  112.2 8.0 %collective-permute-done.15.there = bf16[4096,128]{1,0:T(8,128)(2,1)S(1)} collective-permute-done((bf16[4096,128]{1,0:T(8,128)(2,1)}, bf16[4096,128]{1,0:T(8,128)(2,1)S(1)}, u32[]{:S(2)}, u32[]{:S(2)}) %collective-permute-start.15) | collective-permute-done | bytes 1048608 | tf_op jit(solution)/shard_map/ppermute | solution.py:32
  120.1 3.2 collective-permute-done.14.there.branch_there
  125.9 10.2 %collective-permute-done.17.refs_5_ = bf16[3072,128]{1,0:T(8,128)(2,1)S(1)} collective-permute-done((bf16[3072,128]{1,0:T(8,128)(2,1)S(1)}, bf16[3072,128]{1,0:T(8,128)(2,1)S(1)}, u32[]{:S(2)}, u32[]{:S(2)}) %collective-permute-start.17) | collective-permute-done | bytes 786464 | tf_op jit(solution)/shard_map/ppermute | solution.py:32
  139.2 3.8 shard_map.209
  152.7 12.1 %collective-permute-done.20.there.branch_there = bf16[256,1024]{1,0:T(8,128)(2,1)S(1)} collective-permute-done((bf16[256,1024]{1,0:T(8,128)(2,1)S(1)}, bf16[256,1024]{1,0:T(8,128)(2,1)S(1)}, u32[]{:S(2)}, u32[]{:S(2)}) %collective-permute-start.20) | collective-permute-done | bytes 524320 | tf_op jit(solution)/shard_map/ppermute | solution.py:32
  164.8 2.4 shard_map.211
  176.5 6.9 %shard_map.214 = (f32[256,1024]{1,0:T(8,128)S(1)}, bf16[128,1024]{1,0:T(8,128)(2,1)}, bf16[128,1024]{1,0:T(8,128)(2,1)}, bf16[512,1024]{1,0:T(8,128)(2,1)S(1)}, f32[512,12]{1,0:T(8,128)S(1)}) custom-call(bf16[256,1024]{1,0:T(8,128)(2,1)} %get-tuple-element.161.own.refs_4_, bf16[256,1024]{1,0:T(8,128)(2,1)} %collective-permute-done.21.other.refs_5_, ...), custom_call_target="tpu_custom_call" | custom-call | flops 1 | bytes 1 | tf_op jit(solution)/shard_map/pallas_call | solution.py:362
  193.0 5.3 %collective-permute-done.27.there = bf16[4096,128]{1,0:T(8,128)(2,1)} collective-permute-done((bf16[4096,128]{1,0:T(8,128)(2,1)}, bf16[4096,128]{1,0:T(8,128)(2,1)}, u32[]{:S(2)}, u32[]{:S(2)}) %collective-permute-start.27) | collective-permute-done | bytes 1048608 | tf_op jit(solution)/shard_map/ppermute | solution.py:32
  198.3 6.6 %collective-permute-done.26.there.branch_there = bf16[256,1024]{1,0:T(8,128)(2,1)S(1)} collective-permute-done((bf16[256,1024]{1,0:T(8,128)(2,1)S(1)}, bf16[256,1024]{1,0:T(8,128)(2,1)S(1)}, u32[]{:S(2)}, u32[]{:S(2)}) %collective-permute-start.26) | collective-permute-done | bytes 524320 | tf_op jit(solution)/shard_map/ppermute | solution.py:32
  208.3 11.6 %collective-permute-done.29.there = bf16[4096,128]{1,0:T(8,128)(2,1)S(1)} collective-permute-done((bf16[4096,128]{1,0:T(8,128)(2,1)S(1)}, bf16[4096,128]{1,0:T(8,128)(2,1)S(1)}, u32[]{:S(2)}, u32[]{:S(2)}) %collective-permute-start.29) | collective-permute-done | bytes 1048608 | tf_op jit(solution)/shard_map/ppermute | solution.py:32
  221.1 3.0 shard_map.221
  228.0 12.2 %collective-permute-done.32.there = bf16[256,1024]{1,0:T(8,128)(2,1)S(1)} collective-permute-done((bf16[256,1024]{1,0:T(8,128)(2,1)S(1)}, bf16[256,1024]{1,0:T(8,128)(2,1)S(1)}, u32[]{:S(2)}, u32[]{:S(2)}) %collective-permute-start.32) | collective-permute-done | bytes 524320 | tf_op jit(solution)/shard_map/ppermute | solution.py:32
  245.1 2.4 shard_map.227
  257.0 6.6 %collective-permute-done.36.there = bf16[256,1024]{1,0:T(8,128)(2,1)S(1)} collective-permute-done((bf16[256,1024]{1,0:T(8,128)(2,1)S(1)}, bf16[256,1024]{1,0:T(8,128)(2,1)S(1)}, u32[]{:S(2)}, u32[]{:S(2)}) %collective-permute-start.36) | collective-permute-done | bytes 524320 | tf_op jit(solution)/shard_map/ppermute | solution.py:32
  267.6 8.0 %shard_map.231 = (f32[256,1024]{1,0:T(8,128)S(1)}, bf16[128,1024]{1,0:T(8,128)(2,1)S(1)}, bf16[128,1024]{1,0:T(8,128)(2,1)S(1)}, bf16[512,768]{1,0:T(8,128)(2,1)S(1)}, f32[1,4]{1,0:T(1,128)S(1)}) custom-call(bf16[256,1024]{1,0:T(8,128)(2,1)S(1)} %get-tuple-element.195.own.refs_1_, bf16[256,1024]{1,0:T(8,128)(2,1)S(1)} %collective-permute-done.37.other.refs_2_, ...), custom_call_target="tpu_custom_call" | custom-call | flops 1 | bytes 1 | tf_op jit(solution)/shard_map/pallas_call | solution.py:362
  287.6 2.5 shard_map.234
  292.1 6.1 %collective-permute-done.41.there = bf16[256,1024]{1,0:T(8,128)(2,1)S(1)} collective-permute-done((bf16[256,1024]{1,0:T(8,128)(2,1)S(1)}, bf16[256,1024]{1,0:T(8,128)(2,1)S(1)}, u32[]{:S(2)}, u32[]{:S(2)}) %collective-permute-start.41) | collective-permute-done | bytes 524320 | tf_op jit(solution)/shard_map/ppermute | solution.py:32
  302.9 7.1 %collective-permute-done.43.arrived = bf16[1024,512]{1,0:T(8,128)(2,1)S(1)} collective-permute-done((bf16[1024,512]{1,0:T(8,128)(2,1)}, bf16[1024,512]{1,0:T(8,128)(2,1)S(1)}, u32[]{:S(2)}, u32[]{:S(2)}) %collective-permute-start.43) | collective-permute-done | bytes 1048608 | tf_op jit(solution)/shard_map/ppermute | solution.py:32
  321.5 2.4 shard_map.238
  327.3 9.2 %collective-permute-done.44.arrived = bf16[1024,512]{1,0:T(8,128)(2,1)S(1)} collective-permute-done((bf16[1024,512]{1,0:T(8,128)(2,1)}, bf16[1024,512]{1,0:T(8,128)(2,1)S(1)}, u32[]{:S(2)}, u32[]{:S(2)}) %collective-permute-start.44) | collective-permute-done | bytes 1048608 | tf_op jit(solution)/shard_map/ppermute | solution.py:32
  348.3 2.3 shard_map.241
  351.5 4.6 collective-permute-done.47.there
  357.4 3.1 shard_map.242
  364.6 5.1 %collective-permute-done.49.arrived = bf16[1024,512]{1,0:T(8,128)(2,1)} collective-permute-done((bf16[1024,512]{1,0:T(8,128)(2,1)}, bf16[1024,512]{1,0:T(8,128)(2,1)}, u32[]{:S(2)}, u32[]{:S(2)}) %collective-permute-start.49) | collective-permute-done | bytes 1048608 | tf_op jit(solution)/shard_map/ppermute | solution.py:32
  371.7 2.5 shard_map.243
  379.5 8.7 %shard_map.244 = (f32[256,1024]{1,0:T(8,128)S(1)}, bf16[128,1024]{1,0:T(8,128)(2,1)}, bf16[128,1024]{1,0:T(8,128)(2,1)}, bf16[512,768]{1,0:T(8,128)(2,1)S(1)}, f32[1,4]{1,0:T(1,128)S(1)}) custom-call(bf16[256,1024]{1,0:T(8,128)(2,1)S(1)} %copy-done.53, bf16[256,1024]{1,0:T(8,128)(2,1)S(1)} %copy-done.56, bf16[512,1024]{1,0:T(8,128)(2,1)S(1)} %copy-done.32, ...), custom_call_target="tpu_custom_call" | custom-call | flops 1 | bytes 1 | tf_op jit(solution)/shard_map/pallas_call | solution.py:362
  389.2 2.2 shard_map.245
  402.5 9.4 %collective-permute-done.52.there = bf16[256,1024]{1,0:T(8,128)(2,1)S(1)} collective-permute-done((bf16[256,1024]{1,0:T(8,128)(2,1)S(1)}, bf16[256,1024]{1,0:T(8,128)(2,1)S(1)}, u32[]{:S(2)}, u32[]{:S(2)}) %collective-permute-start.52) | collective-permute-done | bytes 524320 | tf_op jit(solution)/shard_map/ppermute | solution.py:32
  413.9 2.4 shard_map.247
  426.8 5.9 %all-to-all-start.2 = ((bf16[8,38,1024]{2,1,0:T(8,128)(2,1)}), bf16[8,38,1024]{2,1,0:T(8,128)(2,1)}, u32[]{:S(2)}, u32[]{:S(2)}) async-start(bf16[8,38,1024]{2,1,0:T(8,128)(2,1)} %pad_maximum_fusion.1), calls=%async_computation.5 | async-start | bytes 1310720 | tf_op jit(solution)/shard_map/all_to_all | solution.py:342
  433.3 3.0 convert_add_fusion
  436.4 23.6 %all-to-all-done.2 = bf16[8,38,1024]{2,1,0:T(8,128)(2,1)} async-done(((bf16[8,38,1024]{2,1,0:T(8,128)(2,1)}), bf16[8,38,1024]{2,1,0:T(8,128)(2,1)}, u32[]{:S(2)}, u32[]{:S(2)}) %all-to-all-start.2) | async-done | bytes 622624 | tf_op jit(solution)/shard_map/all_to_all | solution.py:342
  469.3 3.8 collective-permute-start.58
  474.2 11.9 %collective-permute-done.58 = f32[40,256]{1,0:T(8,128)S(1)} collective-permute-done((f32[40,256]{1,0:T(8,128)S(1)}, f32[40,256]{1,0:T(8,128)S(1)}, u32[]{:S(2)}, u32[]{:S(2)}) %collective-permute-start.58) | collective-permute-done | bytes 40992 | tf_op jit(solution)/shard_map/ppermute | solution.py:32
  488.3 2.7 collective-permute-done.59
  (613 shorter events, 206.0 us)
Async XLA Ops:
  7.2 52.1 %all-gather.7.cloned.1.call-start = ((), (), s32[]{:S(2)}) async-start(), calls=%async_computation.8 | async-start | bytes 1310720 | tf_op jit(solution)/shard_map/all_gather | solution.py:871
  10.4 73.7 %all-gather.9.cloned.1.call-start = ((), (), s32[]{:S(2)}) async-start(), calls=%async_computation.9 | async-start | bytes 1310720 | tf_op jit(solution)/shard_map/all_gather | solution.py:871
  11.2 135.7 %all-gather.11.cloned.1.call-start = ((), (), s32[]{:S(2)}) async-start(), calls=%async_computation.10 | async-start | bytes 1310720 | tf_op jit(solution)/shard_map/all_gather | solution.py:871
  12.4 159.6 %all-gather.13.cloned.1.call-start = ((), (), s32[]{:S(2)}) async-start(), calls=%async_computation.11 | async-start | bytes 1310720 | tf_op jit(solution)/shard_map/all_gather | solution.py:871
  27.4 25.3 %all-to-all-start = ((bf16[8,32,1024]{2,1,0:T(8,128)(2,1)}), bf16[8,32,1024]{2,1,0:T(8,128)(2,1)S(1)}, u32[]{:S(2)}, u32[]{:S(2)}) async-start(bf16[8,32,1024]{2,1,0:T(8,128)(2,1)} %maximum_select_fusion), calls=%async_computation | async-start | bytes 1048576 | tf_op jit(solution)/shard_map/all_to_all | solution.py:342
  52.6 11.5 %all-to-all-start.1 = ((bf16[8,16,768]{2,1,0:T(8,128)(2,1)}), bf16[8,16,768]{2,1,0:T(8,128)(2,1)S(1)}, u32[]{:S(2)}, u32[]{:S(2)}) async-start(bf16[8,16,768]{2,1,0:T(8,128)(2,1)} %reshape.290), calls=%async_computation.1 | async-start | bytes 393216 | tf_op jit(solution)/shard_map/all_to_all | solution.py:342
  56.1 130.5 %all-gather.15.cloned.1.call-start = ((), (), s32[]{:S(2)}) async-start(), calls=%async_computation.17 | async-start | bytes 1310720 | tf_op jit(solution)/shard_map/all_gather | solution.py:871
  57.7 7.6 %collective-permute-start.3 = (bf16[128,1024]{1,0:T(8,128)(2,1)S(1)}, bf16[128,1024]{1,0:T(8,128)(2,1)S(1)}, u32[]{:S(2)}, u32[]{:S(2)}) collective-permute-start(bf16[128,1024]{1,0:T(8,128)(2,1)S(1)} %shard_map.196), channel_id=1, source_target_pairs={{0,2},{1,3},{2,0},{3,1},{4,6},{5,7},{6,4},{7,5},{8,10},{9,11},{10,... | collective-permute-start | bytes 786440 | tf_op jit(solution)/shard_map/ppermute | solution.py:32
  59.3 33.4 %collective-permute-start.7 = (bf16[4096,128]{1,0:T(8,128)(2,1)}, bf16[4096,128]{1,0:T(8,128)(2,1)S(1)}, u32[]{:S(2)}, u32[]{:S(2)}) collective-permute-start(bf16[4096,128]{1,0:T(8,128)(2,1)} %all-gather.7.cloned.1.call-done.here), channel_id=1, source_target_pairs={{0,4},{4,0},{8,12},{12,8},{16,20},{20,16},{24,28},{28,24},{1,5},{5... | collective-permute-start | bytes 3145736 | tf_op jit(solution)/shard_map/ppermute | solution.py:32
  66.5 17.6 %collective-permute-start.6 = (bf16[256,1024]{1,0:T(8,128)(2,1)S(1)}, bf16[256,1024]{1,0:T(8,128)(2,1)S(1)}, u32[]{:S(2)}, u32[]{:S(2)}) collective-permute-start(bf16[256,1024]{1,0:T(8,128)(2,1)S(1)} %shard_map.199.own.refs_4_), channel_id=1, source_target_pairs={{0,1},{1,0},{2,3},{3,2},{4,5},{5,4},{6,7},{7,6},{8,9},{9,8},{10,11... | collective-permute-start | bytes 1572872 | tf_op jit(solution)/shard_map/ppermute | solution.py:32
  67.5 39.6 %collective-permute-start.11 = (bf16[1024,128]{1,0:T(8,128)(2,1)}, bf16[1024,128]{1,0:T(8,128)(2,1)}, u32[]{:S(2)}, u32[]{:S(2)}) collective-permute-start(bf16[1024,128]{1,0:T(8,128)(2,1)} %get-tuple-element.147.refs_0_), channel_id=1, source_target_pairs={{0,4},{4,0},{8,12},{12,8},{16,20},{20,16},{24,28},{28,24},{1,5},{5... | collective-permute-start | bytes 786440 | tf_op jit(solution)/shard_map/ppermute | solution.py:32
  69.2 37.9 %collective-permute-start.10 = (bf16[1024,128]{1,0:T(8,128)(2,1)}, bf16[1024,128]{1,0:T(8,128)(2,1)}, u32[]{:S(2)}, u32[]{:S(2)}) collective-permute-start(bf16[1024,128]{1,0:T(8,128)(2,1)} %get-tuple-element.147.refs_0_), channel_id=1, source_target_pairs={{0,24},{4,28},{8,0},{12,4},{16,8},{20,12},{24,16},{28,20},{1,25},{... | collective-permute-start | bytes 786440 | tf_op jit(solution)/shard_map/ppermute | solution.py:55
  72.5 34.7 %collective-permute-start.9 = (bf16[1024,128]{1,0:T(8,128)(2,1)}, bf16[1024,128]{1,0:T(8,128)(2,1)}, u32[]{:S(2)}, u32[]{:S(2)}) collective-permute-start(bf16[1024,128]{1,0:T(8,128)(2,1)} %get-tuple-element.147.refs_0_), channel_id=1, source_target_pairs={{0,16},{4,20},{8,24},{12,28},{16,0},{20,4},{24,8},{28,12},{1,17},{... | collective-permute-start | bytes 786440 | tf_op jit(solution)/shard_map/ppermute | solution.py:55
  84.1 23.1 %collective-permute-start.8 = (bf16[1024,128]{1,0:T(8,128)(2,1)}, bf16[1024,128]{1,0:T(8,128)(2,1)}, u32[]{:S(2)}, u32[]{:S(2)}) collective-permute-start(bf16[1024,128]{1,0:T(8,128)(2,1)} %get-tuple-element.147.refs_0_), channel_id=1, source_target_pairs={{0,8},{4,12},{8,16},{12,20},{16,24},{20,28},{24,0},{28,4},{1,9},{5... | collective-permute-start | bytes 786440 | tf_op jit(solution)/shard_map/ppermute | solution.py:55
  93.7 26.5 %collective-permute-start.15 = (bf16[4096,128]{1,0:T(8,128)(2,1)}, bf16[4096,128]{1,0:T(8,128)(2,1)S(1)}, u32[]{:S(2)}, u32[]{:S(2)}) collective-permute-start(bf16[4096,128]{1,0:T(8,128)(2,1)} %all-gather.9.cloned.1.call-done.here), channel_id=1, source_target_pairs={{0,4},{4,0},{8,12},{12,8},{16,20},{20,16},{24,28},{28,24},{1,5},{5... | collective-permute-start | bytes 3145736 | tf_op jit(solution)/shard_map/ppermute | solution.py:32
  109.3 14.0 %collective-permute-start.14 = (bf16[256,1024]{1,0:T(8,128)(2,1)S(1)}, bf16[256,1024]{1,0:T(8,128)(2,1)S(1)}, u32[]{:S(2)}, u32[]{:S(2)}) collective-permute-start(bf16[256,1024]{1,0:T(8,128)(2,1)S(1)} %shard_map.203.here.branch_here), channel_id=1, source_target_pairs={{0,2},{1,3},{2,0},{3,1},{4,6},{5,7},{6,4},{7,5},{8,10},{9,11},{10,... | collective-permute-start | bytes 1572872 | tf_op jit(solution)/shard_map/ppermute | solution.py:32
  112.0 24.1 %collective-permute-start.17 = (bf16[3072,128]{1,0:T(8,128)(2,1)S(1)}, bf16[3072,128]{1,0:T(8,128)(2,1)S(1)}, u32[]{:S(2)}, u32[]{:S(2)}) collective-permute-start(bf16[3072,128]{1,0:T(8,128)(2,1)S(1)} %shard_map.207), channel_id=1, source_target_pairs={{0,4},{4,0},{8,12},{12,8},{16,20},{20,16},{24,28},{28,24},{1,5},{5... | collective-permute-start | bytes 2359304 | tf_op jit(solution)/shard_map/ppermute | solution.py:32
  125.9 13.3 %collective-permute-start.16 = (bf16[256,1024]{1,0:T(8,128)(2,1)S(1)}, bf16[256,1024]{1,0:T(8,128)(2,1)S(1)}, u32[]{:S(2)}, u32[]{:S(2)}) collective-permute-start(bf16[256,1024]{1,0:T(8,128)(2,1)S(1)} %get-tuple-element.153.own.refs_1_), channel_id=1, source_target_pairs={{0,1},{1,0},{2,3},{3,2},{4,5},{5,4},{6,7},{7,6},{8,9},{9,8},{10,11... | collective-permute-start | bytes 1572872 | tf_op jit(solution)/shard_map/ppermute | solution.py:32
  146.5 205.1 %reduce-scatter.6.cloned.1.call-start = ((), (), s32[]{:S(2)}) async-start(), calls=%async_computation.12 | async-start | bytes 1310720 | tf_op jit(solution)/shard_map/reduce_scatter | solution.py:276
  146.9 26.6 %collective-permute-start.22 = (bf16[4096,128]{1,0:T(8,128)(2,1)}, bf16[4096,128]{1,0:T(8,128)(2,1)}, u32[]{:S(2)}, u32[]{:S(2)}) collective-permute-start(bf16[4096,128]{1,0:T(8,128)(2,1)} %all-gather.11.cloned.1.call-done.here), channel_id=1, source_target_pairs={{0,4},{4,0},{8,12},{12,8},{16,20},{20,16},{24,28},{28,24},{1,5},{5... | collective-permute-start | bytes 3145736 | tf_op jit(solution)/shard_map/ppermute | solution.py:32
  151.2 13.6 %collective-permute-start.20 = (bf16[256,1024]{1,0:T(8,128)(2,1)S(1)}, bf16[256,1024]{1,0:T(8,128)(2,1)S(1)}, u32[]{:S(2)}, u32[]{:S(2)}) collective-permute-start(bf16[256,1024]{1,0:T(8,128)(2,1)S(1)} %shard_map.210.here.branch_here), channel_id=1, source_target_pairs={{0,2},{1,3},{2,0},{3,1},{4,6},{5,7},{6,4},{7,5},{8,10},{9,11},{10,... | collective-permute-start | bytes 1572872 | tf_op jit(solution)/shard_map/ppermute | solution.py:32
  168.9 7.5 %collective-permute-start.21 = (bf16[256,1024]{1,0:T(8,128)(2,1)}, bf16[256,1024]{1,0:T(8,128)(2,1)}, u32[]{:S(2)}, u32[]{:S(2)}) collective-permute-start(bf16[256,1024]{1,0:T(8,128)(2,1)} %get-tuple-element.161.own.refs_4_), channel_id=1, source_target_pairs={{0,1},{1,0},{2,3},{3,2},{4,5},{5,4},{6,7},{7,6},{8,9},{9,8},{10,11... | collective-permute-start | bytes 1572872 | tf_op jit(solution)/shard_map/ppermute | solution.py:32
  170.5 15.7 %collective-permute-start.23 = (bf16[128,1024]{1,0:T(8,128)(2,1)}, bf16[128,1024]{1,0:T(8,128)(2,1)}, u32[]{:S(2)}, u32[]{:S(2)}) collective-permute-start(bf16[128,1024]{1,0:T(8,128)(2,1)} %shard_map.215), channel_id=1, source_target_pairs={{0,2},{1,3},{2,0},{3,1},{4,6},{5,7},{6,4},{7,5},{8,10},{9,11},{10,... | collective-permute-start | bytes 786440 | tf_op jit(solution)/shard_map/ppermute | solution.py:32
  171.9 26.3 %collective-permute-start.27 = (bf16[4096,128]{1,0:T(8,128)(2,1)}, bf16[4096,128]{1,0:T(8,128)(2,1)}, u32[]{:S(2)}, u32[]{:S(2)}) collective-permute-start(bf16[4096,128]{1,0:T(8,128)(2,1)} %all-gather.13.cloned.1.call-done.here), channel_id=1, source_target_pairs={{0,4},{4,0},{8,12},{12,8},{16,20},{20,16},{24,28},{28,24},{1,5},{5... | collective-permute-start | bytes 3145736 | tf_op jit(solution)/shard_map/ppermute | solution.py:32
  190.8 14.0 %collective-permute-start.26 = (bf16[256,1024]{1,0:T(8,128)(2,1)S(1)}, bf16[256,1024]{1,0:T(8,128)(2,1)S(1)}, u32[]{:S(2)}, u32[]{:S(2)}) collective-permute-start(bf16[256,1024]{1,0:T(8,128)(2,1)S(1)} %shard_map.216.here.branch_here), channel_id=1, source_target_pairs={{0,2},{1,3},{2,0},{3,1},{4,6},{5,7},{6,4},{7,5},{8,10},{9,11},{10,... | collective-permute-start | bytes 1572872 | tf_op jit(solution)/shard_map/ppermute | solution.py:32
  191.4 28.5 %collective-permute-start.29 = (bf16[4096,128]{1,0:T(8,128)(2,1)S(1)}, bf16[4096,128]{1,0:T(8,128)(2,1)S(1)}, u32[]{:S(2)}, u32[]{:S(2)}) collective-permute-start(bf16[4096,128]{1,0:T(8,128)(2,1)S(1)} %bitcast.92), channel_id=1, source_target_pairs={{0,4},{4,0},{8,12},{12,8},{16,20},{20,16},{24,28},{28,24},{1,5},{5... | collective-permute-start | bytes 3145736 | tf_op jit(solution)/shard_map/ppermute | solution.py:32
  206.4 14.6 %collective-permute-start.28 = (bf16[256,1024]{1,0:T(8,128)(2,1)S(1)}, bf16[256,1024]{1,0:T(8,128)(2,1)S(1)}, u32[]{:S(2)}, u32[]{:S(2)}) collective-permute-start(bf16[256,1024]{1,0:T(8,128)(2,1)S(1)} %get-tuple-element.174.own.refs_1_), channel_id=1, source_target_pairs={{0,1},{1,0},{2,3},{3,2},{4,5},{5,4},{6,7},{7,6},{8,9},{9,8},{10,11... | collective-permute-start | bytes 1572872 | tf_op jit(solution)/shard_map/ppermute | solution.py:32
  226.2 14.0 %collective-permute-start.32 = (bf16[256,1024]{1,0:T(8,128)(2,1)S(1)}, bf16[256,1024]{1,0:T(8,128)(2,1)S(1)}, u32[]{:S(2)}, u32[]{:S(2)}) collective-permute-start(bf16[256,1024]{1,0:T(8,128)(2,1)S(1)} %shard_map.222.here), channel_id=1, source_target_pairs={{0,2},{1,3},{2,0},{3,1},{4,6},{5,7},{6,4},{7,5},{8,10},{9,11},{10,... | collective-permute-start | bytes 1572872 | tf_op jit(solution)/shard_map/ppermute | solution.py:32
  249.5 14.0 %collective-permute-start.36 = (bf16[256,1024]{1,0:T(8,128)(2,1)S(1)}, bf16[256,1024]{1,0:T(8,128)(2,1)S(1)}, u32[]{:S(2)}, u32[]{:S(2)}) collective-permute-start(bf16[256,1024]{1,0:T(8,128)(2,1)S(1)} %shard_map.228.here), channel_id=1, source_target_pairs={{0,2},{1,3},{2,0},{3,1},{4,6},{5,7},{6,4},{7,5},{8,10},{9,11},{10,... | collective-permute-start | bytes 1572872 | tf_op jit(solution)/shard_map/ppermute | solution.py:32
  250.1 28.7 %collective-permute-start.38 = (bf16[1024,512]{1,0:T(8,128)(2,1)S(1)}, bf16[1024,512]{1,0:T(8,128)(2,1)S(1)}, u32[]{:S(2)}, u32[]{:S(2)}) collective-permute-start(bf16[1024,512]{1,0:T(8,128)(2,1)S(1)} %get-tuple-element.185), channel_id=1, source_target_pairs={{0,4},{4,0},{8,12},{12,8},{16,20},{20,16},{24,28},{28,24},{1,5},{5... | collective-permute-start | bytes 3145736 | tf_op jit(solution)/shard_map/ppermute | solution.py:32
  280.6 89.9 %reduce-scatter.8.cloned.1.call-start = ((), (), s32[]{:S(2)}) async-start(), calls=%async_computation.13 | async-start | bytes 1310720 | tf_op jit(solution)/shard_map/reduce_scatter | solution.py:276
  284.2 14.0 %collective-permute-start.41 = (bf16[256,1024]{1,0:T(8,128)(2,1)S(1)}, bf16[256,1024]{1,0:T(8,128)(2,1)S(1)}, u32[]{:S(2)}, u32[]{:S(2)}) collective-permute-start(bf16[256,1024]{1,0:T(8,128)(2,1)S(1)} %shard_map.233.here), channel_id=1, source_target_pairs={{0,2},{1,3},{2,0},{3,1},{4,6},{5,7},{6,4},{7,5},{8,10},{9,11},{10,... | collective-permute-start | bytes 1572872 | tf_op jit(solution)/shard_map/ppermute | solution.py:32
  284.9 25.1 %collective-permute-start.43 = (bf16[1024,512]{1,0:T(8,128)(2,1)}, bf16[1024,512]{1,0:T(8,128)(2,1)S(1)}, u32[]{:S(2)}, u32[]{:S(2)}) collective-permute-start(bf16[1024,512]{1,0:T(8,128)(2,1)} %copy-done.141), channel_id=1, source_target_pairs={{0,4},{4,0},{8,12},{12,8},{16,20},{20,16},{24,28},{28,24},{1,5},{5... | collective-permute-start | bytes 3145736 | tf_op jit(solution)/shard_map/ppermute | solution.py:32
  302.1 7.9 %collective-permute-start.42 = (bf16[256,1024]{1,0:T(8,128)(2,1)S(1)}, bf16[256,1024]{1,0:T(8,128)(2,1)S(1)}, u32[]{:S(2)}, u32[]{:S(2)}) collective-permute-start(bf16[256,1024]{1,0:T(8,128)(2,1)S(1)} %get-tuple-element.210.refs_1_.own), channel_id=1, source_target_pairs={{0,1},{1,0},{2,3},{3,2},{4,5},{5,4},{6,7},{7,6},{8,9},{9,8},{10,11... | collective-permute-start | bytes 1572872 | tf_op jit(solution)/shard_map/ppermute | solution.py:32
  312.1 100.6 %reduce-scatter.10.cloned.1.call-start = ((), (), s32[]{:S(2)}) async-start(), calls=%async_computation.14 | async-start | bytes 1310720 | tf_op jit(solution)/shard_map/reduce_scatter | solution.py:276
  312.1 24.3 %collective-permute-start.44 = (bf16[1024,512]{1,0:T(8,128)(2,1)}, bf16[1024,512]{1,0:T(8,128)(2,1)S(1)}, u32[]{:S(2)}, u32[]{:S(2)}) collective-permute-start(bf16[1024,512]{1,0:T(8,128)(2,1)} %copy-done.143), channel_id=1, source_target_pairs={{0,4},{4,0},{8,12},{12,8},{16,20},{20,16},{24,28},{28,24},{1,5},{5... | collective-permute-start | bytes 3145736 | tf_op jit(solution)/shard_map/ppermute | solution.py:32
  337.7 156.9 %reduce-scatter.14.cloned.1.call-start = ((), (), s32[]{:S(2)}) async-start(), calls=%async_computation.16 | async-start | bytes 1310720 | tf_op jit(solution)/shard_map/reduce_scatter | solution.py:276
  341.9 14.3 %collective-permute-start.47 = (bf16[256,1024]{1,0:T(8,128)(2,1)}, bf16[256,1024]{1,0:T(8,128)(2,1)}, u32[]{:S(2)}, u32[]{:S(2)}) collective-permute-start(bf16[256,1024]{1,0:T(8,128)(2,1)} %shard_map.240.here), channel_id=1, source_target_pairs={{0,2},{1,3},{2,0},{3,1},{4,6},{5,7},{6,4},{7,5},{8,10},{9,11},{10,... | collective-permute-start | bytes 1572872 | tf_op jit(solution)/shard_map/ppermute | solution.py:32
  343.3 26.4 %collective-permute-start.49 = (bf16[1024,512]{1,0:T(8,128)(2,1)}, bf16[1024,512]{1,0:T(8,128)(2,1)}, u32[]{:S(2)}, u32[]{:S(2)}) collective-permute-start(bf16[1024,512]{1,0:T(8,128)(2,1)} %copy-done.142), channel_id=1, source_target_pairs={{0,4},{4,0},{8,12},{12,8},{16,20},{20,16},{24,28},{28,24},{1,5},{5... | collective-permute-start | bytes 3145736 | tf_op jit(solution)/shard_map/ppermute | solution.py:32
  363.0 49.7 %collective-permute-start.53 = (bf16[1024,512]{1,0:T(8,128)(2,1)}, bf16[1024,512]{1,0:T(8,128)(2,1)}, u32[]{:S(2)}, u32[]{:S(2)}) collective-permute-start(bf16[1024,512]{1,0:T(8,128)(2,1)} %get-tuple-element.228), channel_id=1, source_target_pairs={{0,4},{4,0},{8,12},{12,8},{16,20},{20,16},{24,28},{28,24},{1,5},{5... | collective-permute-start | bytes 3145736 | tf_op jit(solution)/shard_map/ppermute | solution.py:32
  397.8 14.0 %collective-permute-start.52 = (bf16[256,1024]{1,0:T(8,128)(2,1)S(1)}, bf16[256,1024]{1,0:T(8,128)(2,1)S(1)}, u32[]{:S(2)}, u32[]{:S(2)}) collective-permute-start(bf16[256,1024]{1,0:T(8,128)(2,1)S(1)} %shard_map.246.here), channel_id=1, source_target_pairs={{0,2},{1,3},{2,0},{3,1},{4,6},{5,7},{6,4},{7,5},{8,10},{9,11},{10,... | collective-permute-start | bytes 1572872 | tf_op jit(solution)/shard_map/ppermute | solution.py:32
  398.5 25.4 %collective-permute-start.54 = (bf16[1024,512]{1,0:T(8,128)(2,1)}, bf16[1024,512]{1,0:T(8,128)(2,1)}, u32[]{:S(2)}, u32[]{:S(2)}) collective-permute-start(bf16[1024,512]{1,0:T(8,128)(2,1)} %get-tuple-element.241), channel_id=1, source_target_pairs={{0,4},{4,0},{8,12},{12,8},{16,20},{20,16},{24,28},{28,24},{1,5},{5... | collective-permute-start | bytes 3145736 | tf_op jit(solution)/shard_map/ppermute | solution.py:32
  426.8 33.2 %all-to-all-start.2 = ((bf16[8,38,1024]{2,1,0:T(8,128)(2,1)}), bf16[8,38,1024]{2,1,0:T(8,128)(2,1)}, u32[]{:S(2)}, u32[]{:S(2)}) async-start(bf16[8,38,1024]{2,1,0:T(8,128)(2,1)} %pad_maximum_fusion.1), calls=%async_computation.5 | async-start | bytes 1310720 | tf_op jit(solution)/shard_map/all_to_all | solution.py:342
  432.8 65.2 %reduce-scatter.12.cloned.1.call-start = ((), (), s32[]{:S(2)}) async-start(), calls=%async_computation.15 | async-start | bytes 1310720 | tf_op jit(solution)/shard_map/reduce_scatter | solution.py:276
  466.6 28.0 %collective-permute-start.60 = (bf16[1024,128]{1,0:T(8,128)(2,1)}, bf16[1024,128]{1,0:T(8,128)(2,1)S(1)}, u32[]{:S(2)}, u32[]{:S(2)}) collective-permute-start(bf16[1024,128]{1,0:T(8,128)(2,1)} %get-tuple-element.300), channel_id=1, source_target_pairs={{0,24},{4,28},{8,0},{12,4},{16,8},{20,12},{24,16},{28,20},{1,25},{... | collective-permute-start | bytes 786440 | tf_op jit(solution)/shard_map/ppermute | solution.py:286
  468.4 26.3 %collective-permute-start.62 = (bf16[1024,128]{1,0:T(8,128)(2,1)}, bf16[1024,128]{1,0:T(8,128)(2,1)S(1)}, u32[]{:S(2)}, u32[]{:S(2)}) collective-permute-start(bf16[1024,128]{1,0:T(8,128)(2,1)} %get-tuple-element.301), channel_id=1, source_target_pairs={{0,8},{4,12},{8,16},{12,20},{16,24},{20,28},{24,0},{28,4},{1,9},{5... | collective-permute-start | bytes 786440 | tf_op jit(solution)/shard_map/ppermute | solution.py:286
  468.9 25.7 %collective-permute-start.61 = (bf16[1024,128]{1,0:T(8,128)(2,1)}, bf16[1024,128]{1,0:T(8,128)(2,1)S(1)}, u32[]{:S(2)}, u32[]{:S(2)}) collective-permute-start(bf16[1024,128]{1,0:T(8,128)(2,1)} %get-tuple-element.302), channel_id=1, source_target_pairs={{0,16},{4,20},{8,24},{12,28},{16,0},{20,4},{24,8},{28,12},{1,17},{... | collective-permute-start | bytes 786440 | tf_op jit(solution)/shard_map/ppermute | solution.py:286
  469.3 16.8 %collective-permute-start.58 = (f32[40,256]{1,0:T(8,128)S(1)}, f32[40,256]{1,0:T(8,128)S(1)}, u32[]{:S(2)}, u32[]{:S(2)}) collective-permute-start(f32[40,256]{1,0:T(8,128)S(1)} %fusion.21), channel_id=1, source_target_pairs={{0,8},{4,12},{8,0},{12,4},{16,24},{20,28},{24,16},{28,20},{1,9},{5... | collective-permute-start | bytes 122888 | tf_op jit(solution)/shard_map/ppermute | solution.py:32
  (201 other events, 1216.9 us)
Sparse Core Ops, SparseCore 0:
  10.5 38.6 all-gather.6
  51.3 32.6 all-gather.8
  86.2 37.7 all-gather.10
  125.5 27.4 all-gather.12
  154.9 27.4 all-gather.14
  280.7 27.5 reduce-scatter.5
  312.2 28.3 reduce-scatter.7
  342.9 25.7 reduce-scatter.9
  392.1 27.4 reduce-scatter.13
  435.6 32.0 reduce-scatter.11

commit v4 on v3

--- a/solution.py
+++ b/solution.py
@@ -357,7 +357,7 @@
 stripe = 64
 
 
-def call(kernel, outs, *operands, scratch=(), scalars=0, cost=1):
+def call(kernel, outs, *operands, scratch=(), scalars=0, cost=400_000_000):
     spec = pl.BlockSpec(memory_space=pltpu.VMEM)
     return pl.pallas_call(
         kernel,
@@ -1020,14 +1020,13 @@
             sums_fc2 = Sums(*terms)
             slope = tie(slope, *terms)
         part_own, part_a, part_b, grad_hidden = mlp_back(*grad_branch, slope, fc1_full, fc2_full)
-        if near and layer == 0:
-            part_a = tie(part_a, layer_sums[1][0].arrived)
-            part_a = layer_sums[1][0].fold(True, part_a)
         here, there = sum_pack_rows(part_own, (part_a, part_b))
         if near:
             terms = gradients((tie(grad_hidden, here), second))
             sums_fc1 = Sums(*terms)
-            there = tie(there, *terms, *([layer_sums[1][2].blocks] if layer == 0 else [mixed_out]))
+            there = tie(there, *terms, *([layer_sums[1][2].blocks, layer_sums[1][0].arrived] if layer == 0 else [mixed_out]))
+            if layer == 0:
+                there = layer_sums[1][0].fold(True, there)
         else:
             sums_fc2 = WholeSums(gradient_blocks(order, (activated, grad_branch)))
             sums_fc1 = WholeSums(gradient_blocks(order, (grad_hidden, second)))
@@ -1037,15 +1036,15 @@
         mod_sums[layer][3], mod_sums[layer][5], mod_sums[layer][0] = ((sums, i * width) for i in range(3))
         other = across_cores(grad_low)
         if near and layer == 0:
-            other = tie(other, sums_fc2.arrived, layer_sums[1][1].blocks)
-            other = sums_fc2.fold(True, other)
+            other = tie(other, layer_sums[1][1].blocks)
         grad_attended = (grad_low, other)
         part_own, part_a, part_b, grad_projected, scale_grads[layer] = attend_back(
             *grad_attended, kept, qkv_full, proj_full, scales[layer], layout, heads_here
         )
         if near and layer == 0:
             terms = gradients(((kept[0], 3 * span, 4 * span), grad_attended), (grad_projected, first))
-            part_a = tie(part_a, *terms)
+            part_a = tie(part_a, *terms, sums_fc2.arrived)
+            part_a = sums_fc2.fold(True, part_a)
         elif near:
             part_a = tie(part_a, sums_fc2.arrived)
             part_a = sums_fc2.fold(True, part_a)
@@ -1071,7 +1070,6 @@
         layer_sums[layer] = (sums_attn, sums_fc1, sums_fc2)
     if near:
         grad_carried = tie(grad_carried, layer_sums[0][0].arrived)
-        layer_sums[0][0].fold(False, grad_carried)
 
     grads_back = repack(to_rows, grad_carried, order).reshape(groups, slots, width)
     sent = jnp.stack([give(layer) for layer in range(layers)], axis=1).reshape(groups, layers * items * columns)
@@ -1084,6 +1082,8 @@
         mods_back = back[:, 2 * slots :]
     mixed_back, grads_back = back[:, :slots], back[:, slots : 2 * slots]
     mods_back = mods_back.reshape(groups, layers, items, columns)
+    if near:
+        mods_back = tie(mods_back, layer_sums[0][1].blocks)
     mods_back = [mods_back[:, layer] for layer in range(layers)]
 
     mixed = contract_rows(to_slots, mixed_back.reshape(rows, width)).astype(low)
@@ -1096,6 +1096,8 @@
     if paired(groups):
         for offset in (1, 2, 4):
             summed = summed + swap(summed, "dp", offset)
+            if offset == 2:
+                layer_sums[0][0].fold(False, summed)
     else:
         summed = lax.psum(summed, "dp")
     grad_silu = summed[: cond.shape[0]]

time: 514 us -> 494 us (0.961)
  local copies, waits for them, and re-layouts: 86.1 us -> 74.6 us
    ppermute x3, waiting for transfers between devices: 0.01 us -> 14.2 us  [fold(): self.parts[back] = lax.ppermute(self.parts[back].astype(low), 'dp', pairs)]
    ppermute x57, waiting for transfers between devices: 160 us -> 151 us  [swap(): return lax.ppermute(value, axis, [(i, i ^ offset) for i in range(size)])]
    unnamed x350 -> x346, local copies, waits for them, and re-layouts: 74.6 us -> 66.4 us
    ppermute x57, starting transfers between devices: 51.6 us -> 45.4 us  [swap(): return lax.ppermute(value, axis, [(i, i ^ offset) for i in range(size)])]
  transfers between devices with their start and end apart: 76 -> 76, of which waited for: 43 -> 47; matrix products, arithmetic and copies ran while one was open for 5% -> 4% of each run, Pallas kernels for 18% -> 18%
where the time goes in v4:
time: 494 us; the launch traced here: 487 us
  waiting for transfers between devices  206 us (42%)
  Pallas kernels  98.6 us (20%)
  starting transfers between devices  77.7 us (16%)
  local copies, waits for them, and re-layouts  74.6 us (15%)
  between operations  16.4 us (3%)
  other arithmetic  11.1 us (2%)
    ppermute x57, waiting for transfers between devices, swap(): return lax.ppermute(value, axis, [(i, i ^ offset) for i in range(size)])  151 us
    pallas_call x60, Pallas kernels, call(): pl.pallas_call(kernel, out_shape=[jax.ShapeDtypeStruct(shape, kind) for s...  98.6 us
    unnamed x346, local copies, waits for them, and re-layouts  66.4 us
    ppermute x57, starting transfers between devices, swap(): return lax.ppermute(value, axis, [(i, i ^ offset) for i in range(size)])  45.4 us
    all_to_all x3, waiting for transfers between devices, exchange(): return lax.all_to_all(value, 'dp', split_axis=0, concat_axis=0, tiled=True)  30.5 us
    ppermute x3, waiting for transfers between devices, fold(): self.parts[back] = lax.ppermute(self.parts[back].astype(low), 'dp', pairs)  14.2 us
    all_to_all x3, starting transfers between devices, exchange(): return lax.all_to_all(value, 'dp', split_axis=0, concat_axis=0, tiled=True)  13.8 us
    ppermute x3, starting transfers between devices, straight(): lax.ppermute(block, 'dp', [(i, (i + 2 * back) % 8) for i in range(8)])  12.4 us
  transfers between devices with their start and end apart: 76, of which 47 were waited for; matrix products, arithmetic and copies ran while one was open for 4% of the time, Pallas kernels for 18%

profile of v4, /device:TPU:0, one launch (start us, length us, event | category | flops | bytes accessed | tf_op | source)
XLA Modules:
  0.0 487.2 jit_solution(5097449384257295521)
XLA Ops:
  12.4 3.0 collective-permute-start
  20.0 2.0 collective-permute-done.1
  22.0 2.7 collective-permute-start.2
  24.6 1.9 collective-permute-done.2
  27.9 5.4 %all-to-all-start = ((bf16[8,32,1024]{2,1,0:T(8,128)(2,1)}), bf16[8,32,1024]{2,1,0:T(8,128)(2,1)S(1)}, u32[]{:S(2)}, u32[]{:S(2)}) async-start(bf16[8,32,1024]{2,1,0:T(8,128)(2,1)} %maximum_select_fusion), calls=%async_computation | async-start | bytes 1048576 | tf_op jit(solution)/shard_map/all_to_all | solution.py:342
  36.9 5.6 %collective-permute-done.5 = f32[2,32,768]{2,1,0:T(8,128)S(1)} collective-permute-done((f32[2,32,768]{2,1,0:T(8,128)S(1)}, f32[2,32,768]{2,1,0:T(8,128)S(1)}, u32[]{:S(2)}, u32[]{:S(2)}) %collective-permute-start.5) | collective-permute-done | bytes 196640 | tf_op jit(solution)/shard_map/ppermute | solution.py:32
  43.6 9.0 %all-to-all-done = bf16[8,32,1024]{2,1,0:T(8,128)(2,1)S(1)} async-done(((bf16[8,32,1024]{2,1,0:T(8,128)(2,1)}), bf16[8,32,1024]{2,1,0:T(8,128)(2,1)S(1)}, u32[]{:S(2)}, u32[]{:S(2)}) %all-to-all-start) | async-done | bytes 524320 | tf_op jit(solution)/shard_map/all_to_all | solution.py:342
  52.6 3.5 all-to-all-start.1
  57.0 2.0 collective-permute-start.7
  61.3 3.8 all-to-all-done.1.arrived
  70.7 3.5 collective-permute-start.10
  74.2 8.9 %all-gather.9.cloned.1.call-done.here = bf16[4096,128]{1,0:T(8,128)(2,1)} async-done(((bf16[1024,128]{1,0:T(8,128)(2,1)}), bf16[4096,128]{1,0:T(8,128)(2,1)}) %all-gather.9.cloned.1.call-update) | async-done | bytes 1048592 | tf_op jit(solution)/shard_map/all_gather | solution.py:871
  83.1 8.9 %collective-permute-start.8 = (bf16[1024,128]{1,0:T(8,128)(2,1)S(1)}, bf16[1024,128]{1,0:T(8,128)(2,1)S(1)}, u32[]{:S(2)}, u32[]{:S(2)}) collective-permute-start(bf16[1024,128]{1,0:T(8,128)(2,1)S(1)} %get-tuple-element.147.refs_0_), channel_id=1, source_target_pairs={{0,8},{4,12},{8,16},{12,20},{16,24},{20,28},{24,0},{28,4},{1,9},{5... | collective-permute-start | bytes 786440 | tf_op jit(solution)/shard_map/ppermute | solution.py:55
  97.0 4.2 shard_map.202
  109.1 9.2 %collective-permute-done.15.there = bf16[4096,128]{1,0:T(8,128)(2,1)S(1)} collective-permute-done((bf16[4096,128]{1,0:T(8,128)(2,1)}, bf16[4096,128]{1,0:T(8,128)(2,1)S(1)}, u32[]{:S(2)}, u32[]{:S(2)}) %collective-permute-start.15) | collective-permute-done | bytes 1048608 | tf_op jit(solution)/shard_map/ppermute | solution.py:32
  121.8 12.4 %collective-permute-done.17.refs_5_ = bf16[3072,128]{1,0:T(8,128)(2,1)S(1)} collective-permute-done((bf16[3072,128]{1,0:T(8,128)(2,1)S(1)}, bf16[3072,128]{1,0:T(8,128)(2,1)S(1)}, u32[]{:S(2)}, u32[]{:S(2)}) %collective-permute-start.17) | collective-permute-done | bytes 786464 | tf_op jit(solution)/shard_map/ppermute | solution.py:32
  137.9 3.8 shard_map.209
  151.2 12.0 %collective-permute-done.20.there.branch_there = bf16[256,1024]{1,0:T(8,128)(2,1)S(1)} collective-permute-done((bf16[256,1024]{1,0:T(8,128)(2,1)S(1)}, bf16[256,1024]{1,0:T(8,128)(2,1)S(1)}, u32[]{:S(2)}, u32[]{:S(2)}) %collective-permute-start.20) | collective-permute-done | bytes 524320 | tf_op jit(solution)/shard_map/ppermute | solution.py:32
  163.3 2.4 shard_map.211
  175.2 6.9 %shard_map.214 = (f32[256,1024]{1,0:T(8,128)S(1)}, bf16[128,1024]{1,0:T(8,128)(2,1)}, bf16[128,1024]{1,0:T(8,128)(2,1)}, bf16[512,1024]{1,0:T(8,128)(2,1)S(1)}, f32[512,12]{1,0:T(8,128)S(1)}) custom-call(bf16[256,1024]{1,0:T(8,128)(2,1)} %get-tuple-element.161.own.refs_4_, bf16[256,1024]{1,0:T(8,128)(2,1)} %collective-permute-done.21.other.refs_5_, ...), custom_call_target="tpu_custom_call" | custom-call | flops 400000000 | bytes 1 | tf_op jit(solution)/shard_map/pallas_call | solution.py:362
  191.5 5.3 %collective-permute-done.27.there = bf16[4096,128]{1,0:T(8,128)(2,1)} collective-permute-done((bf16[4096,128]{1,0:T(8,128)(2,1)}, bf16[4096,128]{1,0:T(8,128)(2,1)}, u32[]{:S(2)}, u32[]{:S(2)}) %collective-permute-start.27) | collective-permute-done | bytes 1048608 | tf_op jit(solution)/shard_map/ppermute | solution.py:32
  196.7 6.7 %collective-permute-done.26.there.branch_there = bf16[256,1024]{1,0:T(8,128)(2,1)S(1)} collective-permute-done((bf16[256,1024]{1,0:T(8,128)(2,1)S(1)}, bf16[256,1024]{1,0:T(8,128)(2,1)S(1)}, u32[]{:S(2)}, u32[]{:S(2)}) %collective-permute-start.26) | collective-permute-done | bytes 524320 | tf_op jit(solution)/shard_map/ppermute | solution.py:32
  206.9 11.5 %collective-permute-done.29.there = bf16[4096,128]{1,0:T(8,128)(2,1)S(1)} collective-permute-done((bf16[4096,128]{1,0:T(8,128)(2,1)S(1)}, bf16[4096,128]{1,0:T(8,128)(2,1)S(1)}, u32[]{:S(2)}, u32[]{:S(2)}) %collective-permute-start.29) | collective-permute-done | bytes 1048608 | tf_op jit(solution)/shard_map/ppermute | solution.py:32
  219.6 3.0 shard_map.221
  226.4 12.3 %collective-permute-done.32.there = bf16[256,1024]{1,0:T(8,128)(2,1)S(1)} collective-permute-done((bf16[256,1024]{1,0:T(8,128)(2,1)S(1)}, bf16[256,1024]{1,0:T(8,128)(2,1)S(1)}, u32[]{:S(2)}, u32[]{:S(2)}) %collective-permute-start.32) | collective-permute-done | bytes 524320 | tf_op jit(solution)/shard_map/ppermute | solution.py:32
  243.2 2.4 shard_map.227
  254.6 7.1 %collective-permute-done.36.there = bf16[256,1024]{1,0:T(8,128)(2,1)S(1)} collective-permute-done((bf16[256,1024]{1,0:T(8,128)(2,1)S(1)}, bf16[256,1024]{1,0:T(8,128)(2,1)S(1)}, u32[]{:S(2)}, u32[]{:S(2)}) %collective-permute-start.36) | collective-permute-done | bytes 524320 | tf_op jit(solution)/shard_map/ppermute | solution.py:32
  266.3 8.0 %shard_map.231 = (f32[256,1024]{1,0:T(8,128)S(1)}, bf16[128,1024]{1,0:T(8,128)(2,1)S(1)}, bf16[128,1024]{1,0:T(8,128)(2,1)S(1)}, bf16[512,768]{1,0:T(8,128)(2,1)S(1)}, f32[1,4]{1,0:T(1,128)S(1)}) custom-call(bf16[256,1024]{1,0:T(8,128)(2,1)S(1)} %get-tuple-element.195.own.refs_1_, bf16[256,1024]{1,0:T(8,128)(2,1)S(1)} %collective-permute-done.37.other.refs_2_, ...), custom_call_target="tpu_custom_call" | custom-call | flops 400000000 | bytes 1 | tf_op jit(solution)/shard_map/pallas_call | solution.py:362
  286.1 2.5 shard_map.234
  290.6 6.1 %collective-permute-done.41.there = bf16[256,1024]{1,0:T(8,128)(2,1)S(1)} collective-permute-done((bf16[256,1024]{1,0:T(8,128)(2,1)S(1)}, bf16[256,1024]{1,0:T(8,128)(2,1)S(1)}, u32[]{:S(2)}, u32[]{:S(2)}) %collective-permute-start.41) | collective-permute-done | bytes 524320 | tf_op jit(solution)/shard_map/ppermute | solution.py:32
  301.1 7.3 %collective-permute-done.43.arrived = bf16[1024,512]{1,0:T(8,128)(2,1)S(1)} collective-permute-done((bf16[1024,512]{1,0:T(8,128)(2,1)}, bf16[1024,512]{1,0:T(8,128)(2,1)S(1)}, u32[]{:S(2)}, u32[]{:S(2)}) %collective-permute-start.43) | collective-permute-done | bytes 1048608 | tf_op jit(solution)/shard_map/ppermute | solution.py:32
  320.1 2.4 shard_map.238
  326.1 2.3 shard_map.240
  329.4 5.4 %collective-permute-done.47.arrived = bf16[1024,512]{1,0:T(8,128)(2,1)S(1)} collective-permute-done((bf16[1024,512]{1,0:T(8,128)(2,1)}, bf16[1024,512]{1,0:T(8,128)(2,1)S(1)}, u32[]{:S(2)}, u32[]{:S(2)}) %collective-permute-start.47) | collective-permute-done | bytes 1048608 | tf_op jit(solution)/shard_map/ppermute | solution.py:32
  335.8 2.8 collective-permute-done.46.there
  360.8 8.0 %shard_map.243 = (f32[256,1024]{1,0:T(8,128)S(1)}, bf16[128,1024]{1,0:T(8,128)(2,1)S(1)}, bf16[128,1024]{1,0:T(8,128)(2,1)S(1)}, bf16[512,768]{1,0:T(8,128)(2,1)S(1)}, f32[1,4]{1,0:T(1,128)S(1)}) custom-call(bf16[256,1024]{1,0:T(8,128)(2,1)S(1)} %copy-done.51, bf16[256,1024]{1,0:T(8,128)(2,1)S(1)} %copy-done.54, bf16[512,1024]{1,0:T(8,128)(2,1)S(1)} %copy-done.32, ...), custom_call_target="tpu_custom_call" | custom-call | flops 400000000 | bytes 1 | tf_op jit(solution)/shard_map/pallas_call | solution.py:362
  372.0 2.5 shard_map.245
  383.0 8.9 %collective-permute-done.52.there = bf16[256,1024]{1,0:T(8,128)(2,1)S(1)} collective-permute-done((bf16[256,1024]{1,0:T(8,128)(2,1)S(1)}, bf16[256,1024]{1,0:T(8,128)(2,1)S(1)}, u32[]{:S(2)}, u32[]{:S(2)}) %collective-permute-start.52) | collective-permute-done | bytes 524320 | tf_op jit(solution)/shard_map/ppermute | solution.py:32
  393.2 2.4 shard_map.247
  402.4 8.9 %collective-permute-done.54 = bf16[1024,512]{1,0:T(8,128)(2,1)} collective-permute-done((bf16[1024,512]{1,0:T(8,128)(2,1)}, bf16[1024,512]{1,0:T(8,128)(2,1)}, u32[]{:S(2)}, u32[]{:S(2)}) %collective-permute-start.54) | collective-permute-done | bytes 1048608 | tf_op jit(solution)/shard_map/ppermute | solution.py:32
  413.1 4.9 %all-to-all-start.2 = ((bf16[8,38,1024]{2,1,0:T(8,128)(2,1)}), bf16[8,38,1024]{2,1,0:T(8,128)(2,1)S(1)}, u32[]{:S(2)}, u32[]{:S(2)}) async-start(bf16[8,38,1024]{2,1,0:T(8,128)(2,1)} %pad_maximum_fusion.1), calls=%async_computation.5 | async-start | bytes 1310720 | tf_op jit(solution)/shard_map/all_to_all | solution.py:342
  418.8 17.6 %all-to-all-done.2 = bf16[8,38,1024]{2,1,0:T(8,128)(2,1)S(1)} async-done(((bf16[8,38,1024]{2,1,0:T(8,128)(2,1)}), bf16[8,38,1024]{2,1,0:T(8,128)(2,1)S(1)}, u32[]{:S(2)}, u32[]{:S(2)}) %all-to-all-start.2) | async-done | bytes 622624 | tf_op jit(solution)/shard_map/all_to_all | solution.py:342
  443.5 4.9 collective-permute-done.58
  453.2 2.9 collective-permute-start.61
  460.1 1.9 shard_map.255
  462.0 2.0 maximum_convert_fusion.3
  464.0 4.7 collective-permute-done.62
  468.7 9.4 %collective-permute-done.61 = bf16[1024,128]{1,0:T(8,128)(2,1)S(1)} collective-permute-done((bf16[1024,128]{1,0:T(8,128)(2,1)}, bf16[1024,128]{1,0:T(8,128)(2,1)S(1)}, u32[]{:S(2)}, u32[]{:S(2)}) %collective-permute-start.61) | collective-permute-done | bytes 262176 | tf_op jit(solution)/shard_map/ppermute | solution.py:286
  (609 shorter events, 195.6 us)
Async XLA Ops:
  7.2 49.8 %all-gather.7.cloned.1.call-start = ((), (), s32[]{:S(2)}) async-start(), calls=%async_computation.8 | async-start | bytes 1310720 | tf_op jit(solution)/shard_map/all_gather | solution.py:871
  10.4 72.7 %all-gather.9.cloned.1.call-start = ((), (), s32[]{:S(2)}) async-start(), calls=%async_computation.9 | async-start | bytes 1310720 | tf_op jit(solution)/shard_map/all_gather | solution.py:871
  11.2 134.2 %all-gather.11.cloned.1.call-start = ((), (), s32[]{:S(2)}) async-start(), calls=%async_computation.10 | async-start | bytes 1310720 | tf_op jit(solution)/shard_map/all_gather | solution.py:871
  12.4 158.1 %all-gather.13.cloned.1.call-start = ((), (), s32[]{:S(2)}) async-start(), calls=%async_computation.11 | async-start | bytes 1310720 | tf_op jit(solution)/shard_map/all_gather | solution.py:871
  27.9 24.7 %all-to-all-start = ((bf16[8,32,1024]{2,1,0:T(8,128)(2,1)}), bf16[8,32,1024]{2,1,0:T(8,128)(2,1)S(1)}, u32[]{:S(2)}, u32[]{:S(2)}) async-start(bf16[8,32,1024]{2,1,0:T(8,128)(2,1)} %maximum_select_fusion), calls=%async_computation | async-start | bytes 1048576 | tf_op jit(solution)/shard_map/all_to_all | solution.py:342
  52.6 12.5 %all-to-all-start.1 = ((bf16[8,16,768]{2,1,0:T(8,128)(2,1)}), bf16[8,16,768]{2,1,0:T(8,128)(2,1)S(1)}, u32[]{:S(2)}, u32[]{:S(2)}) async-start(bf16[8,16,768]{2,1,0:T(8,128)(2,1)} %reshape.290), calls=%async_computation.1 | async-start | bytes 393216 | tf_op jit(solution)/shard_map/all_to_all | solution.py:342
  56.1 129.1 %all-gather.15.cloned.1.call-start = ((), (), s32[]{:S(2)}) async-start(), calls=%async_computation.17 | async-start | bytes 1310720 | tf_op jit(solution)/shard_map/all_gather | solution.py:871
  57.0 35.1 %collective-permute-start.7 = (bf16[4096,128]{1,0:T(8,128)(2,1)}, bf16[4096,128]{1,0:T(8,128)(2,1)}, u32[]{:S(2)}, u32[]{:S(2)}) collective-permute-start(bf16[4096,128]{1,0:T(8,128)(2,1)} %all-gather.7.cloned.1.call-done.here), channel_id=1, source_target_pairs={{0,4},{4,0},{8,12},{12,8},{16,20},{20,16},{24,28},{28,24},{1,5},{5... | collective-permute-start | bytes 3145736 | tf_op jit(solution)/shard_map/ppermute | solution.py:32
  68.0 15.1 %collective-permute-start.6 = (bf16[256,1024]{1,0:T(8,128)(2,1)S(1)}, bf16[256,1024]{1,0:T(8,128)(2,1)S(1)}, u32[]{:S(2)}, u32[]{:S(2)}) collective-permute-start(bf16[256,1024]{1,0:T(8,128)(2,1)S(1)} %shard_map.199.own.refs_4_), channel_id=1, source_target_pairs={{0,1},{1,0},{2,3},{3,2},{4,5},{5,4},{6,7},{7,6},{8,9},{9,8},{10,11... | collective-permute-start | bytes 1572872 | tf_op jit(solution)/shard_map/ppermute | solution.py:32
  70.4 31.9 %collective-permute-start.11 = (bf16[1024,128]{1,0:T(8,128)(2,1)S(1)}, bf16[1024,128]{1,0:T(8,128)(2,1)}, u32[]{:S(2)}, u32[]{:S(2)}) collective-permute-start(bf16[1024,128]{1,0:T(8,128)(2,1)S(1)} %get-tuple-element.147.refs_0_), channel_id=1, source_target_pairs={{0,4},{4,0},{8,12},{12,8},{16,20},{20,16},{24,28},{28,24},{1,5},{5... | collective-permute-start | bytes 786440 | tf_op jit(solution)/shard_map/ppermute | solution.py:32
  70.7 31.6 %collective-permute-start.10 = (bf16[1024,128]{1,0:T(8,128)(2,1)S(1)}, bf16[1024,128]{1,0:T(8,128)(2,1)S(1)}, u32[]{:S(2)}, u32[]{:S(2)}) collective-permute-start(bf16[1024,128]{1,0:T(8,128)(2,1)S(1)} %get-tuple-element.147.refs_0_), channel_id=1, source_target_pairs={{0,24},{4,28},{8,0},{12,4},{16,8},{20,12},{24,16},{28,20},{1,25},{... | collective-permute-start | bytes 786440 | tf_op jit(solution)/shard_map/ppermute | solution.py:55
  74.2 28.9 %collective-permute-start.9 = (bf16[1024,128]{1,0:T(8,128)(2,1)S(1)}, bf16[1024,128]{1,0:T(8,128)(2,1)}, u32[]{:S(2)}, u32[]{:S(2)}) collective-permute-start(bf16[1024,128]{1,0:T(8,128)(2,1)S(1)} %get-tuple-element.147.refs_0_), channel_id=1, source_target_pairs={{0,16},{4,20},{8,24},{12,28},{16,0},{20,4},{24,8},{28,12},{1,17},{... | collective-permute-start | bytes 786440 | tf_op jit(solution)/shard_map/ppermute | solution.py:55
  83.1 20.0 %collective-permute-start.8 = (bf16[1024,128]{1,0:T(8,128)(2,1)S(1)}, bf16[1024,128]{1,0:T(8,128)(2,1)S(1)}, u32[]{:S(2)}, u32[]{:S(2)}) collective-permute-start(bf16[1024,128]{1,0:T(8,128)(2,1)S(1)} %get-tuple-element.147.refs_0_), channel_id=1, source_target_pairs={{0,8},{4,12},{8,16},{12,20},{16,24},{20,28},{24,0},{28,4},{1,9},{5... | collective-permute-start | bytes 786440 | tf_op jit(solution)/shard_map/ppermute | solution.py:55
  92.0 26.2 %collective-permute-start.15 = (bf16[4096,128]{1,0:T(8,128)(2,1)}, bf16[4096,128]{1,0:T(8,128)(2,1)S(1)}, u32[]{:S(2)}, u32[]{:S(2)}) collective-permute-start(bf16[4096,128]{1,0:T(8,128)(2,1)} %all-gather.9.cloned.1.call-done.here), channel_id=1, source_target_pairs={{0,4},{4,0},{8,12},{12,8},{16,20},{20,16},{24,28},{28,24},{1,5},{5... | collective-permute-start | bytes 3145736 | tf_op jit(solution)/shard_map/ppermute | solution.py:32
  105.2 14.0 %collective-permute-start.14 = (bf16[256,1024]{1,0:T(8,128)(2,1)S(1)}, bf16[256,1024]{1,0:T(8,128)(2,1)S(1)}, u32[]{:S(2)}, u32[]{:S(2)}) collective-permute-start(bf16[256,1024]{1,0:T(8,128)(2,1)S(1)} %shard_map.203.here.branch_here), channel_id=1, source_target_pairs={{0,2},{1,3},{2,0},{3,1},{4,6},{5,7},{6,4},{7,5},{8,10},{9,11},{10,... | collective-permute-start | bytes 1572872 | tf_op jit(solution)/shard_map/ppermute | solution.py:32
  107.7 26.5 %collective-permute-start.17 = (bf16[3072,128]{1,0:T(8,128)(2,1)S(1)}, bf16[3072,128]{1,0:T(8,128)(2,1)S(1)}, u32[]{:S(2)}, u32[]{:S(2)}) collective-permute-start(bf16[3072,128]{1,0:T(8,128)(2,1)S(1)} %shard_map.207), channel_id=1, source_target_pairs={{0,4},{4,0},{8,12},{12,8},{16,20},{20,16},{24,28},{28,24},{1,5},{5... | collective-permute-start | bytes 2359304 | tf_op jit(solution)/shard_map/ppermute | solution.py:32
  121.8 16.1 %collective-permute-start.16 = (bf16[256,1024]{1,0:T(8,128)(2,1)S(1)}, bf16[256,1024]{1,0:T(8,128)(2,1)S(1)}, u32[]{:S(2)}, u32[]{:S(2)}) collective-permute-start(bf16[256,1024]{1,0:T(8,128)(2,1)S(1)} %get-tuple-element.153.own.refs_1_), channel_id=1, source_target_pairs={{0,1},{1,0},{2,3},{3,2},{4,5},{5,4},{6,7},{7,6},{8,9},{9,8},{10,11... | collective-permute-start | bytes 1572872 | tf_op jit(solution)/shard_map/ppermute | solution.py:32
  145.1 190.7 %reduce-scatter.6.cloned.1.call-start = ((), (), s32[]{:S(2)}) async-start(), calls=%async_computation.12 | async-start | bytes 1310720 | tf_op jit(solution)/shard_map/reduce_scatter | solution.py:276
  145.4 26.8 %collective-permute-start.22 = (bf16[4096,128]{1,0:T(8,128)(2,1)}, bf16[4096,128]{1,0:T(8,128)(2,1)}, u32[]{:S(2)}, u32[]{:S(2)}) collective-permute-start(bf16[4096,128]{1,0:T(8,128)(2,1)} %all-gather.11.cloned.1.call-done.here), channel_id=1, source_target_pairs={{0,4},{4,0},{8,12},{12,8},{16,20},{20,16},{24,28},{28,24},{1,5},{5... | collective-permute-start | bytes 3145736 | tf_op jit(solution)/shard_map/ppermute | solution.py:32
  149.6 13.6 %collective-permute-start.20 = (bf16[256,1024]{1,0:T(8,128)(2,1)S(1)}, bf16[256,1024]{1,0:T(8,128)(2,1)S(1)}, u32[]{:S(2)}, u32[]{:S(2)}) collective-permute-start(bf16[256,1024]{1,0:T(8,128)(2,1)S(1)} %shard_map.210.here.branch_here), channel_id=1, source_target_pairs={{0,2},{1,3},{2,0},{3,1},{4,6},{5,7},{6,4},{7,5},{8,10},{9,11},{10,... | collective-permute-start | bytes 1572872 | tf_op jit(solution)/shard_map/ppermute | solution.py:32
  167.4 7.7 %collective-permute-start.21 = (bf16[256,1024]{1,0:T(8,128)(2,1)}, bf16[256,1024]{1,0:T(8,128)(2,1)}, u32[]{:S(2)}, u32[]{:S(2)}) collective-permute-start(bf16[256,1024]{1,0:T(8,128)(2,1)} %get-tuple-element.161.own.refs_4_), channel_id=1, source_target_pairs={{0,1},{1,0},{2,3},{3,2},{4,5},{5,4},{6,7},{7,6},{8,9},{9,8},{10,11... | collective-permute-start | bytes 1572872 | tf_op jit(solution)/shard_map/ppermute | solution.py:32
  168.9 15.8 %collective-permute-start.23 = (bf16[128,1024]{1,0:T(8,128)(2,1)}, bf16[128,1024]{1,0:T(8,128)(2,1)}, u32[]{:S(2)}, u32[]{:S(2)}) collective-permute-start(bf16[128,1024]{1,0:T(8,128)(2,1)} %shard_map.215), channel_id=1, source_target_pairs={{0,2},{1,3},{2,0},{3,1},{4,6},{5,7},{6,4},{7,5},{8,10},{9,11},{10,... | collective-permute-start | bytes 786440 | tf_op jit(solution)/shard_map/ppermute | solution.py:32
  170.4 26.3 %collective-permute-start.27 = (bf16[4096,128]{1,0:T(8,128)(2,1)}, bf16[4096,128]{1,0:T(8,128)(2,1)}, u32[]{:S(2)}, u32[]{:S(2)}) collective-permute-start(bf16[4096,128]{1,0:T(8,128)(2,1)} %all-gather.13.cloned.1.call-done.here), channel_id=1, source_target_pairs={{0,4},{4,0},{8,12},{12,8},{16,20},{20,16},{24,28},{28,24},{1,5},{5... | collective-permute-start | bytes 3145736 | tf_op jit(solution)/shard_map/ppermute | solution.py:32
  189.4 14.0 %collective-permute-start.26 = (bf16[256,1024]{1,0:T(8,128)(2,1)S(1)}, bf16[256,1024]{1,0:T(8,128)(2,1)S(1)}, u32[]{:S(2)}, u32[]{:S(2)}) collective-permute-start(bf16[256,1024]{1,0:T(8,128)(2,1)S(1)} %shard_map.216.here.branch_here), channel_id=1, source_target_pairs={{0,2},{1,3},{2,0},{3,1},{4,6},{5,7},{6,4},{7,5},{8,10},{9,11},{10,... | collective-permute-start | bytes 1572872 | tf_op jit(solution)/shard_map/ppermute | solution.py:32
  190.0 28.4 %collective-permute-start.29 = (bf16[4096,128]{1,0:T(8,128)(2,1)S(1)}, bf16[4096,128]{1,0:T(8,128)(2,1)S(1)}, u32[]{:S(2)}, u32[]{:S(2)}) collective-permute-start(bf16[4096,128]{1,0:T(8,128)(2,1)S(1)} %bitcast.92), channel_id=1, source_target_pairs={{0,4},{4,0},{8,12},{12,8},{16,20},{20,16},{24,28},{28,24},{1,5},{5... | collective-permute-start | bytes 3145736 | tf_op jit(solution)/shard_map/ppermute | solution.py:32
  205.0 14.5 %collective-permute-start.28 = (bf16[256,1024]{1,0:T(8,128)(2,1)S(1)}, bf16[256,1024]{1,0:T(8,128)(2,1)S(1)}, u32[]{:S(2)}, u32[]{:S(2)}) collective-permute-start(bf16[256,1024]{1,0:T(8,128)(2,1)S(1)} %get-tuple-element.174.own.refs_1_), channel_id=1, source_target_pairs={{0,1},{1,0},{2,3},{3,2},{4,5},{5,4},{6,7},{7,6},{8,9},{9,8},{10,11... | collective-permute-start | bytes 1572872 | tf_op jit(solution)/shard_map/ppermute | solution.py:32
  224.7 14.0 %collective-permute-start.32 = (bf16[256,1024]{1,0:T(8,128)(2,1)S(1)}, bf16[256,1024]{1,0:T(8,128)(2,1)S(1)}, u32[]{:S(2)}, u32[]{:S(2)}) collective-permute-start(bf16[256,1024]{1,0:T(8,128)(2,1)S(1)} %shard_map.222.here), channel_id=1, source_target_pairs={{0,2},{1,3},{2,0},{3,1},{4,6},{5,7},{6,4},{7,5},{8,10},{9,11},{10,... | collective-permute-start | bytes 1572872 | tf_op jit(solution)/shard_map/ppermute | solution.py:32
  247.7 14.0 %collective-permute-start.36 = (bf16[256,1024]{1,0:T(8,128)(2,1)S(1)}, bf16[256,1024]{1,0:T(8,128)(2,1)S(1)}, u32[]{:S(2)}, u32[]{:S(2)}) collective-permute-start(bf16[256,1024]{1,0:T(8,128)(2,1)S(1)} %shard_map.228.here), channel_id=1, source_target_pairs={{0,2},{1,3},{2,0},{3,1},{4,6},{5,7},{6,4},{7,5},{8,10},{9,11},{10,... | collective-permute-start | bytes 1572872 | tf_op jit(solution)/shard_map/ppermute | solution.py:32
  248.2 29.3 %collective-permute-start.38 = (bf16[1024,512]{1,0:T(8,128)(2,1)S(1)}, bf16[1024,512]{1,0:T(8,128)(2,1)S(1)}, u32[]{:S(2)}, u32[]{:S(2)}) collective-permute-start(bf16[1024,512]{1,0:T(8,128)(2,1)S(1)} %get-tuple-element.185), channel_id=1, source_target_pairs={{0,4},{4,0},{8,12},{12,8},{16,20},{20,16},{24,28},{28,24},{1,5},{5... | collective-permute-start | bytes 3145736 | tf_op jit(solution)/shard_map/ppermute | solution.py:32
  278.8 76.6 %reduce-scatter.8.cloned.1.call-start = ((), (), s32[]{:S(2)}) async-start(), calls=%async_computation.13 | async-start | bytes 1310720 | tf_op jit(solution)/shard_map/reduce_scatter | solution.py:276
  282.6 14.0 %collective-permute-start.41 = (bf16[256,1024]{1,0:T(8,128)(2,1)S(1)}, bf16[256,1024]{1,0:T(8,128)(2,1)S(1)}, u32[]{:S(2)}, u32[]{:S(2)}) collective-permute-start(bf16[256,1024]{1,0:T(8,128)(2,1)S(1)} %shard_map.233.here), channel_id=1, source_target_pairs={{0,2},{1,3},{2,0},{3,1},{4,6},{5,7},{6,4},{7,5},{8,10},{9,11},{10,... | collective-permute-start | bytes 1572872 | tf_op jit(solution)/shard_map/ppermute | solution.py:32
  283.2 25.1 %collective-permute-start.43 = (bf16[1024,512]{1,0:T(8,128)(2,1)}, bf16[1024,512]{1,0:T(8,128)(2,1)S(1)}, u32[]{:S(2)}, u32[]{:S(2)}) collective-permute-start(bf16[1024,512]{1,0:T(8,128)(2,1)} %copy-done.126), channel_id=1, source_target_pairs={{0,4},{4,0},{8,12},{12,8},{16,20},{20,16},{24,28},{28,24},{1,5},{5... | collective-permute-start | bytes 3145736 | tf_op jit(solution)/shard_map/ppermute | solution.py:32
  300.3 8.1 %collective-permute-start.42 = (bf16[256,1024]{1,0:T(8,128)(2,1)S(1)}, bf16[256,1024]{1,0:T(8,128)(2,1)S(1)}, u32[]{:S(2)}, u32[]{:S(2)}) collective-permute-start(bf16[256,1024]{1,0:T(8,128)(2,1)S(1)} %get-tuple-element.210.refs_1_.own), channel_id=1, source_target_pairs={{0,1},{1,0},{2,3},{3,2},{4,5},{5,4},{6,7},{7,6},{8,9},{9,8},{10,11... | collective-permute-start | bytes 1572872 | tf_op jit(solution)/shard_map/ppermute | solution.py:32
  310.4 81.5 %reduce-scatter.10.cloned.1.call-start = ((), (), s32[]{:S(2)}) async-start(), calls=%async_computation.14 | async-start | bytes 1310720 | tf_op jit(solution)/shard_map/reduce_scatter | solution.py:276
  310.5 24.3 %collective-permute-start.47 = (bf16[1024,512]{1,0:T(8,128)(2,1)}, bf16[1024,512]{1,0:T(8,128)(2,1)S(1)}, u32[]{:S(2)}, u32[]{:S(2)}) collective-permute-start(bf16[1024,512]{1,0:T(8,128)(2,1)} %copy-done.127), channel_id=1, source_target_pairs={{0,4},{4,0},{8,12},{12,8},{16,20},{20,16},{24,28},{28,24},{1,5},{5... | collective-permute-start | bytes 3145736 | tf_op jit(solution)/shard_map/ppermute | solution.py:32
  324.5 14.0 %collective-permute-start.46 = (bf16[256,1024]{1,0:T(8,128)(2,1)S(1)}, bf16[256,1024]{1,0:T(8,128)(2,1)S(1)}, u32[]{:S(2)}, u32[]{:S(2)}) collective-permute-start(bf16[256,1024]{1,0:T(8,128)(2,1)S(1)} %shard_map.239.here), channel_id=1, source_target_pairs={{0,2},{1,3},{2,0},{3,1},{4,6},{5,7},{6,4},{7,5},{8,10},{9,11},{10,... | collective-permute-start | bytes 1572872 | tf_op jit(solution)/shard_map/ppermute | solution.py:32
  341.3 95.3 %reduce-scatter.12.cloned.1.call-start = ((), (), s32[]{:S(2)}) async-start(), calls=%async_computation.15 | async-start | bytes 1310720 | tf_op jit(solution)/shard_map/reduce_scatter | solution.py:276
  341.5 30.5 %collective-permute-start.49 = (bf16[1024,512]{1,0:T(8,128)(2,1)}, bf16[1024,512]{1,0:T(8,128)(2,1)}, u32[]{:S(2)}, u32[]{:S(2)}) collective-permute-start(bf16[1024,512]{1,0:T(8,128)(2,1)} %copy-done.124), channel_id=1, source_target_pairs={{0,4},{4,0},{8,12},{12,8},{16,20},{20,16},{24,28},{28,24},{1,5},{5... | collective-permute-start | bytes 3145736 | tf_op jit(solution)/shard_map/ppermute | solution.py:32
  353.1 38.8 %collective-permute-start.53 = (bf16[1024,512]{1,0:T(8,128)(2,1)}, bf16[1024,512]{1,0:T(8,128)(2,1)}, u32[]{:S(2)}, u32[]{:S(2)}) collective-permute-start(bf16[1024,512]{1,0:T(8,128)(2,1)} %get-tuple-element.225), channel_id=1, source_target_pairs={{0,4},{4,0},{8,12},{12,8},{16,20},{20,16},{24,28},{28,24},{1,5},{5... | collective-permute-start | bytes 3145736 | tf_op jit(solution)/shard_map/ppermute | solution.py:32
  377.8 14.1 %collective-permute-start.52 = (bf16[256,1024]{1,0:T(8,128)(2,1)S(1)}, bf16[256,1024]{1,0:T(8,128)(2,1)S(1)}, u32[]{:S(2)}, u32[]{:S(2)}) collective-permute-start(bf16[256,1024]{1,0:T(8,128)(2,1)S(1)} %shard_map.246.here), channel_id=1, source_target_pairs={{0,2},{1,3},{2,0},{3,1},{4,6},{5,7},{6,4},{7,5},{8,10},{9,11},{10,... | collective-permute-start | bytes 1572872 | tf_op jit(solution)/shard_map/ppermute | solution.py:32
  379.4 31.9 %collective-permute-start.54 = (bf16[1024,512]{1,0:T(8,128)(2,1)}, bf16[1024,512]{1,0:T(8,128)(2,1)}, u32[]{:S(2)}, u32[]{:S(2)}) collective-permute-start(bf16[1024,512]{1,0:T(8,128)(2,1)} %copy-done.125), channel_id=1, source_target_pairs={{0,4},{4,0},{8,12},{12,8},{16,20},{20,16},{24,28},{28,24},{1,5},{5... | collective-permute-start | bytes 3145736 | tf_op jit(solution)/shard_map/ppermute | solution.py:32
  383.0 12.6 %collective-permute-start.56 = (f32[8,6144]{1,0:T(8,128)}, f32[8,6144]{1,0:T(8,128)}, u32[]{:S(2)}, u32[]{:S(2)}) collective-permute-start(f32[8,6144]{1,0:T(8,128)} %shard_map.252.own), channel_id=1, source_target_pairs={{0,1},{1,0},{2,3},{3,2},{4,5},{5,4},{6,7},{7,6},{8,9},{9,8},{10,11... | collective-permute-start | bytes 589832 | tf_op jit(solution)/shard_map/ppermute | solution.py:32
  413.1 23.3 %all-to-all-start.2 = ((bf16[8,38,1024]{2,1,0:T(8,128)(2,1)}), bf16[8,38,1024]{2,1,0:T(8,128)(2,1)S(1)}, u32[]{:S(2)}, u32[]{:S(2)}) async-start(bf16[8,38,1024]{2,1,0:T(8,128)(2,1)} %pad_maximum_fusion.1), calls=%async_computation.5 | async-start | bytes 1310720 | tf_op jit(solution)/shard_map/all_to_all | solution.py:342
  418.0 39.5 %reduce-scatter.14.cloned.1.call-start = ((), (), s32[]{:S(2)}) async-start(), calls=%async_computation.16 | async-start | bytes 1310720 | tf_op jit(solution)/shard_map/reduce_scatter | solution.py:276
  448.4 7.7 %collective-permute-start.59 = (f32[40,256]{1,0:T(8,128)S(1)}, f32[40,256]{1,0:T(8,128)S(1)}, u32[]{:S(2)}, u32[]{:S(2)}) collective-permute-start(f32[40,256]{1,0:T(8,128)S(1)} %add.164), channel_id=1, source_target_pairs={{0,16},{4,20},{8,24},{12,28},{16,0},{20,4},{24,8},{28,12},{1,17},{... | collective-permute-start | bytes 122888 | tf_op jit(solution)/shard_map/ppermute | solution.py:32
  451.1 12.9 %collective-permute-start.60 = (bf16[1024,128]{1,0:T(8,128)(2,1)}, bf16[1024,128]{1,0:T(8,128)(2,1)S(1)}, u32[]{:S(2)}, u32[]{:S(2)}) collective-permute-start(bf16[1024,128]{1,0:T(8,128)(2,1)} %get-tuple-element.300), channel_id=1, source_target_pairs={{0,24},{4,28},{8,0},{12,4},{16,8},{20,12},{24,16},{28,20},{1,25},{... | collective-permute-start | bytes 786440 | tf_op jit(solution)/shard_map/ppermute | solution.py:286
  452.7 16.0 %collective-permute-start.62 = (bf16[1024,128]{1,0:T(8,128)(2,1)}, bf16[1024,128]{1,0:T(8,128)(2,1)S(1)}, u32[]{:S(2)}, u32[]{:S(2)}) collective-permute-start(bf16[1024,128]{1,0:T(8,128)(2,1)} %get-tuple-element.301), channel_id=1, source_target_pairs={{0,8},{4,12},{8,16},{12,20},{16,24},{20,28},{24,0},{28,4},{1,9},{5... | collective-permute-start | bytes 786440 | tf_op jit(solution)/shard_map/ppermute | solution.py:286
  453.2 25.0 %collective-permute-start.61 = (bf16[1024,128]{1,0:T(8,128)(2,1)}, bf16[1024,128]{1,0:T(8,128)(2,1)S(1)}, u32[]{:S(2)}, u32[]{:S(2)}) collective-permute-start(bf16[1024,128]{1,0:T(8,128)(2,1)} %get-tuple-element.302), channel_id=1, source_target_pairs={{0,16},{4,20},{8,24},{12,28},{16,0},{20,4},{24,8},{28,12},{1,17},{... | collective-permute-start | bytes 786440 | tf_op jit(solution)/shard_map/ppermute | solution.py:286
  (199 other events, 1419.8 us)
Sparse Core Ops, SparseCore 0:
  10.5 36.9 all-gather.6
  49.6 33.4 all-gather.8
  85.2 37.8 all-gather.10
  124.6 27.4 all-gather.12
  154.0 27.4 all-gather.14
  279.0 27.6 reduce-scatter.5
  310.5 28.6 reduce-scatter.7
  342.1 26.7 reduce-scatter.9
  395.8 28.8 reduce-scatter.11
  426.8 30.7 reduce-scatter.13
